TPU v7x, 256 devices: a whole 4x4x8 slice. The times are simulated.
256 devices in a mesh: dom: 64 (over x, z, core), hid: 4 (over y).
Axes of the slice: x: 4, y: 4, z: 8, core: 2. Of those that a mesh axis runs over, the one named last changes fastest.
Arguments:
- features: bfloat16 [32768, 640], P('dom'), may hold values from -6 to 6
- self_weight: bfloat16 [640, 1024], P(None, 'hid'), may hold values from -0.25 to 0.25
- neigh_weight: bfloat16 [640, 1024], P(None, 'hid'), may hold values from -0.25 to 0.25
- cotangent: bfloat16 [32768, 1024], P('dom', 'hid'), may hold values from -6 to 6
- neighbor_blocks: int32 [64, 4, 8], P('dom'), may hold values from 0 to 3
- local_tiles: bfloat16 [64, 4, 8, 128, 128], P('dom'), may hold values from 0 to 1, as said below
- send_blocks: int32 [64, 4, 2], P('dom'), may hold values from 0 to 3
- recv_blocks: int32 [64, 4, 2], P('dom'), may hold values from 0 to 3
- live_slots: int32 [64, 4], P('dom'), may hold values from 1 to 2, as said below
- boundary_tiles: bfloat16 [64, 4, 2, 128, 128], P('dom'), may hold values from 0 to 1, as said below
Outputs:
- activated: bfloat16 [32768, 1024], P('dom', 'hid')
- grad_self: float32 [640, 1024], P(None, 'hid')
- grad_neigh: float32 [640, 1024], P(None, 'hid')
- grad_input: bfloat16 [32768, 640], P('dom', 'hid')
Inputs may be any that keep to these rules, and one draw needn't show every extreme that they name: `local_tiles`: entries are 0 or 1; in the first of a block's 8 tiles every row holds a one. `boundary_tiles`: entries are 0 or 1. `live_slots`: slots at or beyond this count are padding; in every round some partition has 2 and some has 1.
All inputs are finite; a program needn't handle non-finite values.
Results may differ from a plain program's by a relative error of at most 0.006.
Values may be sent and summed in bfloat16 or wider, within the bound.
No kernel may reach another device: no remote copies, remote signals or barrier semaphores. Data moves between devices by JAX's collectives and lax.ppermute only.
A program may use at most 64 MiB of HBM per device.

v0:
```python
import math

import jax
import jax.numpy as jnp
from jax import lax
from jax.sharding import PartitionSpec as P

BS = 128
K_IN = 8
ROUNDS = 4
NB = 2


def passed_along(array, axis, by):
    count = lax.axis_size(axis)
    return lax.ppermute(array, axis, [(i, (i + by) % count) for i in range(count)])


def round_offsets():
    return [(round_index // 2 + 1) * (1 - 2 * (round_index % 2)) for round_index in range(ROUNDS)]


def scatter_blocks(target, where_to, values, count):
    one_hot = (where_to[:, None] == jnp.arange(count)[None, :]).astype(jnp.float32)
    return target + jnp.einsum("sb,s...->b...", one_hot, values, precision=lax.Precision.HIGHEST)


def on_device(
    features,
    self_weight,
    neigh_weight,
    cotangent,
    neighbor_blocks,
    local_tiles,
    send_blocks,
    recv_blocks,
    live_slots,
    boundary_tiles,
):
    rows_dev, width = features.shape
    blocks_dev = rows_dev // BS
    hidden_dev = self_weight.shape[1]
    grouped = features.reshape(blocks_dev, BS, width)
    adjacency = neighbor_blocks[0]
    tiles_local = local_tiles[0]
    outgoing_ids = send_blocks[0]
    incoming_ids = recv_blocks[0]
    boundary = boundary_tiles[0]
    live_count = live_slots[0]
    offsets = round_offsets()
    slot_range = jnp.arange(NB)
    degree = jnp.sum(tiles_local.astype(jnp.float32), axis=(1, 3))
    masked_tiles = []
    for round_index in range(ROUNDS):
        live_mask = (slot_range < live_count[round_index]).astype(jnp.bfloat16)
        live_tiles = boundary[round_index] * live_mask[:, None, None]
        masked_tiles.append(live_tiles)
        degree = scatter_blocks(
            degree,
            incoming_ids[round_index],
            jnp.sum(live_tiles.astype(jnp.float32), axis=2),
            blocks_dev,
        )
    received_all = [
        passed_along(
            jnp.take(grouped, outgoing_ids[round_index], axis=0), "dom", offsets[round_index]
        )
        for round_index in range(ROUNDS)
    ]
    summed = jnp.zeros((blocks_dev, BS, grouped.shape[2]), jnp.float32)
    for neighbor_neighbor_slot in range(K_IN):
        neighbor_picked = jnp.take(grouped, adjacency[:, neighbor_neighbor_slot], axis=0)
        tile_slice = tiles_local[:, neighbor_neighbor_slot]
        summed = summed + jnp.einsum(
            "bij,bjw->biw",
            tile_slice,
            neighbor_picked,
            preferred_element_type=jnp.float32,
            precision=None,
        )
    boundary_summed = summed
    for boundary_round_index in range(ROUNDS):
        received = received_all[boundary_round_index]
        tile_slice = masked_tiles[boundary_round_index]
        contribution = jnp.einsum(
            "sij,sjw->siw", tile_slice, received, preferred_element_type=jnp.float32, precision=None
        )
        boundary_summed = scatter_blocks(
            boundary_summed, incoming_ids[boundary_round_index], contribution, blocks_dev
        )
    summed = boundary_summed
    mean_rows = (summed / degree[:, :, None]).reshape(rows_dev, width)
    neighbor_term = jnp.dot(
        mean_rows, neigh_weight.astype(jnp.float32), precision=lax.Precision.HIGHEST
    )
    preact = jnp.dot(features, self_weight, preferred_element_type=jnp.float32) + neighbor_term
    activated = jax.nn.silu(preact).astype(jnp.bfloat16)
    sigmoid_z = jax.nn.sigmoid(preact)
    grad_pre = cotangent.astype(jnp.float32) * sigmoid_z * (1.0 + preact * (1.0 - sigmoid_z))
    grad_low = grad_pre.astype(jnp.bfloat16)
    spread = (
        (grad_pre / degree.reshape(rows_dev)[:, None])
        .astype(jnp.bfloat16)
        .reshape(blocks_dev, BS, hidden_dev)
    )
    back_sum = jnp.zeros((blocks_dev, BS, hidden_dev), jnp.float32)
    returned_all = []
    for round_index in range(ROUNDS):
        picked = jnp.take(spread, incoming_ids[round_index], axis=0)
        term = jnp.einsum(
            "sij,siw->sjw", masked_tiles[round_index], picked, preferred_element_type=jnp.float32
        )
        returned_all.append(
            passed_along(term.astype(jnp.bfloat16), "dom", -offsets[round_index]).astype(term.dtype)
        )
    for neighbor_slot in range(K_IN):
        term = jnp.einsum(
            "bij,biw->bjw",
            tiles_local[:, neighbor_slot],
            spread,
            preferred_element_type=jnp.float32,
        )
        back_sum = scatter_blocks(back_sum, adjacency[:, neighbor_slot], term, blocks_dev)
    for round_index in range(ROUNDS):
        back_sum = scatter_blocks(
            back_sum, outgoing_ids[round_index], returned_all[round_index], blocks_dev
        )
    back_rows = back_sum.astype(jnp.bfloat16).reshape(rows_dev, hidden_dev)
    over_rows = (((0,), (0,)), ((), ()))
    self_part = lax.dot_general(features, grad_low, over_rows, preferred_element_type=jnp.float32)
    neigh_part = lax.dot_general(features, back_rows, over_rows, preferred_element_type=jnp.float32)
    grad_self, grad_neigh = lax.psum((self_part, neigh_part), "dom")
    grad_scale = 1.0 / math.sqrt(rows_dev * lax.axis_size("dom"))
    over_hidden = (((1,), (1,)), ((), ()))
    partial_input = lax.dot_general(
        grad_low, self_weight, over_hidden, preferred_element_type=jnp.float32
    ) + lax.dot_general(back_rows, neigh_weight, over_hidden, preferred_element_type=jnp.float32)
    grad_input = lax.psum_scatter(partial_input, "hid", scatter_dimension=1, tiled=True).astype(
        jnp.bfloat16
    )
    return (activated, grad_self * grad_scale, grad_neigh * grad_scale, grad_input)


def solution(mesh):
    return jax.shard_map(
        on_device,
        mesh=mesh,
        in_specs=(
            P("dom", None),
            P(None, "hid"),
            P(None, "hid"),
            P("dom", "hid"),
            P("dom", None, None),
            P("dom", None, None, None, None),
            P("dom", None, None),
            P("dom", None, None),
            P("dom", None),
            P("dom", None, None, None, None),
        ),
        out_specs=(P("dom", "hid"), P(None, "hid"), P(None, "hid"), P("dom", "hid")),
        check_vma=False,
    )
```

profile of v0, /device:TPU:1, one launch (start us, length us, event | category | flops | bytes accessed | tf_op | source)
XLA Modules:
  0.0 308.8 jit_solution(424367686069169520)
XLA Ops:
  11.1 8.6 %collective-permute-start.3 = (bf16[2,128,640]{2,1,0:T(8,128)(2,1)}, bf16[2,128,640]{2,1,0:T(8,128)(2,1)}, u32[]{:S(2)}, u32[]{:S(2)}) collective-permute-start(bf16[2,128,640]{2,1,0:T(8,128)(2,1)} %broadcast_select_fusion), channel_id=1, source_target_pairs={{0,248},{4,252},{8,0},{12,4},{16,8},{20,12},{24,16},{28,20},{32,24... | collective-permute-start | bytes 983048 | tf_op jit(solution)/shard_map/ppermute | solution.py:16
  30.3 1.5 gather_fusion.2
  31.7 1.5 gather_fusion.3
  33.2 1.5 gather_fusion.4
  34.7 1.5 gather_fusion.5
  39.5 2.1 fusion.159
  50.5 1.5 gather_fusion.6
  52.0 1.5 gather_fusion.7
  53.5 1.5 convolution_add_fusion.1
  55.0 1.3 fusion.82
  56.2 1.9 fusion.10
  58.2 1.3 fusion.81
  59.5 1.9 fusion.12
  61.4 1.3 fusion.80
  62.7 1.9 fusion.14
  64.7 1.3 fusion.79
  66.0 2.2 fusion.16
  68.2 1.2 fusion.5
  69.5 1.9 divide_convert_fusion
  71.4 1.1 fusion.67
  73.5 1.1 fusion.69
  77.6 1.3 copy.33
  79.0 2.0 fusion.42
  82.0 2.1 copy.35
  90.1 8.2 %collective-permute-start.6 = (bf16[2,128,256]{2,0,1:T(2,128)(2,1)S(1)}, bf16[2,128,256]{2,0,1:T(2,128)(2,1)S(1)}, u32[]{:S(2)}, u32[]{:S(2)}) collective-permute-start(bf16[2,128,256]{2,0,1:T(2,128)(2,1)S(1)} %copy.65), channel_id=1, source_target_pairs={{0,248},{4,252},{8,0},{12,4},{16,8},{20,12},{24,16},{28,20},{32,24... | collective-permute-start | bytes 393224 | tf_op jit(solution)/shard_map/ppermute | solution.py:16
  101.6 2.5 convolution_bitcast_fusion.1
  110.9 1.2 convolution_bitcast_fusion
  113.1 1.4 convolution_add_fusion.7
  114.6 181.7 %all-reduce.3.cloned.1.call-done = (f32[640,256]{0,1:T(8,128)}, f32[640,256]{0,1:T(8,128)}) async-done(((f32[640,256]{0,1:T(8,128)}, f32[640,256]{0,1:T(8,128)}), (f32[640,256]{0,1:T(8,128)}, f32[640,256]{0,1:T(8,128)})) %all-reduce.3.cloned.1.call-update) | async-done | bytes 1310736 | tf_op jit(solution)/shard_map/psum | solution.py:132
  296.3 1.2 broadcast_multiply_fusion.1
  298.7 1.1 copy.28
  299.7 1.7 convert_element_type.116
  (237 shorter events, 48.2 us)
Async XLA Ops:
  8.0 288.3 %all-reduce.3.cloned.1.call-start = ((), (), s32[]{:S(2)}) async-start(), calls=%async_computation.2 | async-start | bytes 2621440 | tf_op jit(solution)/shard_map/psum | solution.py:132
  9.1 12.1 %copy-start.43 = (s32[2]{0:T(128)}, s32[2]{0:T(128)S(1)}, u32[]{:S(2)}) copy-start(s32[2]{0:T(128)S(1)} %get-tuple-element.34) | copy-start | bytes 28
  9.1 12.1 %copy-start.41 = (s32[2]{0:T(128)}, s32[2]{0:T(128)S(1)}, u32[]{:S(2)}) copy-start(s32[2]{0:T(128)S(1)} %get-tuple-element.32) | copy-start | bytes 28
  9.1 14.6 %copy-start.47 = (s32[2]{0:T(128)}, s32[2]{0:T(128)S(1)}, u32[]{:S(2)}) copy-start(s32[2]{0:T(128)S(1)} %get-tuple-element.31) | copy-start | bytes 28
  11.1 43.8 %collective-permute-start.3 = (bf16[2,128,640]{2,1,0:T(8,128)(2,1)}, bf16[2,128,640]{2,1,0:T(8,128)(2,1)}, u32[]{:S(2)}, u32[]{:S(2)}) collective-permute-start(bf16[2,128,640]{2,1,0:T(8,128)(2,1)} %broadcast_select_fusion), channel_id=1, source_target_pairs={{0,248},{4,252},{8,0},{12,4},{16,8},{20,12},{24,16},{28,20},{32,24... | collective-permute-start | bytes 983048 | tf_op jit(solution)/shard_map/ppermute | solution.py:16
  21.2 37.0 %collective-permute-start.2 = (bf16[2,128,640]{2,1,0:T(8,128)(2,1)}, bf16[2,128,640]{2,1,0:T(8,128)(2,1)}, u32[]{:S(2)}, u32[]{:S(2)}) collective-permute-start(bf16[2,128,640]{2,1,0:T(8,128)(2,1)} %broadcast_select_fusion.1), channel_id=1, source_target_pairs={{0,8},{4,12},{8,16},{12,20},{16,24},{20,28},{24,32},{28,36},{32,40... | collective-permute-start | bytes 983048 | tf_op jit(solution)/shard_map/ppermute | solution.py:16
  21.3 4.7 %copy-start.23 = (s32[1,4,8]{2,1,0:T(4,128)S(1)}, s32[1,4,8]{2,1,0:T(4,128)}, u32[]{:S(2)}) copy-start(s32[1,4,8]{2,1,0:T(4,128)} %param.20) | copy-start | bytes 388
  21.3 5.6 %copy-start.1 = (bf16[1,4,8,128,128]{4,3,2,1,0:T(8,128)(2,1)S(1)}, bf16[1,4,8,128,128]{4,3,2,1,0:T(8,128)(2,1)}, u32[]{:S(2)}) copy-start(bf16[1,4,8,128,128]{4,3,2,1,0:T(8,128)(2,1)} %param.21) | copy-start | bytes 3145732
  22.7 38.7 %collective-permute-start.1 = (bf16[2,128,640]{2,1,0:T(8,128)(2,1)}, bf16[2,128,640]{2,1,0:T(8,128)(2,1)}, u32[]{:S(2)}, u32[]{:S(2)}) collective-permute-start(bf16[2,128,640]{2,1,0:T(8,128)(2,1)} %broadcast_select_fusion.2), channel_id=1, source_target_pairs={{0,252},{4,0},{8,4},{12,8},{16,12},{20,16},{24,20},{28,24},{32,28}... | collective-permute-start | bytes 983048 | tf_op jit(solution)/shard_map/ppermute | solution.py:16
  25.2 39.5 %collective-permute-start = (bf16[2,128,640]{2,1,0:T(8,128)(2,1)}, bf16[2,128,640]{2,1,0:T(8,128)(2,1)}, u32[]{:S(2)}, u32[]{:S(2)}) collective-permute-start(bf16[2,128,640]{2,1,0:T(8,128)(2,1)} %broadcast_select_fusion.3), channel_id=1, source_target_pairs={{0,4},{4,8},{8,12},{12,16},{16,20},{20,24},{24,28},{28,32},{32,36}... | collective-permute-start | bytes 983048 | tf_op jit(solution)/shard_map/ppermute | solution.py:16
  33.2 3.0 copy-start.32
  34.7 8.7 %copy-start.16 = (bf16[1,4,2,128,128]{4,3,2,1,0:T(8,128)(2,1)S(1)}, bf16[1,4,2,128,128]{4,3,2,1,0:T(8,128)(2,1)}, u32[]{:S(2)}) copy-start(bf16[1,4,2,128,128]{4,3,2,1,0:T(8,128)(2,1)} %param.25) | copy-start | bytes 786436
  37.5 17.5 %copy-start.39 = (bf16[2]{0:T(256)(128)(2,1)}, bf16[2]{0:T(256)(128)(2,1)S(1)}, u32[]{:S(2)}) copy-start(bf16[2]{0:T(256)(128)(2,1)S(1)} %compare_convert_fusion) | copy-start | bytes 16
  38.1 20.1 %copy-start.37 = (bf16[2]{0:T(256)(128)(2,1)}, bf16[2]{0:T(256)(128)(2,1)S(1)}, u32[]{:S(2)}) copy-start(bf16[2]{0:T(256)(128)(2,1)S(1)} %compare_convert_fusion.1) | copy-start | bytes 16
  38.8 22.6 %copy-start.35 = (bf16[2]{0:T(256)(128)(2,1)}, bf16[2]{0:T(256)(128)(2,1)S(1)}, u32[]{:S(2)}) copy-start(bf16[2]{0:T(256)(128)(2,1)S(1)} %compare_convert_fusion.2) | copy-start | bytes 16
  39.5 25.2 %copy-start.33 = (bf16[2]{0:T(256)(128)(2,1)}, bf16[2]{0:T(256)(128)(2,1)S(1)}, u32[]{:S(2)}) copy-start(bf16[2]{0:T(256)(128)(2,1)S(1)} %compare_convert_fusion.3) | copy-start | bytes 16
  64.7 3.5 %copy-start.2 = (bf16[4,128,640]{2,1,0:T(8,128)(2,1)S(1)}, bf16[4,128,640]{2,1,0:T(8,128)(2,1)}, u32[]{:S(2)}) copy-start(bf16[4,128,640]{2,1,0:T(8,128)(2,1)} %gather_fusion.7) | copy-start | bytes 1966084
  77.6 3.4 %copy-start.9 = (f32[4,256,128]{2,1,0:T(8,128)S(1)}, f32[4,256,128]{2,1,0:T(8,128)}, u32[]{:S(2)}) copy-start(f32[4,256,128]{2,1,0:T(8,128)} %fusion.68) | copy-start | bytes 1572868
  81.0 3.1 %copy-start.8 = (f32[4,256,128]{2,1,0:T(8,128)S(1)}, f32[4,256,128]{2,1,0:T(8,128)}, u32[]{:S(2)}) copy-start(f32[4,256,128]{2,1,0:T(8,128)} %fusion.70) | copy-start | bytes 1572868
  82.0 3.1 %copy-start.7 = (f32[4,256,128]{2,1,0:T(8,128)S(1)}, f32[4,256,128]{2,1,0:T(8,128)}, u32[]{:S(2)}) copy-start(f32[4,256,128]{2,1,0:T(8,128)} %fusion.71) | copy-start | bytes 1572868
  87.4 11.5 %copy-start.36 = (bf16[2]{0:T(256)(128)(2,1)S(1)}, bf16[2]{0:T(256)(128)(2,1)}, u32[]{:S(2)}) copy-start(bf16[2]{0:T(256)(128)(2,1)} %copy-done.35) | copy-start | bytes 16
  87.4 11.5 %copy-start.50 = (pred[2]{0:T(512)(128)(4,1)S(1)}, pred[2]{0:T(512)(128)(4,1)}, u32[]{:S(2)}) copy-start(pred[2]{0:T(512)(128)(4,1)} %get-tuple-element.50) | copy-start | bytes 10
  88.3 11.8 %copy-start.34 = (bf16[2]{0:T(256)(128)(2,1)S(1)}, bf16[2]{0:T(256)(128)(2,1)}, u32[]{:S(2)}) copy-start(bf16[2]{0:T(256)(128)(2,1)} %copy-done.33) | copy-start | bytes 16
  88.3 11.8 %copy-start.49 = (pred[2]{0:T(512)(128)(4,1)S(1)}, pred[2]{0:T(512)(128)(4,1)}, u32[]{:S(2)}) copy-start(pred[2]{0:T(512)(128)(4,1)} %get-tuple-element.51) | copy-start | bytes 10
  88.8 20.1 %collective-permute-start.7 = (bf16[2,128,256]{2,0,1:T(2,128)(2,1)S(1)}, bf16[2,128,256]{2,0,1:T(2,128)(2,1)S(1)}, u32[]{:S(2)}, u32[]{:S(2)}) collective-permute-start(bf16[2,128,256]{2,0,1:T(2,128)(2,1)S(1)} %copy.64), channel_id=1, source_target_pairs={{0,8},{4,12},{8,16},{12,20},{16,24},{20,28},{24,32},{28,36},{32,40... | collective-permute-start | bytes 393224 | tf_op jit(solution)/shard_map/ppermute | solution.py:16
  90.1 19.3 %collective-permute-start.6 = (bf16[2,128,256]{2,0,1:T(2,128)(2,1)S(1)}, bf16[2,128,256]{2,0,1:T(2,128)(2,1)S(1)}, u32[]{:S(2)}, u32[]{:S(2)}) collective-permute-start(bf16[2,128,256]{2,0,1:T(2,128)(2,1)S(1)} %copy.65), channel_id=1, source_target_pairs={{0,248},{4,252},{8,0},{12,4},{16,8},{20,12},{24,16},{28,20},{32,24... | collective-permute-start | bytes 393224 | tf_op jit(solution)/shard_map/ppermute | solution.py:16
  99.4 10.5 %collective-permute-start.5 = (bf16[2,128,256]{2,0,1:T(2,128)(2,1)S(1)}, bf16[2,128,256]{2,0,1:T(2,128)(2,1)S(1)}, u32[]{:S(2)}, u32[]{:S(2)}) collective-permute-start(bf16[2,128,256]{2,0,1:T(2,128)(2,1)S(1)} %copy.66), channel_id=1, source_target_pairs={{0,4},{4,8},{8,12},{12,16},{16,20},{20,24},{24,28},{28,32},{32,36}... | collective-permute-start | bytes 393224 | tf_op jit(solution)/shard_map/ppermute | solution.py:16
  100.6 9.7 %collective-permute-start.4 = (bf16[2,128,256]{2,0,1:T(2,128)(2,1)S(1)}, bf16[2,128,256]{2,0,1:T(2,128)(2,1)S(1)}, u32[]{:S(2)}, u32[]{:S(2)}) collective-permute-start(bf16[2,128,256]{2,0,1:T(2,128)(2,1)S(1)} %copy.67), channel_id=1, source_target_pairs={{0,252},{4,0},{8,4},{12,8},{16,12},{20,16},{24,20},{28,24},{32,28}... | collective-permute-start | bytes 393224 | tf_op jit(solution)/shard_map/ppermute | solution.py:16
  101.6 2.6 copy-start.13
  101.6 2.6 copy-start.15
  101.6 2.6 copy-start.30
  112.1 187.6 %reduce-scatter.2.cloned.1.call-start = ((), (), s32[]{:S(2)}) async-start(), calls=%async_computation.1 | async-start | bytes 1638400 | tf_op jit(solution)/shard_map/reduce_scatter | solution.py:138
  (34 other events, 42.1 us)
Sparse Core Ops, SparseCore 0:
  112.2 184.0 all-reduce.2
Sparse Core Ops, SparseCore 1:
  115.3 23.9 reduce-scatter.1
where the time goes:
time: 311 us; the launch traced here: 309 us
  waiting for transfers between devices  182 us (59%)
  matrix products  44.3 us (14%)
  local copies, waits for them, and re-layouts  33.2 us (11%)
  starting transfers between devices  19.8 us (6%)
  between operations  16.8 us (5%)
  other arithmetic  13 us (4%)
    psum x1, waiting for transfers between devices, on_device(): grad_self, grad_neigh = lax.psum((self_part, neigh_part), 'dom')  182 us
    ppermute x8, starting transfers between devices, passed_along(): lax.ppermute(array, axis, [(i, (i + by) % count) for i in range(count)])  19.7 us
    dot_general x20, matrix products, scatter_blocks(): jnp.einsum('sb,s...->b...', one_hot, values, precision=lax.Precision.HIGH...  17 us
    gather x8, local copies, waits for them, and re-layouts, on_device(): jnp.take(grouped, adjacency[:, neighbor_neighbor_slot], axis=0)  10.1 us
    dot_general x8, local copies, waits for them, and re-layouts, on_device(): jnp.einsum('bij,biw->bjw', tiles_local[:, neighbor_slot], spread, preferr...  7.89 us
    unnamed x115, local copies, waits for them, and re-layouts  7.3 us
  transfers between devices with their start and end apart: 10, of which 1 were waited for; matrix products, arithmetic and copies ran while one was open for 18% of the time, Pallas kernels for 0%

commit v1 on v0

v1 whole, which is shorter than its diff:
```python
import functools
import math

import jax
import jax.numpy as jnp
from jax import lax
from jax.experimental import pallas as pl
from jax.experimental.pallas import tpu as pltpu
from jax.sharding import PartitionSpec as P

BS = 128
BLK = 4
K_IN = 8
ROUNDS = 4
NB = 2
CORES = 2
Z = 8
X = 4
HID = 4
OFFSETS = (1, -1, 2, -2)
BF16 = jnp.bfloat16
F32 = jnp.float32

VMEM = pl.BlockSpec(memory_space=pltpu.VMEM)
SMEM = pl.BlockSpec(memory_space=pltpu.SMEM)


def dot(a, b, dims=((1,), (0,))):
    return lax.dot_general(a, b, (dims, ((), ())), preferred_element_type=F32)


def call(kernel, outs, specs, flops=0, nbytes=0, limit=24, scratch=()):
    return pl.pallas_call(
        kernel,
        out_shape=[jax.ShapeDtypeStruct(shape, dtype) for shape, dtype in outs],
        in_specs=specs,
        out_specs=[VMEM] * len(outs),
        scratch_shapes=list(scratch),
        compiler_params=pltpu.CompilerParams(vmem_limit_bytes=limit * 1024 * 1024),
        cost_estimate=pl.CostEstimate(flops=flops, bytes_accessed=nbytes, transcendentals=0),
    )


def dom_shift(array, by):
    count = lax.axis_size("dom")
    return lax.ppermute(array, "dom", [(i, (i + by) % count) for i in range(count)])


def dom_swap(array, mask):
    count = lax.axis_size("dom")
    return lax.ppermute(array, "dom", [(i, i ^ mask) for i in range(count)])


def hid_swap(array, mask):
    return lax.ppermute(array, "hid", [(i, i ^ mask) for i in range(HID)])


def rows(block, size=BS):
    return pl.ds(pl.multiple_of(block * size, size), size)


def pack_kernel(send, feats, *outs):
    for r in range(ROUNDS):
        for s in range(NB):
            outs[r][s * BS : (s + 1) * BS, :] = feats[rows(send[0, r, s]), :]


def before_kernel(
    neighbors, recv, live, feats, self_w, tiles, edge_tiles, local, edge, local_sum, degree, own_pre
):
    local[...] = jnp.zeros_like(local)
    edge[...] = jnp.zeros_like(edge)
    for b in range(BLK):
        for k in range(K_IN):
            cols = rows(neighbors[0, b, k])
            here = slice(b * BS, (b + 1) * BS)
            local[here, cols] = local[here, cols] + tiles[0, b, k]
    for r in range(ROUNDS):
        for s in range(NB):
            slot = r * NB + s

            @pl.when(s < live[0, r])
            def _():
                edge[rows(recv[0, r, s]), slot * BS : (slot + 1) * BS] = edge_tiles[0, r, s]

    feats_now = feats[...]
    own_pre[...] = dot(feats_now, self_w[...])
    local_now = local[...]
    local_sum[...] = dot(local_now, feats_now)
    ones = jnp.ones((BS * BLK, BS), BF16)
    edge_ones = jnp.ones((BS * NB * ROUNDS, BS), BF16)
    degree[...] = dot(local_now, ones) + dot(edge[...], edge_ones)


def middle_kernel(
    edge,
    got0,
    got1,
    got2,
    got3,
    local_sum,
    degree,
    own_pre,
    neigh_w,
    cot,
    feats,
    activated,
    low_out,
    spread_out,
    keep,
    give,
    term0,
    term1,
    term2,
    term3,
):
    core = lax.rem(lax.axis_index("dom"), CORES)
    width = NB * BS
    total = local_sum[...]
    for r, got in enumerate((got0, got1, got2, got3)):
        total = total + dot(edge[:, r * width : (r + 1) * width], got[...])
    inverse = 1.0 / degree[...]
    mean = total * jnp.concatenate([inverse] * (total.shape[1] // BS), axis=1)
    mean_high = mean.astype(BF16)
    mean_rest = (mean - mean_high.astype(F32)).astype(BF16)
    weights = neigh_w[...]
    pre = own_pre[...] + dot(mean_high, weights) + dot(mean_rest, weights)
    sig = jax.nn.sigmoid(pre)
    activated[...] = (pre * sig).astype(BF16)
    grad = cot[...].astype(F32) * sig * (1.0 + pre * (1.0 - sig))
    low = grad.astype(BF16)
    low_out[...] = low
    spread = (grad * jnp.concatenate([inverse] * (grad.shape[1] // BS), axis=1)).astype(BF16)
    spread_out[...] = spread
    over_rows = ((0,), (0,))
    of_self = dot(feats[...], low, over_rows)
    of_neigh = dot(mean_high, low, over_rows)

    @pl.when(core == 0)
    def _():
        keep[...] = of_self
        give[...] = of_neigh.astype(BF16)

    @pl.when(core == 1)
    def _():
        keep[...] = of_neigh
        give[...] = of_self.astype(BF16)

    for r, term in enumerate((term0, term1, term2, term3)):
        term[...] = dot(edge[:, r * width : (r + 1) * width], spread, over_rows).astype(BF16)


def z_index():
    return lax.rem(lax.axis_index("dom") // CORES, Z)


def cut_kernel(keep, got, own, *gives):
    z = z_index()
    size = own.shape[0]
    own[...] = keep[rows(z, size), :] + got[rows(z, size), :].astype(F32)
    for k in range(1, Z):
        at = rows(jnp.bitwise_xor(z, k), size)
        gives[k - 1][...] = (keep[at, :] + got[at, :].astype(F32)).astype(BF16)


def add_kernel(own, *refs):
    total = own[...]
    for got in refs[:-1]:
        total = total + got[...].astype(F32)
    refs[-1][...] = total.astype(BF16)


def pair_kernel(a, b, c, d, out):
    out[...] = (
        (a[...].astype(F32) + b[...].astype(F32)) + (c[...].astype(F32) + d[...].astype(F32))
    ).astype(BF16)


def join_kernel(own, *refs):
    z = z_index()
    size = own.shape[0]
    out = refs[-1]
    out[rows(z, size), :] = own[...]
    for k in range(1, Z):
        out[rows(jnp.bitwise_xor(z, k), size), :] = refs[k - 1][...]


def last_kernel(scale, mine, other, of_self, of_neigh):
    core = lax.rem(lax.axis_index("dom"), CORES)

    @pl.when(core == 0)
    def _():
        of_self[...] = mine[...].astype(F32) * scale
        of_neigh[...] = other[...].astype(F32) * scale

    @pl.when(core == 1)
    def _():
        of_self[...] = other[...].astype(F32) * scale
        of_neigh[...] = mine[...].astype(F32) * scale


def back_kernel(
    send, local, spread, got0, got1, got2, got3, low, self_w, neigh_w, own, give1, give2, give3, back
):
    back[...] = dot(local[...], spread[...], ((0,), (0,)))
    for r, got in enumerate((got0, got1, got2, got3)):
        for s in range(NB):
            at = rows(send[0, r, s])
            back[at, :] = back[at, :] + got[s * BS : (s + 1) * BS, :].astype(F32)
    back_low = back[...].astype(BF16)
    low_now = low[...]
    y = lax.axis_index("hid")
    size = own.shape[0]
    over_hidden = ((1,), (1,))
    for k in range(HID):
        at = rows(jnp.bitwise_xor(y, k), size)
        part = dot(self_w[at, :], low_now, over_hidden) + dot(neigh_w[at, :], back_low, over_hidden)
        if k == 0:
            own[...] = part
        else:
            (give1, give2, give3)[k - 1][...] = part.astype(BF16)


def on_device(
    features,
    self_weight,
    neigh_weight,
    cotangent,
    neighbor_blocks,
    local_tiles,
    send_blocks,
    recv_blocks,
    live_slots,
    boundary_tiles,
):
    n, width = features.shape
    hidden = self_weight.shape[1]
    slots = ROUNDS * NB * BS
    packed = call(pack_kernel, [((NB * BS, width), BF16)] * ROUNDS, [SMEM, VMEM], nbytes=2_000_000)(
        send_blocks, features
    )
    received = [dom_shift(packed[r], OFFSETS[r]) for r in range(ROUNDS)]
    local, edge, local_sum, degree, own_pre = call(
        before_kernel,
        [((n, n), BF16), ((n, slots), BF16), ((n, width), F32), ((n, BS), F32), ((n, hidden), F32)],
        [SMEM] * 3 + [VMEM] * 4,
        flops=1_000_000_000,
        nbytes=6_000_000,
    )(
        neighbor_blocks,
        recv_blocks,
        live_slots,
        features,
        self_weight,
        local_tiles,
        boundary_tiles,
    )
    activated, low, spread, keep, give, *terms = call(
        middle_kernel,
        [((n, hidden), BF16)] * 3
        + [((width, hidden), F32), ((width, hidden), BF16)]
        + [((NB * BS, hidden), BF16)] * ROUNDS,
        [VMEM] * 11,
        flops=1_600_000_000,
        nbytes=8_000_000,
        limit=32,
    )(edge, *received, local_sum, degree, own_pre, neigh_weight, cotangent, features)

    got = dom_swap(give, 1)
    piece = (width // Z, hidden)
    own, *gives = call(
        cut_kernel, [(piece, F32)] + [(piece, BF16)] * (Z - 1), [VMEM] * 2, nbytes=1_500_000
    )(keep, got)
    pieces = [dom_swap(gives[k - 1], CORES * k) for k in range(1, Z)]
    returned = [dom_shift(terms[r], -OFFSETS[r]) for r in range(ROUNDS)]
    (part,) = call(add_kernel, [(piece, BF16)], [VMEM] * Z, nbytes=400_000)(own, *pieces)
    across = [dom_swap(part, CORES * Z * k) for k in range(1, X)]
    (done,) = call(pair_kernel, [(piece, BF16)], [VMEM] * X, nbytes=200_000)(part, *across)
    gathered = [dom_swap(done, CORES * k) for k in range(1, Z)]
    shape = (width // HID, n)
    in_own, *in_gives = call(
        back_kernel,
        [(shape, F32)] + [(shape, BF16)] * (HID - 1),
        [SMEM] + [VMEM] * 9,
        flops=600_000_000,
        nbytes=3_000_000,
        scratch=[pltpu.VMEM((n, hidden), F32)],
    )(send_blocks, local, spread, *returned, low, self_weight, neigh_weight)
    in_parts = [hid_swap(in_gives[k - 1], k) for k in range(1, HID)]
    (mine,) = call(join_kernel, [((width, hidden), BF16)], [VMEM] * Z, nbytes=700_000)(
        done, *gathered
    )
    other = dom_swap(mine, 1)
    scale = 1.0 / math.sqrt(n * lax.axis_size("dom"))
    grad_self, grad_neigh = call(
        functools.partial(last_kernel, scale),
        [((width, hidden), F32)] * 2,
        [VMEM] * 2,
        nbytes=2_000_000,
    )(mine, other)
    grad_input = in_own
    for part in in_parts:
        grad_input = grad_input + part.astype(F32)
    return activated, grad_self, grad_neigh, grad_input.astype(BF16).T


def solution(mesh):
    return jax.shard_map(
        on_device,
        mesh=mesh,
        in_specs=(
            P("dom", None),
            P(None, "hid"),
            P(None, "hid"),
            P("dom", "hid"),
            P("dom", None, None),
            P("dom", None, None, None, None),
            P("dom", None, None),
            P("dom", None, None),
            P("dom", None),
            P("dom", None, None, None, None),
        ),
        out_specs=(P("dom", "hid"), P(None, "hid"), P(None, "hid"), P("dom", "hid")),
        check_vma=False,
    )
```

time: 311 us -> 94.8 us (0.30)
  waiting for transfers between devices: 182 us -> 17.1 us
  matrix products: 44.3 us -> 0 us
  starting transfers between devices: 19.8 us -> 58 us
  local copies, waits for them, and re-layouts: 33.2 us -> 8.2 us
  between operations: 16.8 us -> 0.79 us
  other arithmetic: 13 us -> 0.75 us
  Pallas kernels: 0 us -> 9.51 us
    psum x1 -> x0, waiting for transfers between devices: 182 us -> none  [on_device(): grad_self, grad_neigh = lax.psum((self_part, neigh_part), 'dom')]
    dot_general x50 -> x0, matrix products: 44.3 us -> none  [the longest x20 17 us: scatter_blocks(): jnp.einsum('sb,s...->b...', one_hot, values, precision=lax.Precision.HIGH...]
    ppermute x8 -> x30, starting transfers between devices: 19.7 us -> 58 us  [the longest x19 36.4 us: dom_swap(): return lax.ppermute(array, 'dom', [(i, i ^ mask) for i in range(count)])]
    ppermute x8 -> x30, waiting for transfers between devices: 0.02 us -> 17.1 us  [the longest x19 17.1 us: dom_swap(): return lax.ppermute(array, 'dom', [(i, i ^ mask) for i in range(count)])]
    gather x16 -> x0, local copies, waits for them, and re-layouts: 15.3 us -> none  [the longest x8 10.1 us: on_device(): jnp.take(grouped, adjacency[:, neighbor_neighbor_slot], axis=0)]
    pallas_call x0 -> x9, Pallas kernels: none -> 9.51 us  [the longest x1 3.2 us: on_device(): call(middle_kernel, [((n, hidden), BF16)] * 3 + [((width, hidden), F32),...]
    dot_general x12 -> x0, local copies, waits for them, and re-layouts: 8.44 us -> none  [the longest x8 7.89 us: on_device(): jnp.einsum('bij,biw->bjw', tiles_local[:, neighbor_slot], spread, preferr...]
    convert_element_type x5 -> x0, other arithmetic: 4.23 us -> none  [the longest x4 2.57 us: on_device(): live_mask = (slot_range < live_count[round_index]).astype(jnp.bfloat16)]
  transfers between devices with their start and end apart: 10 -> 30, of which waited for: 1 -> 9; matrix products, arithmetic and copies ran while one was open for 18% -> 2% of each run, Pallas kernels for 0% -> 5%
where the time goes in v1:
time: 94.8 us; the launch traced here: 94.4 us
  starting transfers between devices  58 us (61%)
  waiting for transfers between devices  17.1 us (18%)
  Pallas kernels  9.51 us (10%)
  local copies, waits for them, and re-layouts  8.2 us (9%)
    ppermute x19, starting transfers between devices, dom_swap(): return lax.ppermute(array, 'dom', [(i, i ^ mask) for i in range(count)])  36.4 us
    ppermute x8, starting transfers between devices, dom_shift(): lax.ppermute(array, 'dom', [(i, (i + by) % count) for i in range(count)])  17.6 us
    ppermute x19, waiting for transfers between devices, dom_swap(): return lax.ppermute(array, 'dom', [(i, i ^ mask) for i in range(count)])  17.1 us
    unnamed x24, local copies, waits for them, and re-layouts  8.2 us
    ppermute x3, starting transfers between devices, hid_swap(): return lax.ppermute(array, 'hid', [(i, i ^ mask) for i in range(HID)])  4.01 us
    pallas_call x1, Pallas kernels, on_device(): call(middle_kernel, [((n, hidden), BF16)] * 3 + [((width, hidden), F32),...  3.2 us
    pallas_call x1, Pallas kernels, on_device(): call(before_kernel, [((n, n), BF16), ((n, slots), BF16), ((n, width), F32...  2.29 us
    pallas_call x1, Pallas kernels, on_device(): call(back_kernel, [(shape, F32)] + [(shape, BF16)] * (HID - 1), [SMEM] +...  2.02 us
  transfers between devices with their start and end apart: 30, of which 9 were waited for; matrix products, arithmetic and copies ran while one was open for 2% of the time, Pallas kernels for 5%

profile of v1, /device:TPU:1, one launch (start us, length us, event | category | flops | bytes accessed | tf_op | source)
XLA Modules:
  0.0 94.4 jit_solution(6755531673179244095)
XLA Ops:
  1.4 1.1 %copy-done = bf16[512,640]{1,0:T(8,128)(2,1)S(1)} copy-done((bf16[512,640]{1,0:T(8,128)(2,1)S(1)}, bf16[512,640]{1,0:T(8,128)(2,1)}, u32[]{:S(2)}) %copy-start) | copy-done | bytes 655384
  3.2 3.1 %collective-permute-start = (bf16[256,640]{1,0:T(8,128)(2,1)S(1)}, bf16[256,640]{1,0:T(8,128)(2,1)S(1)}, u32[]{:S(2)}, u32[]{:S(2)}) collective-permute-start(bf16[256,640]{1,0:T(8,128)(2,1)S(1)} %get-tuple-element.37), channel_id=1, source_target_pairs={{0,4},{4,8},{8,12},{12,16},{16,20},{20,24},{24,28},{28,32},{32,36}... | collective-permute-start | bytes 983048 | tf_op jit(solution)/shard_map/ppermute | solution.py:46
  6.6 1.3 %collective-permute-start.2 = (bf16[256,640]{1,0:T(8,128)(2,1)S(1)}, bf16[256,640]{1,0:T(8,128)(2,1)S(1)}, u32[]{:S(2)}, u32[]{:S(2)}) collective-permute-start(bf16[256,640]{1,0:T(8,128)(2,1)S(1)} %get-tuple-element.39), channel_id=1, source_target_pairs={{0,8},{4,12},{8,16},{12,20},{16,24},{20,28},{24,32},{28,36},{32,40... | collective-permute-start | bytes 983048 | tf_op jit(solution)/shard_map/ppermute | solution.py:46
  7.9 4.7 %collective-permute-start.3 = (bf16[256,640]{1,0:T(8,128)(2,1)S(1)}, bf16[256,640]{1,0:T(8,128)(2,1)S(1)}, u32[]{:S(2)}, u32[]{:S(2)}) collective-permute-start(bf16[256,640]{1,0:T(8,128)(2,1)S(1)} %get-tuple-element.40), channel_id=1, source_target_pairs={{0,248},{4,252},{8,0},{12,4},{16,8},{20,12},{24,16},{28,20},{32,24... | collective-permute-start | bytes 983048 | tf_op jit(solution)/shard_map/ppermute | solution.py:46
  13.4 1.1 %copy-done.1 = bf16[512,640]{1,0:T(8,128)(2,1)S(1)} copy-done((bf16[512,640]{1,0:T(8,128)(2,1)S(1)}, bf16[512,640]{1,0:T(8,128)(2,1)}, u32[]{:S(2)}) %copy-start.1) | copy-done | bytes 655384
  14.5 1.0 %copy-done.3 = bf16[640,256]{1,0:T(8,128)(2,1)S(1)} copy-done((bf16[640,256]{1,0:T(8,128)(2,1)S(1)}, bf16[640,256]{1,0:T(8,128)(2,1)}, u32[]{:S(2)}) %copy-start.3) | copy-done | bytes 327704
  15.4 1.2 %copy-done.6 = bf16[1,4,8,128,128]{4,3,2,1,0:T(8,128)(2,1)S(1)} copy-done((bf16[1,4,8,128,128]{4,3,2,1,0:T(8,128)(2,1)S(1)}, bf16[1,4,8,128,128]{4,3,2,1,0:T(8,128)(2,1)}, u32[]{:S(2)}) %copy-start.6) | copy-done | bytes 1048600
  19.0 2.3 %shard_map.129 = (bf16[512,512]{1,0:T(8,128)(2,1)S(1)}, bf16[512,1024]{1,0:T(8,128)(2,1)S(1)}, f32[512,640]{1,0:T(8,128)S(1)}, f32[512,128]{1,0:T(8,128)S(1)}, f32[512,256]{1,0:T(8,128)S(1)}) custom-call(s32[1,4,8]{2,1,0:T(4,128)S(1)} %copy-done.9, s32[1,4,2]{2,1,0:T(4,128)S(1)} %copy.14.recv, s32[1,4]{1,0:T(1,128)S(1)} %copy-done.10, ...), custom_call_target="tpu_custom_call" | custom-call | flops 1000000000 | bytes 6000000 | tf_op jit(solution)/shard_map/pallas_call | solution.py:243
  21.4 3.2 %shard_map.131 = (bf16[512,256]{1,0:T(8,128)(2,1)}, bf16[512,256]{1,0:T(8,128)(2,1)S(1)}, bf16[512,256]{1,0:T(8,128)(2,1)S(1)}, f32[640,256]{1,0:T(8,128)S(1)}, ...) custom-call(bf16[512,1024]{1,0:T(8,128)(2,1)S(1)} %get-tuple-element, ...), custom_call_target="tpu_custom_call" | custom-call | flops 1600000000 | bytes 8000000 | tf_op jit(solution)/shard_map/pallas_call | solution.py:258
  24.6 5.0 %collective-permute-start.4 = (bf16[640,256]{1,0:T(8,128)(2,1)S(1)}, bf16[640,256]{1,0:T(8,128)(2,1)S(1)}, u32[]{:S(2)}, u32[]{:S(2)}) collective-permute-start(bf16[640,256]{1,0:T(8,128)(2,1)S(1)} %get-tuple-element.46), channel_id=1, source_target_pairs={{0,4},{4,0},{8,12},{12,8},{16,20},{20,16},{24,28},{28,24},{32,36},... | collective-permute-start | bytes 983048 | tf_op jit(solution)/shard_map/ppermute | solution.py:51
  29.6 1.3 %collective-permute-done.4.got = bf16[640,256]{1,0:T(8,128)(2,1)S(1)} collective-permute-done((bf16[640,256]{1,0:T(8,128)(2,1)S(1)}, bf16[640,256]{1,0:T(8,128)(2,1)S(1)}, u32[]{:S(2)}, u32[]{:S(2)}) %collective-permute-start.4) | collective-permute-done | bytes 327712 | tf_op jit(solution)/shard_map/ppermute | solution.py:51
  31.0 1.1 %collective-permute-start.6 = (bf16[80,256]{1,0:T(8,128)(2,1)S(1)}, bf16[80,256]{1,0:T(8,128)(2,1)S(1)}, u32[]{:S(2)}, u32[]{:S(2)}) collective-permute-start(bf16[80,256]{1,0:T(8,128)(2,1)S(1)} %get-tuple-element.49), channel_id=1, source_target_pairs={{0,16},{4,20},{8,24},{12,28},{16,0},{20,4},{24,8},{28,12},{32,48},... | collective-permute-start | bytes 122888 | tf_op jit(solution)/shard_map/ppermute | solution.py:51
  32.2 2.4 %collective-permute-start.7 = (bf16[80,256]{1,0:T(8,128)(2,1)S(1)}, bf16[80,256]{1,0:T(8,128)(2,1)S(1)}, u32[]{:S(2)}, u32[]{:S(2)}) collective-permute-start(bf16[80,256]{1,0:T(8,128)(2,1)S(1)} %get-tuple-element.50), channel_id=1, source_target_pairs={{0,24},{4,28},{8,16},{12,20},{16,8},{20,12},{24,0},{28,4},{32,56},... | collective-permute-start | bytes 122888 | tf_op jit(solution)/shard_map/ppermute | solution.py:51
  34.7 3.2 %collective-permute-start.9 = (bf16[80,256]{1,0:T(8,128)(2,1)S(1)}, bf16[80,256]{1,0:T(8,128)(2,1)S(1)}, u32[]{:S(2)}, u32[]{:S(2)}) collective-permute-start(bf16[80,256]{1,0:T(8,128)(2,1)S(1)} %get-tuple-element.52), channel_id=1, source_target_pairs={{0,40},{4,44},{8,32},{12,36},{16,56},{20,60},{24,48},{28,52},{32,8... | collective-permute-start | bytes 122888 | tf_op jit(solution)/shard_map/ppermute | solution.py:51
  38.0 1.6 %collective-permute-start.10 = (bf16[80,256]{1,0:T(8,128)(2,1)S(1)}, bf16[80,256]{1,0:T(8,128)(2,1)S(1)}, u32[]{:S(2)}, u32[]{:S(2)}) collective-permute-start(bf16[80,256]{1,0:T(8,128)(2,1)S(1)} %get-tuple-element.53), channel_id=1, source_target_pairs={{0,48},{4,52},{8,56},{12,60},{16,32},{20,36},{24,40},{28,44},{32,1... | collective-permute-start | bytes 122888 | tf_op jit(solution)/shard_map/ppermute | solution.py:51
  39.6 3.0 %collective-permute-start.11 = (bf16[80,256]{1,0:T(8,128)(2,1)S(1)}, bf16[80,256]{1,0:T(8,128)(2,1)S(1)}, u32[]{:S(2)}, u32[]{:S(2)}) collective-permute-start(bf16[80,256]{1,0:T(8,128)(2,1)S(1)} %get-tuple-element.54), channel_id=1, source_target_pairs={{0,56},{4,60},{8,48},{12,52},{16,40},{20,44},{24,32},{28,36},{32,2... | collective-permute-start | bytes 122888 | tf_op jit(solution)/shard_map/ppermute | solution.py:51
  42.6 2.3 %collective-permute-start.23 = (bf16[256,256]{1,0:T(8,128)(2,1)S(1)}, bf16[256,256]{1,0:T(8,128)(2,1)S(1)}, u32[]{:S(2)}, u32[]{:S(2)}) collective-permute-start(bf16[256,256]{1,0:T(8,128)(2,1)S(1)} %get-tuple-element.59), channel_id=1, source_target_pairs={{0,252},{4,0},{8,4},{12,8},{16,12},{20,16},{24,20},{28,24},{32,28}... | collective-permute-start | bytes 393224 | tf_op jit(solution)/shard_map/ppermute | solution.py:46
  45.0 5.8 %collective-permute-start.25 = (bf16[256,256]{1,0:T(8,128)(2,1)S(1)}, bf16[256,256]{1,0:T(8,128)(2,1)S(1)}, u32[]{:S(2)}, u32[]{:S(2)}) collective-permute-start(bf16[256,256]{1,0:T(8,128)(2,1)S(1)} %get-tuple-element.61), channel_id=1, source_target_pairs={{0,248},{4,252},{8,0},{12,4},{16,8},{20,12},{24,16},{28,20},{32,24... | collective-permute-start | bytes 393224 | tf_op jit(solution)/shard_map/ppermute | solution.py:46
  51.0 4.0 %collective-permute-done.14.d = bf16[80,256]{1,0:T(8,128)(2,1)S(1)} collective-permute-done((bf16[80,256]{1,0:T(8,128)(2,1)S(1)}, bf16[80,256]{1,0:T(8,128)(2,1)S(1)}, u32[]{:S(2)}, u32[]{:S(2)}) %collective-permute-start.14) | collective-permute-done | bytes 40992 | tf_op jit(solution)/shard_map/ppermute | solution.py:51
  55.0 4.5 %collective-permute-done.13.c = bf16[80,256]{1,0:T(8,128)(2,1)S(1)} collective-permute-done((bf16[80,256]{1,0:T(8,128)(2,1)S(1)}, bf16[80,256]{1,0:T(8,128)(2,1)S(1)}, u32[]{:S(2)}, u32[]{:S(2)}) %collective-permute-start.13) | collective-permute-done | bytes 40992 | tf_op jit(solution)/shard_map/ppermute | solution.py:51
  59.5 2.8 %collective-permute-done.12.b = bf16[80,256]{1,0:T(8,128)(2,1)S(1)} collective-permute-done((bf16[80,256]{1,0:T(8,128)(2,1)S(1)}, bf16[80,256]{1,0:T(8,128)(2,1)S(1)}, u32[]{:S(2)}, u32[]{:S(2)}) %collective-permute-start.12) | collective-permute-done | bytes 40992 | tf_op jit(solution)/shard_map/ppermute | solution.py:51
  62.4 2.5 %collective-permute-start.21 = (bf16[80,256]{1,0:T(8,128)(2,1)S(1)}, bf16[80,256]{1,0:T(8,128)(2,1)S(1)}, u32[]{:S(2)}, u32[]{:S(2)}) collective-permute-start(bf16[80,256]{1,0:T(8,128)(2,1)S(1)} %shard_map.134.own), channel_id=1, source_target_pairs={{0,56},{4,60},{8,48},{12,52},{16,40},{20,44},{24,32},{28,36},{32,2... | collective-permute-start | bytes 122888 | tf_op jit(solution)/shard_map/ppermute | solution.py:51
  65.0 2.0 %shard_map.137 = (f32[160,512]{1,0:T(8,128)S(1)}, bf16[160,512]{1,0:T(8,128)(2,1)S(1)}, bf16[160,512]{1,0:T(8,128)(2,1)S(1)}, bf16[160,512]{1,0:T(8,128)(2,1)S(1)}) custom-call(s32[1,4,2]{2,1,0:T(4,128)S(1)} %copy.15.send, bf16[512,512]{1,0:T(8,128)(2,1)S(1)} %get-tuple-element.57.local, bf16[512,256]{1,0:T(8,128)(2,1)S(1)} %get-tuple-element.58.spread, ...), custom_call_target="tpu_custom_call" | custom-call | flops 600000000 | bytes 3000000 | tf_op jit(solution)/shard_map/pallas_call | solution.py:281
  67.0 1.4 %collective-permute-start.27 = (bf16[160,512]{1,0:T(8,128)(2,1)S(1)}, bf16[160,512]{1,0:T(8,128)(2,1)S(1)}, u32[]{:S(2)}, u32[]{:S(2)}) collective-permute-start(bf16[160,512]{1,0:T(8,128)(2,1)S(1)} %get-tuple-element.65), channel_id=1, source_target_pairs={{0,1},{1,0},{2,3},{3,2},{4,5},{5,4},{6,7},{7,6},{8,9},{9,8},{10,11... | collective-permute-start | bytes 491528 | tf_op jit(solution)/shard_map/ppermute | solution.py:55
  68.4 2.6 %collective-permute-start.28 = (bf16[160,512]{1,0:T(8,128)(2,1)S(1)}, bf16[160,512]{1,0:T(8,128)(2,1)S(1)}, u32[]{:S(2)}, u32[]{:S(2)}) collective-permute-start(bf16[160,512]{1,0:T(8,128)(2,1)S(1)} %get-tuple-element.66), channel_id=1, source_target_pairs={{0,2},{1,3},{2,0},{3,1},{4,6},{5,7},{6,4},{7,5},{8,10},{9,11},{10,... | collective-permute-start | bytes 491528 | tf_op jit(solution)/shard_map/ppermute | solution.py:55
  71.1 5.6 %collective-permute-start.18 = (bf16[80,256]{1,0:T(8,128)(2,1)S(1)}, bf16[80,256]{1,0:T(8,128)(2,1)S(1)}, u32[]{:S(2)}, u32[]{:S(2)}) collective-permute-start(bf16[80,256]{1,0:T(8,128)(2,1)S(1)} %shard_map.134.own), channel_id=1, source_target_pairs={{0,32},{4,36},{8,40},{12,44},{16,48},{20,52},{24,56},{28,60},{32,0... | collective-permute-start | bytes 122888 | tf_op jit(solution)/shard_map/ppermute | solution.py:51
  76.8 1.3 %collective-permute-done.18.refs_3_ = bf16[80,256]{1,0:T(8,128)(2,1)S(1)} collective-permute-done((bf16[80,256]{1,0:T(8,128)(2,1)S(1)}, bf16[80,256]{1,0:T(8,128)(2,1)S(1)}, u32[]{:S(2)}, u32[]{:S(2)}) %collective-permute-start.18) | collective-permute-done | bytes 40992 | tf_op jit(solution)/shard_map/ppermute | solution.py:51
  78.1 2.6 %collective-permute-start.16 = (bf16[80,256]{1,0:T(8,128)(2,1)S(1)}, bf16[80,256]{1,0:T(8,128)(2,1)S(1)}, u32[]{:S(2)}, u32[]{:S(2)}) collective-permute-start(bf16[80,256]{1,0:T(8,128)(2,1)S(1)} %shard_map.134.own), channel_id=1, source_target_pairs={{0,16},{4,20},{8,24},{12,28},{16,0},{20,4},{24,8},{28,12},{32,48},... | collective-permute-start | bytes 122888 | tf_op jit(solution)/shard_map/ppermute | solution.py:51
  81.3 2.8 %collective-permute-start.15 = (bf16[80,256]{1,0:T(8,128)(2,1)S(1)}, bf16[80,256]{1,0:T(8,128)(2,1)S(1)}, u32[]{:S(2)}, u32[]{:S(2)}) collective-permute-start(bf16[80,256]{1,0:T(8,128)(2,1)S(1)} %shard_map.134.own), channel_id=1, source_target_pairs={{0,8},{4,12},{8,0},{12,4},{16,24},{20,28},{24,16},{28,20},{32,40},... | collective-permute-start | bytes 122888 | tf_op jit(solution)/shard_map/ppermute | solution.py:51
  84.2 1.9 %collective-permute-done.15.refs_0_ = bf16[80,256]{1,0:T(8,128)(2,1)S(1)} collective-permute-done((bf16[80,256]{1,0:T(8,128)(2,1)S(1)}, bf16[80,256]{1,0:T(8,128)(2,1)S(1)}, u32[]{:S(2)}, u32[]{:S(2)}) %collective-permute-start.15) | collective-permute-done | bytes 40992 | tf_op jit(solution)/shard_map/ppermute | solution.py:51
  86.1 5.9 %collective-permute-start.22 = (bf16[640,256]{1,0:T(8,128)(2,1)S(1)}, bf16[640,256]{1,0:T(8,128)(2,1)S(1)}, u32[]{:S(2)}, u32[]{:S(2)}) collective-permute-start(bf16[640,256]{1,0:T(8,128)(2,1)S(1)} %shard_map.135.mine), channel_id=1, source_target_pairs={{0,4},{4,0},{8,12},{12,8},{16,20},{20,16},{24,28},{28,24},{32,36},... | collective-permute-start | bytes 983048 | tf_op jit(solution)/shard_map/ppermute | solution.py:51
  93.3 1.2 %shard_map.136 = (f32[640,256]{1,0:T(8,128)}, f32[640,256]{1,0:T(8,128)}) custom-call(bf16[640,256]{1,0:T(8,128)(2,1)S(1)} %shard_map.135.mine, bf16[640,256]{1,0:T(8,128)(2,1)S(1)} %collective-permute-done.22.other), custom_call_target="tpu_custom_call" | custom-call | bytes 2000000 | tf_op jit(solution)/shard_map/pallas_call | solution.py:295
  (62 shorter events, 7.6 us)
Async XLA Ops:
  3.2 18.1 %collective-permute-start = (bf16[256,640]{1,0:T(8,128)(2,1)S(1)}, bf16[256,640]{1,0:T(8,128)(2,1)S(1)}, u32[]{:S(2)}, u32[]{:S(2)}) collective-permute-start(bf16[256,640]{1,0:T(8,128)(2,1)S(1)} %get-tuple-element.37), channel_id=1, source_target_pairs={{0,4},{4,8},{8,12},{12,16},{16,20},{20,24},{24,28},{28,32},{32,36}... | collective-permute-start | bytes 983048 | tf_op jit(solution)/shard_map/ppermute | solution.py:46
  6.3 15.0 %collective-permute-start.1 = (bf16[256,640]{1,0:T(8,128)(2,1)S(1)}, bf16[256,640]{1,0:T(8,128)(2,1)S(1)}, u32[]{:S(2)}, u32[]{:S(2)}) collective-permute-start(bf16[256,640]{1,0:T(8,128)(2,1)S(1)} %get-tuple-element.38), channel_id=1, source_target_pairs={{0,252},{4,0},{8,4},{12,8},{16,12},{20,16},{24,20},{28,24},{32,28}... | collective-permute-start | bytes 983048 | tf_op jit(solution)/shard_map/ppermute | solution.py:46
  6.6 14.8 %collective-permute-start.2 = (bf16[256,640]{1,0:T(8,128)(2,1)S(1)}, bf16[256,640]{1,0:T(8,128)(2,1)S(1)}, u32[]{:S(2)}, u32[]{:S(2)}) collective-permute-start(bf16[256,640]{1,0:T(8,128)(2,1)S(1)} %get-tuple-element.39), channel_id=1, source_target_pairs={{0,8},{4,12},{8,16},{12,20},{16,24},{20,28},{24,32},{28,36},{32,40... | collective-permute-start | bytes 983048 | tf_op jit(solution)/shard_map/ppermute | solution.py:46
  7.9 13.4 %collective-permute-start.3 = (bf16[256,640]{1,0:T(8,128)(2,1)S(1)}, bf16[256,640]{1,0:T(8,128)(2,1)S(1)}, u32[]{:S(2)}, u32[]{:S(2)}) collective-permute-start(bf16[256,640]{1,0:T(8,128)(2,1)S(1)} %get-tuple-element.40), channel_id=1, source_target_pairs={{0,248},{4,252},{8,0},{12,4},{16,8},{20,12},{24,16},{28,20},{32,24... | collective-permute-start | bytes 983048 | tf_op jit(solution)/shard_map/ppermute | solution.py:46
  19.0 2.4 %copy-start.8 = (bf16[512,256]{1,0:T(8,128)(2,1)S(1)}, bf16[512,256]{1,0:T(8,128)(2,1)}, u32[]{:S(2)}) copy-start(bf16[512,256]{1,0:T(8,128)(2,1)} %cot.1) | copy-start | bytes 786436
  24.6 40.5 %copy-start.4 = (bf16[640,256]{1,0:T(8,128)(2,1)S(1)}, bf16[640,256]{1,0:T(8,128)(2,1)}, u32[]{:S(2)}) copy-start(bf16[640,256]{1,0:T(8,128)(2,1)} %self_w.3) | copy-start | bytes 983044
  24.6 6.3 %collective-permute-start.4 = (bf16[640,256]{1,0:T(8,128)(2,1)S(1)}, bf16[640,256]{1,0:T(8,128)(2,1)S(1)}, u32[]{:S(2)}, u32[]{:S(2)}) collective-permute-start(bf16[640,256]{1,0:T(8,128)(2,1)S(1)} %get-tuple-element.46), channel_id=1, source_target_pairs={{0,4},{4,0},{8,12},{12,8},{16,20},{20,16},{24,28},{28,24},{32,36},... | collective-permute-start | bytes 983048 | tf_op jit(solution)/shard_map/ppermute | solution.py:51
  30.9 7.0 %collective-permute-start.5 = (bf16[80,256]{1,0:T(8,128)(2,1)S(1)}, bf16[80,256]{1,0:T(8,128)(2,1)S(1)}, u32[]{:S(2)}, u32[]{:S(2)}) collective-permute-start(bf16[80,256]{1,0:T(8,128)(2,1)S(1)} %get-tuple-element.48), channel_id=1, source_target_pairs={{0,8},{4,12},{8,0},{12,4},{16,24},{20,28},{24,16},{28,20},{32,40},... | collective-permute-start | bytes 122888 | tf_op jit(solution)/shard_map/ppermute | solution.py:51
  31.0 8.6 %collective-permute-start.6 = (bf16[80,256]{1,0:T(8,128)(2,1)S(1)}, bf16[80,256]{1,0:T(8,128)(2,1)S(1)}, u32[]{:S(2)}, u32[]{:S(2)}) collective-permute-start(bf16[80,256]{1,0:T(8,128)(2,1)S(1)} %get-tuple-element.49), channel_id=1, source_target_pairs={{0,16},{4,20},{8,24},{12,28},{16,0},{20,4},{24,8},{28,12},{32,48},... | collective-permute-start | bytes 122888 | tf_op jit(solution)/shard_map/ppermute | solution.py:51
  32.2 10.5 %collective-permute-start.7 = (bf16[80,256]{1,0:T(8,128)(2,1)S(1)}, bf16[80,256]{1,0:T(8,128)(2,1)S(1)}, u32[]{:S(2)}, u32[]{:S(2)}) collective-permute-start(bf16[80,256]{1,0:T(8,128)(2,1)S(1)} %get-tuple-element.50), channel_id=1, source_target_pairs={{0,24},{4,28},{8,16},{12,20},{16,8},{20,12},{24,0},{28,4},{32,56},... | collective-permute-start | bytes 122888 | tf_op jit(solution)/shard_map/ppermute | solution.py:51
  34.6 10.4 %collective-permute-start.8 = (bf16[80,256]{1,0:T(8,128)(2,1)S(1)}, bf16[80,256]{1,0:T(8,128)(2,1)S(1)}, u32[]{:S(2)}, u32[]{:S(2)}) collective-permute-start(bf16[80,256]{1,0:T(8,128)(2,1)S(1)} %get-tuple-element.51), channel_id=1, source_target_pairs={{0,32},{4,36},{8,40},{12,44},{16,48},{20,52},{24,56},{28,60},{32,0... | collective-permute-start | bytes 122888 | tf_op jit(solution)/shard_map/ppermute | solution.py:51
  34.7 10.3 %collective-permute-start.9 = (bf16[80,256]{1,0:T(8,128)(2,1)S(1)}, bf16[80,256]{1,0:T(8,128)(2,1)S(1)}, u32[]{:S(2)}, u32[]{:S(2)}) collective-permute-start(bf16[80,256]{1,0:T(8,128)(2,1)S(1)} %get-tuple-element.52), channel_id=1, source_target_pairs={{0,40},{4,44},{8,32},{12,36},{16,56},{20,60},{24,48},{28,52},{32,8... | collective-permute-start | bytes 122888 | tf_op jit(solution)/shard_map/ppermute | solution.py:51
  38.0 12.8 %collective-permute-start.10 = (bf16[80,256]{1,0:T(8,128)(2,1)S(1)}, bf16[80,256]{1,0:T(8,128)(2,1)S(1)}, u32[]{:S(2)}, u32[]{:S(2)}) collective-permute-start(bf16[80,256]{1,0:T(8,128)(2,1)S(1)} %get-tuple-element.53), channel_id=1, source_target_pairs={{0,48},{4,52},{8,56},{12,60},{16,32},{20,36},{24,40},{28,44},{32,1... | collective-permute-start | bytes 122888 | tf_op jit(solution)/shard_map/ppermute | solution.py:51
  39.6 11.2 %collective-permute-start.11 = (bf16[80,256]{1,0:T(8,128)(2,1)S(1)}, bf16[80,256]{1,0:T(8,128)(2,1)S(1)}, u32[]{:S(2)}, u32[]{:S(2)}) collective-permute-start(bf16[80,256]{1,0:T(8,128)(2,1)S(1)} %get-tuple-element.54), channel_id=1, source_target_pairs={{0,56},{4,60},{8,48},{12,52},{16,40},{20,44},{24,32},{28,36},{32,2... | collective-permute-start | bytes 122888 | tf_op jit(solution)/shard_map/ppermute | solution.py:51
  42.6 22.2 %collective-permute-start.23 = (bf16[256,256]{1,0:T(8,128)(2,1)S(1)}, bf16[256,256]{1,0:T(8,128)(2,1)S(1)}, u32[]{:S(2)}, u32[]{:S(2)}) collective-permute-start(bf16[256,256]{1,0:T(8,128)(2,1)S(1)} %get-tuple-element.59), channel_id=1, source_target_pairs={{0,252},{4,0},{8,4},{12,8},{16,12},{20,16},{24,20},{28,24},{32,28}... | collective-permute-start | bytes 393224 | tf_op jit(solution)/shard_map/ppermute | solution.py:46
  45.0 19.9 %collective-permute-start.24 = (bf16[256,256]{1,0:T(8,128)(2,1)S(1)}, bf16[256,256]{1,0:T(8,128)(2,1)S(1)}, u32[]{:S(2)}, u32[]{:S(2)}) collective-permute-start(bf16[256,256]{1,0:T(8,128)(2,1)S(1)} %get-tuple-element.60), channel_id=1, source_target_pairs={{0,4},{4,8},{8,12},{12,16},{16,20},{20,24},{24,28},{28,32},{32,36}... | collective-permute-start | bytes 393224 | tf_op jit(solution)/shard_map/ppermute | solution.py:46
  45.0 20.0 %collective-permute-start.25 = (bf16[256,256]{1,0:T(8,128)(2,1)S(1)}, bf16[256,256]{1,0:T(8,128)(2,1)S(1)}, u32[]{:S(2)}, u32[]{:S(2)}) collective-permute-start(bf16[256,256]{1,0:T(8,128)(2,1)S(1)} %get-tuple-element.61), channel_id=1, source_target_pairs={{0,248},{4,252},{8,0},{12,4},{16,8},{20,12},{24,16},{28,20},{32,24... | collective-permute-start | bytes 393224 | tf_op jit(solution)/shard_map/ppermute | solution.py:46
  50.8 14.2 %collective-permute-start.26 = (bf16[256,256]{1,0:T(8,128)(2,1)S(1)}, bf16[256,256]{1,0:T(8,128)(2,1)S(1)}, u32[]{:S(2)}, u32[]{:S(2)}) collective-permute-start(bf16[256,256]{1,0:T(8,128)(2,1)S(1)} %get-tuple-element.62), channel_id=1, source_target_pairs={{0,8},{4,12},{8,16},{12,20},{16,24},{20,28},{24,32},{28,36},{32,40... | collective-permute-start | bytes 393224 | tf_op jit(solution)/shard_map/ppermute | solution.py:46
  50.9 4.2 %collective-permute-start.14 = (bf16[80,256]{1,0:T(8,128)(2,1)S(1)}, bf16[80,256]{1,0:T(8,128)(2,1)S(1)}, u32[]{:S(2)}, u32[]{:S(2)}) collective-permute-start(bf16[80,256]{1,0:T(8,128)(2,1)S(1)} %shard_map.133.a), channel_id=1, source_target_pairs={{0,192},{4,196},{8,200},{12,204},{16,208},{20,212},{24,216},{28,22... | collective-permute-start | bytes 122888 | tf_op jit(solution)/shard_map/ppermute | solution.py:51
  55.0 4.5 %collective-permute-start.13 = (bf16[80,256]{1,0:T(8,128)(2,1)S(1)}, bf16[80,256]{1,0:T(8,128)(2,1)S(1)}, u32[]{:S(2)}, u32[]{:S(2)}) collective-permute-start(bf16[80,256]{1,0:T(8,128)(2,1)S(1)} %shard_map.133.a), channel_id=1, source_target_pairs={{0,128},{4,132},{8,136},{12,140},{16,144},{20,148},{24,152},{28,15... | collective-permute-start | bytes 122888 | tf_op jit(solution)/shard_map/ppermute | solution.py:51
  59.5 2.9 %collective-permute-start.12 = (bf16[80,256]{1,0:T(8,128)(2,1)S(1)}, bf16[80,256]{1,0:T(8,128)(2,1)S(1)}, u32[]{:S(2)}, u32[]{:S(2)}) collective-permute-start(bf16[80,256]{1,0:T(8,128)(2,1)S(1)} %shard_map.133.a), channel_id=1, source_target_pairs={{0,64},{4,68},{8,72},{12,76},{16,80},{20,84},{24,88},{28,92},{32,9... | collective-permute-start | bytes 122888 | tf_op jit(solution)/shard_map/ppermute | solution.py:51
  62.4 8.6 %collective-permute-start.21 = (bf16[80,256]{1,0:T(8,128)(2,1)S(1)}, bf16[80,256]{1,0:T(8,128)(2,1)S(1)}, u32[]{:S(2)}, u32[]{:S(2)}) collective-permute-start(bf16[80,256]{1,0:T(8,128)(2,1)S(1)} %shard_map.134.own), channel_id=1, source_target_pairs={{0,56},{4,60},{8,48},{12,52},{16,40},{20,44},{24,32},{28,36},{32,2... | collective-permute-start | bytes 122888 | tf_op jit(solution)/shard_map/ppermute | solution.py:51
  64.9 6.2 %collective-permute-start.20 = (bf16[80,256]{1,0:T(8,128)(2,1)S(1)}, bf16[80,256]{1,0:T(8,128)(2,1)S(1)}, u32[]{:S(2)}, u32[]{:S(2)}) collective-permute-start(bf16[80,256]{1,0:T(8,128)(2,1)S(1)} %shard_map.134.own), channel_id=1, source_target_pairs={{0,48},{4,52},{8,56},{12,60},{16,32},{20,36},{24,40},{28,44},{32,1... | collective-permute-start | bytes 122888 | tf_op jit(solution)/shard_map/ppermute | solution.py:51
  64.9 11.8 %collective-permute-start.19 = (bf16[80,256]{1,0:T(8,128)(2,1)S(1)}, bf16[80,256]{1,0:T(8,128)(2,1)S(1)}, u32[]{:S(2)}, u32[]{:S(2)}) collective-permute-start(bf16[80,256]{1,0:T(8,128)(2,1)S(1)} %shard_map.134.own), channel_id=1, source_target_pairs={{0,40},{4,44},{8,32},{12,36},{16,56},{20,60},{24,48},{28,52},{32,8... | collective-permute-start | bytes 122888 | tf_op jit(solution)/shard_map/ppermute | solution.py:51
  67.0 25.0 %collective-permute-start.27 = (bf16[160,512]{1,0:T(8,128)(2,1)S(1)}, bf16[160,512]{1,0:T(8,128)(2,1)S(1)}, u32[]{:S(2)}, u32[]{:S(2)}) collective-permute-start(bf16[160,512]{1,0:T(8,128)(2,1)S(1)} %get-tuple-element.65), channel_id=1, source_target_pairs={{0,1},{1,0},{2,3},{3,2},{4,5},{5,4},{6,7},{7,6},{8,9},{9,8},{10,11... | collective-permute-start | bytes 491528 | tf_op jit(solution)/shard_map/ppermute | solution.py:55
  68.4 23.6 %collective-permute-start.28 = (bf16[160,512]{1,0:T(8,128)(2,1)S(1)}, bf16[160,512]{1,0:T(8,128)(2,1)S(1)}, u32[]{:S(2)}, u32[]{:S(2)}) collective-permute-start(bf16[160,512]{1,0:T(8,128)(2,1)S(1)} %get-tuple-element.66), channel_id=1, source_target_pairs={{0,2},{1,3},{2,0},{3,1},{4,6},{5,7},{6,4},{7,5},{8,10},{9,11},{10,... | collective-permute-start | bytes 491528 | tf_op jit(solution)/shard_map/ppermute | solution.py:55
  71.1 21.0 %collective-permute-start.29 = (bf16[160,512]{1,0:T(8,128)(2,1)S(1)}, bf16[160,512]{1,0:T(8,128)(2,1)S(1)}, u32[]{:S(2)}, u32[]{:S(2)}) collective-permute-start(bf16[160,512]{1,0:T(8,128)(2,1)S(1)} %get-tuple-element.67), channel_id=1, source_target_pairs={{0,3},{1,2},{2,1},{3,0},{4,7},{5,6},{6,5},{7,4},{8,11},{9,10},{10,... | collective-permute-start | bytes 491528 | tf_op jit(solution)/shard_map/ppermute | solution.py:55
  71.1 7.0 %collective-permute-start.18 = (bf16[80,256]{1,0:T(8,128)(2,1)S(1)}, bf16[80,256]{1,0:T(8,128)(2,1)S(1)}, u32[]{:S(2)}, u32[]{:S(2)}) collective-permute-start(bf16[80,256]{1,0:T(8,128)(2,1)S(1)} %shard_map.134.own), channel_id=1, source_target_pairs={{0,32},{4,36},{8,40},{12,44},{16,48},{20,52},{24,56},{28,60},{32,0... | collective-permute-start | bytes 122888 | tf_op jit(solution)/shard_map/ppermute | solution.py:51
  76.7 4.7 %collective-permute-start.17 = (bf16[80,256]{1,0:T(8,128)(2,1)S(1)}, bf16[80,256]{1,0:T(8,128)(2,1)S(1)}, u32[]{:S(2)}, u32[]{:S(2)}) collective-permute-start(bf16[80,256]{1,0:T(8,128)(2,1)S(1)} %shard_map.134.own), channel_id=1, source_target_pairs={{0,24},{4,28},{8,16},{12,20},{16,8},{20,12},{24,0},{28,4},{32,56},... | collective-permute-start | bytes 122888 | tf_op jit(solution)/shard_map/ppermute | solution.py:51
  78.1 6.0 %collective-permute-start.16 = (bf16[80,256]{1,0:T(8,128)(2,1)S(1)}, bf16[80,256]{1,0:T(8,128)(2,1)S(1)}, u32[]{:S(2)}, u32[]{:S(2)}) collective-permute-start(bf16[80,256]{1,0:T(8,128)(2,1)S(1)} %shard_map.134.own), channel_id=1, source_target_pairs={{0,16},{4,20},{8,24},{12,28},{16,0},{20,4},{24,8},{28,12},{32,48},... | collective-permute-start | bytes 122888 | tf_op jit(solution)/shard_map/ppermute | solution.py:51
  81.3 4.7 %collective-permute-start.15 = (bf16[80,256]{1,0:T(8,128)(2,1)S(1)}, bf16[80,256]{1,0:T(8,128)(2,1)S(1)}, u32[]{:S(2)}, u32[]{:S(2)}) collective-permute-start(bf16[80,256]{1,0:T(8,128)(2,1)S(1)} %shard_map.134.own), channel_id=1, source_target_pairs={{0,8},{4,12},{8,0},{12,4},{16,24},{20,28},{24,16},{28,20},{32,40},... | collective-permute-start | bytes 122888 | tf_op jit(solution)/shard_map/ppermute | solution.py:51
  86.1 7.2 %collective-permute-start.22 = (bf16[640,256]{1,0:T(8,128)(2,1)S(1)}, bf16[640,256]{1,0:T(8,128)(2,1)S(1)}, u32[]{:S(2)}, u32[]{:S(2)}) collective-permute-start(bf16[640,256]{1,0:T(8,128)(2,1)S(1)} %shard_map.135.mine), channel_id=1, source_target_pairs={{0,4},{4,0},{8,12},{12,8},{16,20},{20,16},{24,28},{28,24},{32,36},... | collective-permute-start | bytes 983048 | tf_op jit(solution)/shard_map/ppermute | solution.py:51
  (9 other events, 11.5 us)

commit v2 on v1

v2 whole, which is shorter than its diff:
```python
import functools
import math

import jax
import jax.numpy as jnp
from jax import lax
from jax.experimental import pallas as pl
from jax.experimental.pallas import tpu as pltpu
from jax.sharding import PartitionSpec as P

BS = 128
BLK = 4
K_IN = 8
ROUNDS = 4
NB = 2
CORES = 2
Z = 8
X = 4
HID = 4
CHIPS = X * Z
PIECE = (40, 128)
BF16 = jnp.bfloat16
F32 = jnp.float32

VMEM = pl.BlockSpec(memory_space=pltpu.VMEM)
HBM = pl.BlockSpec(memory_space=pltpu.MemorySpace.HBM)
DMA = pltpu.SemaphoreType.DMA


def dot(a, b, dims=((1,), (0,))):
    return lax.dot_general(a, b, (dims, ((), ())), preferred_element_type=F32)


def call(kernel, outs, specs, flops=0, nbytes=0, limit=24, scratch=()):
    return pl.pallas_call(
        kernel,
        out_shape=[jax.ShapeDtypeStruct(shape, dtype) for shape, dtype in outs],
        in_specs=specs,
        out_specs=[VMEM] * len(outs),
        scratch_shapes=list(scratch),
        compiler_params=pltpu.CompilerParams(vmem_limit_bytes=limit * 1024 * 1024),
        cost_estimate=pl.CostEstimate(flops=flops, bytes_accessed=nbytes, transcendentals=0),
    )


def dom_swap(array, mask):
    count = lax.axis_size("dom")
    return lax.ppermute(array, "dom", [(i, i ^ mask) for i in range(count)])


def dom_pairs(array, step):
    count = lax.axis_size("dom")
    odd = [i for i in range(count) if (i // step) % 2]
    pairs = [(i, (i + step) % count) for i in odd]
    return lax.ppermute(array, "dom", pairs + [(j, i) for i, j in pairs])


def hid_swap(array, mask):
    return lax.ppermute(array, "hid", [(i, i ^ mask) for i in range(HID)])


def exchange(array):
    groups = [[CORES * chip + core for chip in range(CHIPS)] for core in range(CORES)]
    return lax.all_to_all(array, "dom", 0, 0, axis_index_groups=groups)


def rows(block, size=BS):
    return pl.ds(pl.multiple_of(block * size, size), size)


def swaps(arrays):
    a, b, c, d = arrays
    return [dom_swap(a, 1), dom_swap(b, 2), dom_pairs(c, 2), dom_pairs(d, 1)]


def sent_rounds():
    me = lax.axis_index("dom")
    core, chip = lax.rem(me, CORES), lax.rem(me // CORES, 2)
    return (core, 2 + chip, 3 - chip, 1 - core)


def received_rounds():
    first, second, third, fourth = sent_rounds()
    return (1 - first, 5 - second, 5 - third, 1 - fourth)


def pack_kernel(send, feats, out0, out1, out2, out3, send_now, sems):
    copy = pltpu.make_async_copy(send, send_now, sems.at[ROUNDS * NB])
    copy.start()
    copy.wait()
    copies = []
    for i, (r, out) in enumerate(zip(sent_rounds(), (out0, out1, out2, out3))):
        for s in range(NB):
            copies.append(
                pltpu.make_async_copy(
                    feats.at[rows(send_now[0, s, r]), :],
                    out.at[pl.ds(s * BS, BS), :],
                    sems.at[i * NB + s],
                )
            )
            copies[-1].start()
    for copy in copies:
        copy.wait()


def before_kernel(
    neighbors,
    recv,
    live,
    feats,
    self_w,
    tiles,
    edge_tiles,
    local,
    edge,
    local_sum,
    degree,
    own_pre,
    neighbors_now,
    recv_now,
    live_now,
    feats_now,
    self_w_now,
    tiles_now,
    edge_tiles_now,
    sems,
):
    pairs = (
        (neighbors, neighbors_now),
        (recv, recv_now),
        (live, live_now),
        (tiles, tiles_now),
        (edge_tiles, edge_tiles_now),
        (feats, feats_now),
        (self_w, self_w_now),
    )
    copies = [pltpu.make_async_copy(a, b, sems.at[i]) for i, (a, b) in enumerate(pairs)]
    for copy in copies:
        copy.start()
    local[...] = jnp.zeros_like(local)
    edge[...] = jnp.zeros_like(edge)
    for copy in copies:
        copy.wait()
    for b in range(BLK):
        for k in range(K_IN):
            cols = rows(neighbors_now[0, b, k])
            here = slice(b * BS, (b + 1) * BS)
            local[here, cols] = local[here, cols] + tiles_now[0, b, k]
    for i, r in enumerate(received_rounds()):
        for s in range(NB):
            slot = i * NB + s

            @pl.when(s < live_now[0, r])
            def _():
                edge[rows(recv_now[0, s, r]), slot * BS : (slot + 1) * BS] = edge_tiles_now[0, r, s]

    mine = feats_now[...]
    own_pre[...] = dot(mine, self_w_now[...])
    whole = local[...]
    local_sum[...] = dot(whole, mine)
    ones = jnp.ones((BS * BLK, BS), BF16)
    edge_ones = jnp.ones((BS * NB * ROUNDS, BS), BF16)
    degree[...] = dot(whole, ones) + dot(edge[...], edge_ones)


def middle_kernel(
    edge,
    got0,
    got1,
    got2,
    got3,
    local_sum,
    degree,
    own_pre,
    neigh_w,
    cot,
    feats,
    activated,
    low_out,
    spread_out,
    keep,
    give,
    term0,
    term1,
    term2,
    term3,
):
    core = lax.rem(lax.axis_index("dom"), CORES)
    width = NB * BS
    total = local_sum[...]
    for r, got in enumerate((got0, got1, got2, got3)):
        total = total + dot(edge[:, r * width : (r + 1) * width], got[...])
    inverse = 1.0 / degree[...]
    mean = total * jnp.concatenate([inverse] * (total.shape[1] // BS), axis=1)
    mean_high = mean.astype(BF16)
    mean_rest = (mean - mean_high.astype(F32)).astype(BF16)
    weights = neigh_w[...]
    pre = own_pre[...] + dot(mean_high, weights) + dot(mean_rest, weights)
    sig = jax.nn.sigmoid(pre)
    activated[...] = (pre * sig).astype(BF16)
    grad = cot[...].astype(F32) * sig * (1.0 + pre * (1.0 - sig))
    low = grad.astype(BF16)
    low_out[...] = low
    spread = (grad * jnp.concatenate([inverse] * (grad.shape[1] // BS), axis=1)).astype(BF16)
    spread_out[...] = spread
    over_rows = ((0,), (0,))
    of_self = dot(feats[...], low, over_rows)
    of_neigh = dot(mean_high, low, over_rows)

    @pl.when(core == 0)
    def _():
        keep[...] = of_self
        give[...] = of_neigh.astype(BF16)

    @pl.when(core == 1)
    def _():
        keep[...] = of_neigh
        give[...] = of_self.astype(BF16)

    for r, term in enumerate((term0, term1, term2, term3)):
        term[...] = dot(edge[:, r * width : (r + 1) * width], spread, over_rows).astype(BF16)


def piece_at(i):
    return (i % 16) * PIECE[0], (i // 16) * PIECE[1]


def cut_kernel(keep, got, out):
    total = keep[...] + got[...].astype(F32)
    for i in range(CHIPS):
        at, lane = piece_at(i)
        out[i] = total[at : at + PIECE[0], lane : lane + PIECE[1]].astype(BF16)


def sum_kernel(got, out):
    done = jnp.sum(got[...].astype(F32), axis=0).astype(BF16)
    for i in range(CHIPS):
        out[i] = done


def last_kernel(scale, mine, other, of_self, of_neigh):
    core = lax.rem(lax.axis_index("dom"), CORES)

    def put(a, out):
        for i in range(CHIPS):
            at, lane = piece_at(i)
            out[at : at + PIECE[0], lane : lane + PIECE[1]] = a[i].astype(F32) * scale

    @pl.when(core == 0)
    def _():
        put(mine, of_self)
        put(other, of_neigh)

    @pl.when(core == 1)
    def _():
        put(other, of_self)
        put(mine, of_neigh)


def back_own_kernel(local, spread, low, self_w, back, part):
    back[...] = dot(local[...], spread[...], ((0,), (0,)))
    part[...] = dot(self_w[...], low[...], ((1,), (1,)))


def back_kernel(send, start, part, got0, got1, got2, got3, neigh_w, own, give1, give2, give3, back):
    back[...] = start[...]
    for r, got in zip(sent_rounds(), (got0, got1, got2, got3)):
        for s in range(NB):
            at = rows(send[0, s, r])
            back[at, :] = back[at, :] + got[s * BS : (s + 1) * BS, :].astype(F32)
    back_low = back[...].astype(BF16)
    y = lax.axis_index("hid")
    size = own.shape[0]
    for k in range(HID):
        at = rows(jnp.bitwise_xor(y, k), size)
        total = part[at, :] + dot(neigh_w[at, :], back_low, ((1,), (1,)))
        if k == 0:
            own[...] = total
        else:
            (give1, give2, give3)[k - 1][...] = total.astype(BF16)


def on_device(
    features,
    self_weight,
    neigh_weight,
    cotangent,
    neighbor_blocks,
    local_tiles,
    send_blocks,
    recv_blocks,
    live_slots,
    boundary_tiles,
):
    n, width = features.shape
    hidden = self_weight.shape[1]
    slots = ROUNDS * NB * BS
    send_blocks = jnp.swapaxes(send_blocks, 1, 2)
    recv_blocks = jnp.swapaxes(recv_blocks, 1, 2)
    packed = call(
        pack_kernel,
        [((NB * BS, width), BF16)] * ROUNDS,
        [HBM] * 2,
        nbytes=2_000_000,
        scratch=[pltpu.SMEM((1, NB, ROUNDS), jnp.int32), DMA((ROUNDS * NB + 1,))],
    )(send_blocks, features)
    received = swaps(packed)
    local, edge, local_sum, degree, own_pre = call(
        before_kernel,
        [((n, n), BF16), ((n, slots), BF16), ((n, width), F32), ((n, BS), F32), ((n, hidden), F32)],
        [HBM] * 7,
        flops=1_000_000_000,
        nbytes=6_000_000,
        scratch=[
            pltpu.SMEM((1, BLK, K_IN), jnp.int32),
            pltpu.SMEM((1, NB, ROUNDS), jnp.int32),
            pltpu.SMEM((1, ROUNDS), jnp.int32),
            pltpu.VMEM((n, width), BF16),
            pltpu.VMEM((width, hidden), BF16),
            pltpu.VMEM((1, BLK, K_IN, BS, BS), BF16),
            pltpu.VMEM((1, ROUNDS, NB, BS, BS), BF16),
            DMA((7,)),
        ],
    )(
        neighbor_blocks,
        recv_blocks,
        live_slots,
        features,
        self_weight,
        local_tiles,
        boundary_tiles,
    )
    activated, low, spread, keep, give, *terms = call(
        middle_kernel,
        [((n, hidden), BF16)] * 3
        + [((width, hidden), F32), ((width, hidden), BF16)]
        + [((NB * BS, hidden), BF16)] * ROUNDS,
        [VMEM] * 11,
        flops=1_600_000_000,
        nbytes=8_000_000,
        limit=32,
    )(edge, *received, local_sum, degree, own_pre, neigh_weight, cotangent, features)

    got = dom_swap(give, 1)
    returned = swaps(terms)
    back, in_part = call(
        back_own_kernel,
        [((n, hidden), F32), ((width, n), F32)],
        [VMEM] * 4,
        flops=300_000_000,
        nbytes=3_000_000,
    )(local, spread, low, self_weight)
    got, back, in_part = lax.optimization_barrier((got, back, in_part))
    pieces = (CHIPS,) + PIECE
    (cut,) = call(cut_kernel, [(pieces, BF16)], [VMEM] * 2, nbytes=1_500_000)(keep, got)
    (summed,) = call(sum_kernel, [(pieces, BF16)], [VMEM], nbytes=700_000)(exchange(cut))
    shape = (width // HID, n)
    in_own, *in_gives = call(
        back_kernel,
        [(shape, F32)] + [(shape, BF16)] * (HID - 1),
        [pl.BlockSpec(memory_space=pltpu.SMEM)] + [VMEM] * 7,
        flops=300_000_000,
        nbytes=3_000_000,
        scratch=[pltpu.VMEM((n, hidden), F32)],
    )(send_blocks, back, in_part, *returned, neigh_weight)
    summed, *in_gives = lax.optimization_barrier((summed, *in_gives))
    in_parts = [hid_swap(in_gives[k - 1], k) for k in range(1, HID)]
    mine = exchange(summed)
    other = dom_swap(mine, 1)
    scale = 1.0 / math.sqrt(n * lax.axis_size("dom"))
    grad_self, grad_neigh = call(
        functools.partial(last_kernel, scale),
        [((width, hidden), F32)] * 2,
        [VMEM] * 2,
        nbytes=2_000_000,
    )(mine, other)
    grad_input = in_own
    for part in in_parts:
        grad_input = grad_input + part.astype(F32)
    return activated, grad_self, grad_neigh, grad_input.astype(BF16).T


def solution(mesh):
    return jax.shard_map(
        on_device,
        mesh=mesh,
        in_specs=(
            P("dom", None),
            P(None, "hid"),
            P(None, "hid"),
            P("dom", "hid"),
            P("dom", None, None),
            P("dom", None, None, None, None),
            P("dom", None, None),
            P("dom", None, None),
            P("dom", None),
            P("dom", None, None, None, None),
        ),
        out_specs=(P("dom", "hid"), P(None, "hid"), P(None, "hid"), P("dom", "hid")),
        check_vma=False,
    )
```

time: 94.8 us -> 79.8 us (0.84)
  starting transfers between devices: 58 us -> 41.8 us
  Pallas kernels: 9.51 us -> 12.2 us
  waiting for transfers between devices: 17.1 us -> 15.7 us
    ppermute x19 -> x6, starting transfers between devices: 36.4 us -> 12.9 us  [dom_swap(): return lax.ppermute(array, 'dom', [(i, i ^ mask) for i in range(count)])]
    all_to_all x0 -> x2, starting transfers between devices: none -> 13.5 us  [exchange(): return lax.all_to_all(array, 'dom', 0, 0, axis_index_groups=groups)]
    ppermute x19 -> x6, waiting for transfers between devices: 17.1 us -> 6.04 us  [dom_swap(): return lax.ppermute(array, 'dom', [(i, i ^ mask) for i in range(count)])]
    all_to_all x0 -> x2, waiting for transfers between devices: none -> 6.43 us  [exchange(): return lax.all_to_all(array, 'dom', 0, 0, axis_index_groups=groups)]
    ppermute x8 -> x4, starting transfers between devices: 17.6 us -> 11.4 us  [dom_pairs(): return lax.ppermute(array, 'dom', pairs + [(j, i) for i, j in pairs])]
    ppermute x8 -> x4, waiting for transfers between devices: 0.09 us -> 3.2 us  [dom_pairs(): return lax.ppermute(array, 'dom', pairs + [(j, i) for i, j in pairs])]
    pallas_call x6 -> x5, Pallas kernels: 2.87 us -> 5.65 us  [the longest x1 2.39 us: on_device(): call(pack_kernel, [((NB * BS, width), BF16)] * ROUNDS, [HBM] * 2, nbytes=...]
    unnamed x24 -> x28, local copies, waits for them, and re-layouts: 8.2 us -> 8.03 us
  transfers between devices with their start and end apart: 30 -> 15, of which waited for: 9 -> 5; matrix products, arithmetic and copies ran while one was open for 2% -> 1% of each run, Pallas kernels for 5% -> 5%
where the time goes in v2:
time: 79.8 us; the launch traced here: 79.3 us
  starting transfers between devices  41.8 us (52%)
  waiting for transfers between devices  15.7 us (20%)
  Pallas kernels  12.2 us (15%)
  local copies, waits for them, and re-layouts  8.03 us (10%)
    all_to_all x2, starting transfers between devices, exchange(): return lax.all_to_all(array, 'dom', 0, 0, axis_index_groups=groups)  13.5 us
    ppermute x6, starting transfers between devices, dom_swap(): return lax.ppermute(array, 'dom', [(i, i ^ mask) for i in range(count)])  12.9 us
    ppermute x4, starting transfers between devices, dom_pairs(): return lax.ppermute(array, 'dom', pairs + [(j, i) for i, j in pairs])  11.4 us
    unnamed x28, local copies, waits for them, and re-layouts  8.03 us
    all_to_all x2, waiting for transfers between devices, exchange(): return lax.all_to_all(array, 'dom', 0, 0, axis_index_groups=groups)  6.43 us
    ppermute x6, waiting for transfers between devices, dom_swap(): return lax.ppermute(array, 'dom', [(i, i ^ mask) for i in range(count)])  6.04 us
    ppermute x3, starting transfers between devices, hid_swap(): return lax.ppermute(array, 'hid', [(i, i ^ mask) for i in range(HID)])  4.01 us
    ppermute x4, waiting for transfers between devices, dom_pairs(): return lax.ppermute(array, 'dom', pairs + [(j, i) for i, j in pairs])  3.2 us
  transfers between devices with their start and end apart: 15, of which 5 were waited for; matrix products, arithmetic and copies ran while one was open for 1% of the time, Pallas kernels for 5%

profile of v2, /device:TPU:1, one launch (start us, length us, event | category | flops | bytes accessed | tf_op | source)
XLA Modules:
  0.0 79.3 jit_solution(10485507238175521012)
XLA Ops:
  0.6 1.1 %copy-done = bf16[512,640]{1,0:T(8,128)(2,1)S(1)} copy-done((bf16[512,640]{1,0:T(8,128)(2,1)S(1)}, bf16[512,640]{1,0:T(8,128)(2,1)}, u32[]{:S(2)}) %copy-start) | copy-done | bytes 655384
  1.7 0.7 copy-done.6
  2.4 2.4 %shard_map.130 = (bf16[256,640]{1,0:T(8,128)(2,1)S(1)}, bf16[256,640]{1,0:T(8,128)(2,1)S(1)}, bf16[256,640]{1,0:T(8,128)(2,1)S(1)}, bf16[256,640]{1,0:T(8,128)(2,1)S(1)}) custom-call(s32[1,2,4]{2,1,0:T(2,128)S(1)} %bitcast.4, bf16[512,640]{1,0:T(8,128)(2,1)S(1)} %copy-done), custom_call_target="tpu_custom_call" | custom-call | bytes 2000000 | tf_op jit(solution)/shard_map/pallas_call | solution.py:300
  4.8 3.3 %collective-permute-start = (bf16[256,640]{1,0:T(8,128)(2,1)S(1)}, bf16[256,640]{1,0:T(8,128)(2,1)S(1)}, u32[]{:S(2)}, u32[]{:S(2)}) collective-permute-start(bf16[256,640]{1,0:T(8,128)(2,1)S(1)} %get-tuple-element.38), channel_id=1, source_target_pairs={{0,4},{4,0},{8,12},{12,8},{16,20},{20,16},{24,28},{28,24},{32,36},... | collective-permute-start | bytes 983048 | tf_op jit(solution)/shard_map/ppermute | solution.py:48
  8.1 6.8 %collective-permute-start.2 = (bf16[256,640]{1,0:T(8,128)(2,1)S(1)}, bf16[256,640]{1,0:T(8,128)(2,1)S(1)}, u32[]{:S(2)}, u32[]{:S(2)}) collective-permute-start(bf16[256,640]{1,0:T(8,128)(2,1)S(1)} %get-tuple-element.40), channel_id=1, source_target_pairs={{8,16},{12,20},{24,32},{28,36},{40,48},{44,52},{56,64},{60,68},{72... | collective-permute-start | bytes 983048 | tf_op jit(solution)/shard_map/ppermute | solution.py:55
  14.9 1.1 %copy-done.1 = bf16[512,640]{1,0:T(8,128)(2,1)S(1)} copy-done((bf16[512,640]{1,0:T(8,128)(2,1)S(1)}, bf16[512,640]{1,0:T(8,128)(2,1)}, u32[]{:S(2)}) %copy-start.1) | copy-done | bytes 655384
  16.0 1.0 %copy-done.4 = bf16[640,256]{1,0:T(8,128)(2,1)S(1)} copy-done((bf16[640,256]{1,0:T(8,128)(2,1)S(1)}, bf16[640,256]{1,0:T(8,128)(2,1)}, u32[]{:S(2)}) %copy-start.4) | copy-done | bytes 327704
  17.0 1.2 %copy-done.8 = bf16[1,4,8,128,128]{4,3,2,1,0:T(8,128)(2,1)S(1)} copy-done((bf16[1,4,8,128,128]{4,3,2,1,0:T(8,128)(2,1)S(1)}, bf16[1,4,8,128,128]{4,3,2,1,0:T(8,128)(2,1)}, u32[]{:S(2)}) %copy-start.8) | copy-done | bytes 1048600
  18.2 0.9 %copy-done.9 = bf16[1,4,2,128,128]{4,3,2,1,0:T(8,128)(2,1)S(1)} copy-done((bf16[1,4,2,128,128]{4,3,2,1,0:T(8,128)(2,1)S(1)}, bf16[1,4,2,128,128]{4,3,2,1,0:T(8,128)(2,1)}, u32[]{:S(2)}) %copy-start.9) | copy-done | bytes 262168
  19.1 0.7 copy-done.11
  19.8 0.7 copy-done.12
  20.5 0.7 copy-done.13
  21.2 2.2 %shard_map.129 = (bf16[512,512]{1,0:T(8,128)(2,1)S(1)}, bf16[512,1024]{1,0:T(8,128)(2,1)S(1)}, f32[512,640]{1,0:T(8,128)S(1)}, f32[512,128]{1,0:T(8,128)S(1)}, f32[512,256]{1,0:T(8,128)S(1)}) custom-call(s32[1,4,8]{2,1,0:T(4,128)S(1)} %copy-done.11, s32[1,2,4]{2,1,0:T(2,128)S(1)} %bitcast.6, s32[1,4]{1,0:T(1,128)S(1)} %copy-done.13, ...), custom_call_target="tpu_custom_call" | custom-call | flops 1000000000 | bytes 6000000 | tf_op jit(solution)/shard_map/pallas_call | solution.py:308
  23.5 3.2 %shard_map.131 = (bf16[512,256]{1,0:T(8,128)(2,1)}, bf16[512,256]{1,0:T(8,128)(2,1)S(1)}, bf16[512,256]{1,0:T(8,128)(2,1)S(1)}, f32[640,256]{1,0:T(8,128)S(1)}, ...) custom-call(bf16[512,1024]{1,0:T(8,128)(2,1)S(1)} %get-tuple-element, ...), custom_call_target="tpu_custom_call" | custom-call | flops 1600000000 | bytes 8000000 | tf_op jit(solution)/shard_map/pallas_call | solution.py:333
  26.7 3.6 %collective-permute-start.4 = (bf16[640,256]{1,0:T(8,128)(2,1)S(1)}, bf16[640,256]{1,0:T(8,128)(2,1)S(1)}, u32[]{:S(2)}, u32[]{:S(2)}) collective-permute-start(bf16[640,256]{1,0:T(8,128)(2,1)S(1)} %get-tuple-element.47), channel_id=1, source_target_pairs={{0,4},{4,0},{8,12},{12,8},{16,20},{20,16},{24,28},{28,24},{32,36},... | collective-permute-start | bytes 983048 | tf_op jit(solution)/shard_map/ppermute | solution.py:48
  30.8 0.7 collective-permute-done.4.got
  31.6 0.8 shard_map.133
  32.4 6.1 %all-to-all-start = ((bf16[32,40,128]{2,1,0:T(8,128)(2,1)}), bf16[32,40,128]{2,1,0:T(8,128)(2,1)S(1)}, u32[]{:S(2)}, u32[]{:S(2)}) async-start(bf16[32,40,128]{2,1,0:T(8,128)(2,1)} %shard_map.133), calls=%async_computation | async-start | bytes 655360 | tf_op jit(solution)/shard_map/all_to_all | solution.py:64
  38.5 0.6 collective-permute-start.5
  39.0 1.5 %collective-permute-start.6 = (bf16[256,256]{1,0:T(8,128)(2,1)S(1)}, bf16[256,256]{1,0:T(8,128)(2,1)S(1)}, u32[]{:S(2)}, u32[]{:S(2)}) collective-permute-start(bf16[256,256]{1,0:T(8,128)(2,1)S(1)} %get-tuple-element.57), channel_id=1, source_target_pairs={{0,8},{4,12},{8,0},{12,4},{16,24},{20,28},{24,16},{28,20},{32,40},... | collective-permute-start | bytes 393224 | tf_op jit(solution)/shard_map/ppermute | solution.py:48
  40.6 4.6 %collective-permute-start.7 = (bf16[256,256]{1,0:T(8,128)(2,1)S(1)}, bf16[256,256]{1,0:T(8,128)(2,1)S(1)}, u32[]{:S(2)}, u32[]{:S(2)}) collective-permute-start(bf16[256,256]{1,0:T(8,128)(2,1)S(1)} %get-tuple-element.58), channel_id=1, source_target_pairs={{8,16},{12,20},{24,32},{28,36},{40,48},{44,52},{56,64},{60,68},{72... | collective-permute-start | bytes 393224 | tf_op jit(solution)/shard_map/ppermute | solution.py:55
  45.2 4.8 %collective-permute-done.6.got1 = bf16[256,256]{1,0:T(8,128)(2,1)S(1)} collective-permute-done((bf16[256,256]{1,0:T(8,128)(2,1)S(1)}, bf16[256,256]{1,0:T(8,128)(2,1)S(1)}, u32[]{:S(2)}, u32[]{:S(2)}) %collective-permute-start.6) | collective-permute-done | bytes 131104 | tf_op jit(solution)/shard_map/ppermute | solution.py:48
  50.0 3.2 %collective-permute-done.7.got2 = bf16[256,256]{1,0:T(8,128)(2,1)S(1)} collective-permute-done((bf16[256,256]{1,0:T(8,128)(2,1)S(1)}, bf16[256,256]{1,0:T(8,128)(2,1)S(1)}, u32[]{:S(2)}, u32[]{:S(2)}) %collective-permute-start.7) | collective-permute-done | bytes 131104 | tf_op jit(solution)/shard_map/ppermute | solution.py:55
  53.2 1.2 %shard_map.135 = (f32[160,512]{1,0:T(8,128)S(1)}, bf16[160,512]{1,0:T(8,128)(2,1)S(1)}, bf16[160,512]{1,0:T(8,128)(2,1)S(1)}, bf16[160,512]{1,0:T(8,128)(2,1)S(1)}) custom-call(s32[1,2,4]{2,1,0:T(2,128)S(1)} %bitcast.5, f32[512,256]{1,0:T(8,128)S(1)} %get-tuple-element.54.start, f32[640,512]{1,0:T(8,128)S(1)} %get-tuple-element.55.part, ...), custom_call_target="tpu_custom_call" | custom-call | flops 300000000 | bytes 3000000 | tf_op jit(solution)/shard_map/pallas_call | solution.py:358
  54.4 0.8 shard_map.134
  55.2 7.4 %all-to-all-start.1 = ((bf16[32,40,128]{2,1,0:T(8,128)(2,1)}), bf16[32,40,128]{2,1,0:T(8,128)(2,1)S(1)}, u32[]{:S(2)}, u32[]{:S(2)}) async-start(bf16[32,40,128]{2,1,0:T(8,128)(2,1)} %shard_map.134), calls=%async_computation.1 | async-start | bytes 655360 | tf_op jit(solution)/shard_map/all_to_all | solution.py:64
  62.6 1.4 %collective-permute-start.10 = (bf16[160,512]{1,0:T(8,128)(2,1)S(1)}, bf16[160,512]{1,0:T(8,128)(2,1)S(1)}, u32[]{:S(2)}, u32[]{:S(2)}) collective-permute-start(bf16[160,512]{1,0:T(8,128)(2,1)S(1)} %get-tuple-element.67), channel_id=1, source_target_pairs={{0,1},{1,0},{2,3},{3,2},{4,5},{5,4},{6,7},{7,6},{8,9},{9,8},{10,11... | collective-permute-start | bytes 491528 | tf_op jit(solution)/shard_map/ppermute | solution.py:59
  63.9 2.6 %collective-permute-start.11 = (bf16[160,512]{1,0:T(8,128)(2,1)S(1)}, bf16[160,512]{1,0:T(8,128)(2,1)S(1)}, u32[]{:S(2)}, u32[]{:S(2)}) collective-permute-start(bf16[160,512]{1,0:T(8,128)(2,1)S(1)} %get-tuple-element.68), channel_id=1, source_target_pairs={{0,2},{1,3},{2,0},{3,1},{4,6},{5,7},{6,4},{7,5},{8,10},{9,11},{10,... | collective-permute-start | bytes 491528 | tf_op jit(solution)/shard_map/ppermute | solution.py:59
  66.6 6.4 %all-to-all-done.1.mine = bf16[32,40,128]{2,1,0:T(8,128)(2,1)S(1)} async-done(((bf16[32,40,128]{2,1,0:T(8,128)(2,1)}), bf16[32,40,128]{2,1,0:T(8,128)(2,1)S(1)}, u32[]{:S(2)}, u32[]{:S(2)}) %all-to-all-start.1) | async-done | bytes 327712 | tf_op jit(solution)/shard_map/all_to_all | solution.py:64
  73.0 3.9 %collective-permute-start.9 = (bf16[32,40,128]{2,1,0:T(8,128)(2,1)S(1)}, bf16[32,40,128]{2,1,0:T(8,128)(2,1)S(1)}, u32[]{:S(2)}, u32[]{:S(2)}) collective-permute-start(bf16[32,40,128]{2,1,0:T(8,128)(2,1)S(1)} %all-to-all-done.1.mine), channel_id=1, source_target_pairs={{0,4},{4,0},{8,12},{12,8},{16,20},{20,16},{24,28},{28,24},{32,36},... | collective-permute-start | bytes 983048 | tf_op jit(solution)/shard_map/ppermute | solution.py:48
  76.9 0.7 fusion
  78.2 1.2 %shard_map.136 = (f32[640,256]{1,0:T(8,128)}, f32[640,256]{1,0:T(8,128)}) custom-call(bf16[32,40,128]{2,1,0:T(8,128)(2,1)S(1)} %all-to-all-done.1.mine, bf16[32,40,128]{2,1,0:T(8,128)(2,1)S(1)} %collective-permute-done.9.other), custom_call_target="tpu_custom_call" | custom-call | bytes 2000000 | tf_op jit(solution)/shard_map/pallas_call | solution.py:371
  (35 shorter events, 1.1 us)
Async XLA Ops:
  0.6 1.1 %copy-start = (bf16[512,640]{1,0:T(8,128)(2,1)S(1)}, bf16[512,640]{1,0:T(8,128)(2,1)}, u32[]{:S(2)}) copy-start(bf16[512,640]{1,0:T(8,128)(2,1)} %feats.5) | copy-start | bytes 1966084
  1.7 0.7 copy-start.6
  4.8 18.6 %collective-permute-start = (bf16[256,640]{1,0:T(8,128)(2,1)S(1)}, bf16[256,640]{1,0:T(8,128)(2,1)S(1)}, u32[]{:S(2)}, u32[]{:S(2)}) collective-permute-start(bf16[256,640]{1,0:T(8,128)(2,1)S(1)} %get-tuple-element.38), channel_id=1, source_target_pairs={{0,4},{4,0},{8,12},{12,8},{16,20},{20,16},{24,28},{28,24},{32,36},... | collective-permute-start | bytes 983048 | tf_op jit(solution)/shard_map/ppermute | solution.py:48
  8.1 15.3 %collective-permute-start.1 = (bf16[256,640]{1,0:T(8,128)(2,1)S(1)}, bf16[256,640]{1,0:T(8,128)(2,1)S(1)}, u32[]{:S(2)}, u32[]{:S(2)}) collective-permute-start(bf16[256,640]{1,0:T(8,128)(2,1)S(1)} %get-tuple-element.39), channel_id=1, source_target_pairs={{0,8},{4,12},{8,0},{12,4},{16,24},{20,28},{24,16},{28,20},{32,40},... | collective-permute-start | bytes 983048 | tf_op jit(solution)/shard_map/ppermute | solution.py:48
  8.1 15.3 %collective-permute-start.2 = (bf16[256,640]{1,0:T(8,128)(2,1)S(1)}, bf16[256,640]{1,0:T(8,128)(2,1)S(1)}, u32[]{:S(2)}, u32[]{:S(2)}) collective-permute-start(bf16[256,640]{1,0:T(8,128)(2,1)S(1)} %get-tuple-element.40), channel_id=1, source_target_pairs={{8,16},{12,20},{24,32},{28,36},{40,48},{44,52},{56,64},{60,68},{72... | collective-permute-start | bytes 983048 | tf_op jit(solution)/shard_map/ppermute | solution.py:55
  14.9 8.6 %collective-permute-start.3 = (bf16[256,640]{1,0:T(8,128)(2,1)S(1)}, bf16[256,640]{1,0:T(8,128)(2,1)S(1)}, u32[]{:S(2)}, u32[]{:S(2)}) collective-permute-start(bf16[256,640]{1,0:T(8,128)(2,1)S(1)} %get-tuple-element.41), channel_id=1, source_target_pairs={{4,8},{12,16},{20,24},{28,32},{36,40},{44,48},{52,56},{60,64},{68,... | collective-permute-start | bytes 983048 | tf_op jit(solution)/shard_map/ppermute | solution.py:55
  14.9 1.1 %copy-start.1 = (bf16[512,640]{1,0:T(8,128)(2,1)S(1)}, bf16[512,640]{1,0:T(8,128)(2,1)}, u32[]{:S(2)}) copy-start(bf16[512,640]{1,0:T(8,128)(2,1)} %feats.5) | copy-start | bytes 1966084
  16.0 1.0 %copy-start.4 = (bf16[640,256]{1,0:T(8,128)(2,1)S(1)}, bf16[640,256]{1,0:T(8,128)(2,1)}, u32[]{:S(2)}) copy-start(bf16[640,256]{1,0:T(8,128)(2,1)} %self_w.3) | copy-start | bytes 983044
  17.0 1.2 %copy-start.8 = (bf16[1,4,8,128,128]{4,3,2,1,0:T(8,128)(2,1)S(1)}, bf16[1,4,8,128,128]{4,3,2,1,0:T(8,128)(2,1)}, u32[]{:S(2)}) copy-start(bf16[1,4,8,128,128]{4,3,2,1,0:T(8,128)(2,1)} %tiles.1) | copy-start | bytes 3145732
  18.2 0.9 %copy-start.9 = (bf16[1,4,2,128,128]{4,3,2,1,0:T(8,128)(2,1)S(1)}, bf16[1,4,2,128,128]{4,3,2,1,0:T(8,128)(2,1)}, u32[]{:S(2)}) copy-start(bf16[1,4,2,128,128]{4,3,2,1,0:T(8,128)(2,1)} %edge_tiles.1) | copy-start | bytes 786436
  19.1 0.7 copy-start.11
  19.8 0.7 copy-start.12
  20.5 0.7 copy-start.13
  21.2 2.3 %copy-start.2 = (bf16[512,640]{1,0:T(8,128)(2,1)S(1)}, bf16[512,640]{1,0:T(8,128)(2,1)}, u32[]{:S(2)}) copy-start(bf16[512,640]{1,0:T(8,128)(2,1)} %feats.5) | copy-start | bytes 1966084
  21.2 2.3 %copy-start.3 = (bf16[640,256]{1,0:T(8,128)(2,1)S(1)}, bf16[640,256]{1,0:T(8,128)(2,1)}, u32[]{:S(2)}) copy-start(bf16[640,256]{1,0:T(8,128)(2,1)} %neigh_w.3) | copy-start | bytes 983044
  21.2 2.3 %copy-start.10 = (bf16[512,256]{1,0:T(8,128)(2,1)S(1)}, bf16[512,256]{1,0:T(8,128)(2,1)}, u32[]{:S(2)}) copy-start(bf16[512,256]{1,0:T(8,128)(2,1)} %cot.1) | copy-start | bytes 786436
  23.5 6.8 %copy-start.5 = (bf16[640,256]{1,0:T(8,128)(2,1)S(1)}, bf16[640,256]{1,0:T(8,128)(2,1)}, u32[]{:S(2)}) copy-start(bf16[640,256]{1,0:T(8,128)(2,1)} %self_w.3) | copy-start | bytes 983044
  26.7 4.9 %collective-permute-start.4 = (bf16[640,256]{1,0:T(8,128)(2,1)S(1)}, bf16[640,256]{1,0:T(8,128)(2,1)S(1)}, u32[]{:S(2)}, u32[]{:S(2)}) collective-permute-start(bf16[640,256]{1,0:T(8,128)(2,1)S(1)} %get-tuple-element.47), channel_id=1, source_target_pairs={{0,4},{4,0},{8,12},{12,8},{16,20},{20,16},{24,28},{28,24},{32,36},... | collective-permute-start | bytes 983048 | tf_op jit(solution)/shard_map/ppermute | solution.py:48
  30.8 22.4 %copy-start.7 = (s32[1,4,2]{1,2,0:T(2,128)S(1)}, s32[1,4,2]{1,2,0:T(2,128)}, u32[]{:S(2)}) copy-start(s32[1,4,2]{1,2,0:T(2,128)} %param.16) | copy-start | bytes 100
  32.4 22.0 %all-to-all-start = ((bf16[32,40,128]{2,1,0:T(8,128)(2,1)}), bf16[32,40,128]{2,1,0:T(8,128)(2,1)S(1)}, u32[]{:S(2)}, u32[]{:S(2)}) async-start(bf16[32,40,128]{2,1,0:T(8,128)(2,1)} %shard_map.133), calls=%async_computation | async-start | bytes 655360 | tf_op jit(solution)/shard_map/all_to_all | solution.py:64
  38.5 6.7 %collective-permute-start.5 = (bf16[256,256]{1,0:T(8,128)(2,1)S(1)}, bf16[256,256]{1,0:T(8,128)(2,1)S(1)}, u32[]{:S(2)}, u32[]{:S(2)}) collective-permute-start(bf16[256,256]{1,0:T(8,128)(2,1)S(1)} %get-tuple-element.56), channel_id=1, source_target_pairs={{0,4},{4,0},{8,12},{12,8},{16,20},{20,16},{24,28},{28,24},{32,36},... | collective-permute-start | bytes 393224 | tf_op jit(solution)/shard_map/ppermute | solution.py:48
  39.0 10.9 %collective-permute-start.6 = (bf16[256,256]{1,0:T(8,128)(2,1)S(1)}, bf16[256,256]{1,0:T(8,128)(2,1)S(1)}, u32[]{:S(2)}, u32[]{:S(2)}) collective-permute-start(bf16[256,256]{1,0:T(8,128)(2,1)S(1)} %get-tuple-element.57), channel_id=1, source_target_pairs={{0,8},{4,12},{8,0},{12,4},{16,24},{20,28},{24,16},{28,20},{32,40},... | collective-permute-start | bytes 393224 | tf_op jit(solution)/shard_map/ppermute | solution.py:48
  40.6 12.6 %collective-permute-start.7 = (bf16[256,256]{1,0:T(8,128)(2,1)S(1)}, bf16[256,256]{1,0:T(8,128)(2,1)S(1)}, u32[]{:S(2)}, u32[]{:S(2)}) collective-permute-start(bf16[256,256]{1,0:T(8,128)(2,1)S(1)} %get-tuple-element.58), channel_id=1, source_target_pairs={{8,16},{12,20},{24,32},{28,36},{40,48},{44,52},{56,64},{60,68},{72... | collective-permute-start | bytes 393224 | tf_op jit(solution)/shard_map/ppermute | solution.py:55
  45.2 8.0 %collective-permute-start.8 = (bf16[256,256]{1,0:T(8,128)(2,1)S(1)}, bf16[256,256]{1,0:T(8,128)(2,1)S(1)}, u32[]{:S(2)}, u32[]{:S(2)}) collective-permute-start(bf16[256,256]{1,0:T(8,128)(2,1)S(1)} %get-tuple-element.59), channel_id=1, source_target_pairs={{4,8},{12,16},{20,24},{28,32},{36,40},{44,48},{52,56},{60,64},{68,... | collective-permute-start | bytes 393224 | tf_op jit(solution)/shard_map/ppermute | solution.py:55
  55.2 17.8 %all-to-all-start.1 = ((bf16[32,40,128]{2,1,0:T(8,128)(2,1)}), bf16[32,40,128]{2,1,0:T(8,128)(2,1)S(1)}, u32[]{:S(2)}, u32[]{:S(2)}) async-start(bf16[32,40,128]{2,1,0:T(8,128)(2,1)} %shard_map.134), calls=%async_computation.1 | async-start | bytes 655360 | tf_op jit(solution)/shard_map/all_to_all | solution.py:64
  62.6 14.3 %collective-permute-start.10 = (bf16[160,512]{1,0:T(8,128)(2,1)S(1)}, bf16[160,512]{1,0:T(8,128)(2,1)S(1)}, u32[]{:S(2)}, u32[]{:S(2)}) collective-permute-start(bf16[160,512]{1,0:T(8,128)(2,1)S(1)} %get-tuple-element.67), channel_id=1, source_target_pairs={{0,1},{1,0},{2,3},{3,2},{4,5},{5,4},{6,7},{7,6},{8,9},{9,8},{10,11... | collective-permute-start | bytes 491528 | tf_op jit(solution)/shard_map/ppermute | solution.py:59
  63.9 13.0 %collective-permute-start.11 = (bf16[160,512]{1,0:T(8,128)(2,1)S(1)}, bf16[160,512]{1,0:T(8,128)(2,1)S(1)}, u32[]{:S(2)}, u32[]{:S(2)}) collective-permute-start(bf16[160,512]{1,0:T(8,128)(2,1)S(1)} %get-tuple-element.68), channel_id=1, source_target_pairs={{0,2},{1,3},{2,0},{3,1},{4,6},{5,7},{6,4},{7,5},{8,10},{9,11},{10,... | collective-permute-start | bytes 491528 | tf_op jit(solution)/shard_map/ppermute | solution.py:59
  66.6 10.3 %collective-permute-start.12 = (bf16[160,512]{1,0:T(8,128)(2,1)S(1)}, bf16[160,512]{1,0:T(8,128)(2,1)S(1)}, u32[]{:S(2)}, u32[]{:S(2)}) collective-permute-start(bf16[160,512]{1,0:T(8,128)(2,1)S(1)} %get-tuple-element.69), channel_id=1, source_target_pairs={{0,3},{1,2},{2,1},{3,0},{4,7},{5,6},{6,5},{7,4},{8,11},{9,10},{10,... | collective-permute-start | bytes 491528 | tf_op jit(solution)/shard_map/ppermute | solution.py:59
  73.0 5.2 %collective-permute-start.9 = (bf16[32,40,128]{2,1,0:T(8,128)(2,1)S(1)}, bf16[32,40,128]{2,1,0:T(8,128)(2,1)S(1)}, u32[]{:S(2)}, u32[]{:S(2)}) collective-permute-start(bf16[32,40,128]{2,1,0:T(8,128)(2,1)S(1)} %all-to-all-done.1.mine), channel_id=1, source_target_pairs={{0,4},{4,0},{8,12},{12,8},{16,20},{20,16},{24,28},{28,24},{32,36},... | collective-permute-start | bytes 983048 | tf_op jit(solution)/shard_map/ppermute | solution.py:48

commit v3 on v2

--- a/solution.py
+++ b/solution.py
@@ -64,6 +64,10 @@
     return lax.all_to_all(array, "dom", 0, 0, axis_index_groups=groups)
 
 
+def in_hbm(array):
+    return pltpu.with_memory_space_constraint(array, pltpu.MemorySpace.HBM)
+
+
 def rows(block, size=BS):
     return pl.ds(pl.multiple_of(block * size, size), size)
 
@@ -84,23 +88,18 @@
     return (1 - first, 5 - second, 5 - third, 1 - fourth)
 
 
-def pack_kernel(send, feats, out0, out1, out2, out3, send_now, sems):
-    copy = pltpu.make_async_copy(send, send_now, sems.at[ROUNDS * NB])
-    copy.start()
-    copy.wait()
-    copies = []
-    for i, (r, out) in enumerate(zip(sent_rounds(), (out0, out1, out2, out3))):
-        for s in range(NB):
-            copies.append(
-                pltpu.make_async_copy(
-                    feats.at[rows(send_now[0, s, r]), :],
-                    out.at[pl.ds(s * BS, BS), :],
-                    sems.at[i * NB + s],
-                )
-            )
-            copies[-1].start()
+def pack_kernel(send, feats, out0, out1, out2, out3, send_now, feats_now, sems):
+    copies = [
+        pltpu.make_async_copy(send, send_now, sems.at[0]),
+        pltpu.make_async_copy(feats, feats_now, sems.at[1]),
+    ]
+    for copy in copies:
+        copy.start()
     for copy in copies:
         copy.wait()
+    for r, out in zip(sent_rounds(), (out0, out1, out2, out3)):
+        for s in range(NB):
+            out[s * BS : (s + 1) * BS, :] = feats_now[rows(send_now[0, s, r]), :]
 
 
 def before_kernel(
@@ -116,6 +115,7 @@
     local_sum,
     degree,
     own_pre,
+    turned,
     neighbors_now,
     recv_now,
     live_now,
@@ -156,6 +156,7 @@
 
     mine = feats_now[...]
     own_pre[...] = dot(mine, self_w_now[...])
+    turned[...] = mine.T
     whole = local[...]
     local_sum[...] = dot(whole, mine)
     ones = jnp.ones((BS * BLK, BS), BF16)
@@ -174,16 +175,12 @@
     own_pre,
     neigh_w,
     cot,
-    feats,
+    turned,
     activated,
     low_out,
     spread_out,
     keep,
     give,
-    term0,
-    term1,
-    term2,
-    term3,
 ):
     core = lax.rem(lax.axis_index("dom"), CORES)
     width = NB * BS
@@ -203,9 +200,8 @@
     low_out[...] = low
     spread = (grad * jnp.concatenate([inverse] * (grad.shape[1] // BS), axis=1)).astype(BF16)
     spread_out[...] = spread
-    over_rows = ((0,), (0,))
-    of_self = dot(feats[...], low, over_rows)
-    of_neigh = dot(mean_high, low, over_rows)
+    of_self = dot(turned[...], low)
+    of_neigh = dot(mean_high, low, ((0,), (0,)))
 
     @pl.when(core == 0)
     def _():
@@ -216,9 +212,6 @@
     def _():
         keep[...] = of_neigh
         give[...] = of_self.astype(BF16)
-
-    for r, term in enumerate((term0, term1, term2, term3)):
-        term[...] = dot(edge[:, r * width : (r + 1) * width], spread, over_rows).astype(BF16)
 
 
 def piece_at(i):
@@ -257,8 +250,16 @@
         put(mine, of_neigh)
 
 
-def back_own_kernel(local, spread, low, self_w, back, part):
-    back[...] = dot(local[...], spread[...], ((0,), (0,)))
+def back_own_kernel(
+    edge, spread, act, local, low, self_w, term0, term1, term2, term3, activated, back, part
+):
+    over_rows = ((0,), (0,))
+    width = NB * BS
+    for r, term in enumerate((term0, term1, term2, term3)):
+        of_round = edge[:, r * width : (r + 1) * width]
+        term[...] = dot(of_round, spread[...], over_rows).astype(BF16)
+    activated[...] = act[...]
+    back[...] = dot(local[...], spread[...], over_rows)
     part[...] = dot(self_w[...], low[...], ((1,), (1,)))
 
 
@@ -302,12 +303,19 @@
         [((NB * BS, width), BF16)] * ROUNDS,
         [HBM] * 2,
         nbytes=2_000_000,
-        scratch=[pltpu.SMEM((1, NB, ROUNDS), jnp.int32), DMA((ROUNDS * NB + 1,))],
-    )(send_blocks, features)
+        scratch=[pltpu.SMEM((1, NB, ROUNDS), jnp.int32), pltpu.VMEM((n, width), BF16), DMA((2,))],
+    )(in_hbm(send_blocks), in_hbm(features))
     received = swaps(packed)
-    local, edge, local_sum, degree, own_pre = call(
+    local, edge, local_sum, degree, own_pre, turned = call(
         before_kernel,
-        [((n, n), BF16), ((n, slots), BF16), ((n, width), F32), ((n, BS), F32), ((n, hidden), F32)],
+        [
+            ((n, n), BF16),
+            ((n, slots), BF16),
+            ((n, width), F32),
+            ((n, BS), F32),
+            ((n, hidden), F32),
+            ((width, n), BF16),
+        ],
         [HBM] * 7,
         flops=1_000_000_000,
         nbytes=6_000_000,
@@ -322,38 +330,38 @@
             DMA((7,)),
         ],
     )(
-        neighbor_blocks,
-        recv_blocks,
-        live_slots,
-        features,
-        self_weight,
-        local_tiles,
-        boundary_tiles,
+        in_hbm(neighbor_blocks),
+        in_hbm(recv_blocks),
+        in_hbm(live_slots),
+        in_hbm(features),
+        in_hbm(self_weight),
+        in_hbm(local_tiles),
+        in_hbm(boundary_tiles),
     )
-    activated, low, spread, keep, give, *terms = call(
+    act, low, spread, keep, give = call(
         middle_kernel,
-        [((n, hidden), BF16)] * 3
-        + [((width, hidden), F32), ((width, hidden), BF16)]
-        + [((NB * BS, hidden), BF16)] * ROUNDS,
+        [((n, hidden), BF16)] * 3 + [((width, hidden), F32), ((width, hidden), BF16)],
         [VMEM] * 11,
         flops=1_600_000_000,
         nbytes=8_000_000,
         limit=32,
-    )(edge, *received, local_sum, degree, own_pre, neigh_weight, cotangent, features)
+    )(edge, *received, local_sum, degree, own_pre, neigh_weight, cotangent, turned)
 
     got = dom_swap(give, 1)
+    *terms, activated, back, in_part = call(
+        back_own_kernel,
+        [((NB * BS, hidden), BF16)] * ROUNDS
+        + [((n, hidden), BF16), ((n, hidden), F32), ((width, n), F32)],
+        [VMEM] * 6,
+        flops=600_000_000,
+        nbytes=3_000_000,
+    )(edge, spread, act, local, low, self_weight)
+    got, back, *terms = lax.optimization_barrier((got, back, *terms))
     returned = swaps(terms)
-    back, in_part = call(
-        back_own_kernel,
-        [((n, hidden), F32), ((width, n), F32)],
-        [VMEM] * 4,
-        flops=300_000_000,
-        nbytes=3_000_000,
-    )(local, spread, low, self_weight)
-    got, back, in_part = lax.optimization_barrier((got, back, in_part))
     pieces = (CHIPS,) + PIECE
     (cut,) = call(cut_kernel, [(pieces, BF16)], [VMEM] * 2, nbytes=1_500_000)(keep, got)
     (summed,) = call(sum_kernel, [(pieces, BF16)], [VMEM], nbytes=700_000)(exchange(cut))
+    summed, back, *returned = lax.optimization_barrier((summed, back, *returned))
     shape = (width // HID, n)
     in_own, *in_gives = call(
         back_kernel,
@@ -363,7 +371,6 @@
         nbytes=3_000_000,
         scratch=[pltpu.VMEM((n, hidden), F32)],
     )(send_blocks, back, in_part, *returned, neigh_weight)
-    summed, *in_gives = lax.optimization_barrier((summed, *in_gives))
     in_parts = [hid_swap(in_gives[k - 1], k) for k in range(1, HID)]
     mine = exchange(summed)
     other = dom_swap(mine, 1)

time: 79.8 us -> 75.2 us (0.942)
  local copies, waits for them, and re-layouts: 8.03 us -> 0.02 us
  waiting for transfers between devices: 15.7 us -> 17.6 us
  starting transfers between devices: 41.8 us -> 42.7 us
  Pallas kernels: 12.2 us -> 13 us
    unnamed x28 -> x8, local copies, waits for them, and re-layouts: 8.03 us -> 0.02 us
    ppermute x6, waiting for transfers between devices: 6.04 us -> 0.04 us  [dom_swap(): return lax.ppermute(array, 'dom', [(i, i ^ mask) for i in range(count)])]
    ppermute x4, waiting for transfers between devices: 3.2 us -> 7.68 us  [dom_pairs(): return lax.ppermute(array, 'dom', pairs + [(j, i) for i, j in pairs])]
    all_to_all x2, waiting for transfers between devices: 6.43 us -> 8.52 us  [exchange(): return lax.all_to_all(array, 'dom', 0, 0, axis_index_groups=groups)]
    ppermute x3, waiting for transfers between devices: 0.01 us -> 1.34 us  [hid_swap(): return lax.ppermute(array, 'hid', [(i, i ^ mask) for i in range(HID)])]
    pallas_call x1, Pallas kernels: 2.39 us -> 1.21 us  [on_device(): call(pack_kernel, [((NB * BS, width), BF16)] * ROUNDS, [HBM] * 2, nbytes=...]
    pallas_call x1, Pallas kernels: 2.25 us -> 3.27 us  [on_device(): call(before_kernel, [((n, n), BF16), ((n, slots), BF16), ((n, width), F32...]
    ppermute x6, starting transfers between devices: 12.9 us -> 13.9 us  [dom_swap(): return lax.ppermute(array, 'dom', [(i, i ^ mask) for i in range(count)])]
  transfers between devices with their start and end apart: 15 -> 15, of which waited for: 5 -> 5; matrix products, arithmetic and copies ran while one was open for 1% -> 1% of each run, Pallas kernels for 5% -> 10%
where the time goes in v3:
time: 75.2 us; the launch traced here: 74.8 us
  starting transfers between devices  42.7 us (57%)
  waiting for transfers between devices  17.6 us (23%)
  Pallas kernels  13 us (17%)
    ppermute x6, starting transfers between devices, dom_swap(): return lax.ppermute(array, 'dom', [(i, i ^ mask) for i in range(count)])  13.9 us
    all_to_all x2, starting transfers between devices, exchange(): return lax.all_to_all(array, 'dom', 0, 0, axis_index_groups=groups)  13.6 us
    ppermute x4, starting transfers between devices, dom_pairs(): return lax.ppermute(array, 'dom', pairs + [(j, i) for i, j in pairs])  11.4 us
    all_to_all x2, waiting for transfers between devices, exchange(): return lax.all_to_all(array, 'dom', 0, 0, axis_index_groups=groups)  8.52 us
    ppermute x4, waiting for transfers between devices, dom_pairs(): return lax.ppermute(array, 'dom', pairs + [(j, i) for i, j in pairs])  7.68 us
    ppermute x3, starting transfers between devices, hid_swap(): return lax.ppermute(array, 'hid', [(i, i ^ mask) for i in range(HID)])  3.91 us
    pallas_call x1, Pallas kernels, on_device(): call(before_kernel, [((n, n), BF16), ((n, slots), BF16), ((n, width), F32...  3.27 us
    pallas_call x1, Pallas kernels, on_device(): call(middle_kernel, [((n, hidden), BF16)] * 3 + [((width, hidden), F32),...  2.6 us
  transfers between devices with their start and end apart: 15, of which 5 were waited for; matrix products, arithmetic and copies ran while one was open for 1% of the time, Pallas kernels for 10%

profile of v3, /device:TPU:1, one launch (start us, length us, event | category | flops | bytes accessed | tf_op | source)
XLA Modules:
  0.0 74.8 jit_solution(7106440178178506356)
XLA Ops:
  0.6 1.2 %shard_map.130 = (bf16[256,640]{1,0:T(8,128)(2,1)S(1)}, bf16[256,640]{1,0:T(8,128)(2,1)S(1)}, bf16[256,640]{1,0:T(8,128)(2,1)S(1)}, bf16[256,640]{1,0:T(8,128)(2,1)S(1)}) custom-call(s32[1,2,4]{2,1,0:T(2,128)} %bitcast.4, bf16[512,640]{1,0:T(8,128)(2,1)} %feats.3), custom_call_target="tpu_custom_call" | custom-call | bytes 2000000 | tf_op jit(solution)/shard_map/pallas_call | solution.py:301
  1.8 3.3 %collective-permute-start = (bf16[256,640]{1,0:T(8,128)(2,1)S(1)}, bf16[256,640]{1,0:T(8,128)(2,1)S(1)}, u32[]{:S(2)}, u32[]{:S(2)}) collective-permute-start(bf16[256,640]{1,0:T(8,128)(2,1)S(1)} %get-tuple-element.45), channel_id=1, source_target_pairs={{0,4},{4,0},{8,12},{12,8},{16,20},{20,16},{24,28},{28,24},{32,36},... | collective-permute-start | bytes 983048 | tf_op jit(solution)/shard_map/ppermute | solution.py:48
  5.2 0.0 collective-permute-start.1
  5.2 6.8 %collective-permute-start.2 = (bf16[256,640]{1,0:T(8,128)(2,1)S(1)}, bf16[256,640]{1,0:T(8,128)(2,1)S(1)}, u32[]{:S(2)}, u32[]{:S(2)}) collective-permute-start(bf16[256,640]{1,0:T(8,128)(2,1)S(1)} %get-tuple-element.47), channel_id=1, source_target_pairs={{8,16},{12,20},{24,32},{28,36},{40,48},{44,52},{56,64},{60,68},{72... | collective-permute-start | bytes 983048 | tf_op jit(solution)/shard_map/ppermute | solution.py:55
  12.0 0.0 collective-permute-start.3
  12.0 3.3 %shard_map.129 = (bf16[512,512]{1,0:T(8,128)(2,1)S(1)}, bf16[512,1024]{1,0:T(8,128)(2,1)S(1)}, f32[512,640]{1,0:T(8,128)S(1)}, f32[512,128]{1,0:T(8,128)S(1)}, f...) custom-call(s32[1,4,8]{2,1,0:T(4,128)} %neighbors.1, s32[1,2,4]{2,1,0:T(2,128)} %bitcast.6, s32[1,4]{1,0:T(1,128)} %live.1, ...), custom_call_target="tpu_custom_call" | custom-call | flops 1000000000 | bytes 6000000 | tf_op jit(solution)/shard_map/pallas_call | solution.py:309
  15.2 0.0 collective-permute-done.got0
  15.3 0.0 collective-permute-done.1.got1
  15.3 4.5 %collective-permute-done.2.got2 = bf16[256,640]{1,0:T(8,128)(2,1)S(1)} collective-permute-done((bf16[256,640]{1,0:T(8,128)(2,1)S(1)}, bf16[256,640]{1,0:T(8,128)(2,1)S(1)}, u32[]{:S(2)}, u32[]{:S(2)}) %collective-permute-start.2) | collective-permute-done | bytes 327712 | tf_op jit(solution)/shard_map/ppermute | solution.py:55
  19.8 0.0 collective-permute-done.3.got3
  19.8 0.0 copy-start.1
  19.8 2.6 %shard_map.131 = (bf16[512,256]{1,0:T(8,128)(2,1)S(1)}, bf16[512,256]{1,0:T(8,128)(2,1)S(1)}, bf16[512,256]{1,0:T(8,128)(2,1)S(1)}, f32[640,256]{1,0:T(8,128)S(1)}, bf16[640,256]{1,0:T(8,128)(2,1)S(1)}) custom-call(bf16[512,1024]{1,0:T(8,128)(2,1)S(1)} %get-tuple-element.44.edge, bf16[256,640]{1,0:T(8,128)(2,1)S(1)} %collective-permute-done.got0, ...), custom_call_target="tpu_custom_call" | custom-call | flops 1600000000 | bytes 8000000 | tf_op jit(solution)/shard_map/pallas_call | solution.py:341
  22.4 4.5 %collective-permute-start.4 = (bf16[640,256]{1,0:T(8,128)(2,1)S(1)}, bf16[640,256]{1,0:T(8,128)(2,1)S(1)}, u32[]{:S(2)}, u32[]{:S(2)}) collective-permute-start(bf16[640,256]{1,0:T(8,128)(2,1)S(1)} %get-tuple-element.59), channel_id=1, source_target_pairs={{0,4},{4,0},{8,12},{12,8},{16,20},{20,16},{24,28},{28,24},{32,36},... | collective-permute-start | bytes 983048 | tf_op jit(solution)/shard_map/ppermute | solution.py:48
  26.8 1.4 %shard_map.132 = (bf16[256,256]{1,0:T(8,128)(2,1)}, bf16[256,256]{1,0:T(8,128)(2,1)S(1)}, bf16[256,256]{1,0:T(8,128)(2,1)S(1)}, bf16[256,256]{1,0:T(8,128)(2,1)S...) custom-call(bf16[512,1024]{1,0:T(8,128)(2,1)S(1)} %get-tuple-element.44.edge, ...), custom_call_target="tpu_custom_call" | custom-call | flops 600000000 | bytes 3000000 | tf_op jit(solution)/shard_map/pallas_call | solution.py:351
  28.3 0.8 %shard_map.133 = bf16[32,40,128]{2,1,0:T(8,128)(2,1)} custom-call(f32[640,256]{1,0:T(8,128)S(1)} %get-tuple-element.58.keep, bf16[640,256]{1,0:T(8,128)(2,1)S(1)} %collective-permute-done.4.got), custom_call_target="tpu_custom_call" | custom-call | bytes 1500000 | tf_op jit(solution)/shard_map/pallas_call | solution.py:362
  29.1 6.1 %all-to-all-start = ((bf16[32,40,128]{2,1,0:T(8,128)(2,1)}), bf16[32,40,128]{2,1,0:T(8,128)(2,1)S(1)}, u32[]{:S(2)}, u32[]{:S(2)}) async-start(bf16[32,40,128]{2,1,0:T(8,128)(2,1)} %shard_map.133), calls=%async_computation | async-start | bytes 655360 | tf_op jit(solution)/shard_map/all_to_all | solution.py:64
  35.2 0.7 collective-permute-start.5
  35.8 1.5 %collective-permute-start.6 = (bf16[256,256]{1,0:T(8,128)(2,1)S(1)}, bf16[256,256]{1,0:T(8,128)(2,1)S(1)}, u32[]{:S(2)}, u32[]{:S(2)}) collective-permute-start(bf16[256,256]{1,0:T(8,128)(2,1)S(1)} %get-tuple-element.68), channel_id=1, source_target_pairs={{0,8},{4,12},{8,0},{12,4},{16,24},{20,28},{24,16},{28,20},{32,40},... | collective-permute-start | bytes 393224 | tf_op jit(solution)/shard_map/ppermute | solution.py:48
  37.4 4.6 %collective-permute-start.7 = (bf16[256,256]{1,0:T(8,128)(2,1)S(1)}, bf16[256,256]{1,0:T(8,128)(2,1)S(1)}, u32[]{:S(2)}, u32[]{:S(2)}) collective-permute-start(bf16[256,256]{1,0:T(8,128)(2,1)S(1)} %get-tuple-element.69), channel_id=1, source_target_pairs={{8,16},{12,20},{24,32},{28,36},{40,48},{44,52},{56,64},{60,68},{72... | collective-permute-start | bytes 393224 | tf_op jit(solution)/shard_map/ppermute | solution.py:55
  42.0 3.8 %all-to-all-done.got = bf16[32,40,128]{2,1,0:T(8,128)(2,1)S(1)} async-done(((bf16[32,40,128]{2,1,0:T(8,128)(2,1)}), bf16[32,40,128]{2,1,0:T(8,128)(2,1)S(1)}, u32[]{:S(2)}, u32[]{:S(2)}) %all-to-all-start) | async-done | bytes 327712 | tf_op jit(solution)/shard_map/all_to_all | solution.py:64
  45.7 0.8 %shard_map.134 = bf16[32,40,128]{2,1,0:T(8,128)(2,1)} custom-call(bf16[32,40,128]{2,1,0:T(8,128)(2,1)S(1)} %all-to-all-done.got), custom_call_target="tpu_custom_call" | custom-call | bytes 700000 | tf_op jit(solution)/shard_map/pallas_call | solution.py:363
  46.5 0.0 collective-permute-done.6.got1
  46.6 3.2 %collective-permute-done.7.got2 = bf16[256,256]{1,0:T(8,128)(2,1)S(1)} collective-permute-done((bf16[256,256]{1,0:T(8,128)(2,1)S(1)}, bf16[256,256]{1,0:T(8,128)(2,1)S(1)}, u32[]{:S(2)}, u32[]{:S(2)}) %collective-permute-start.7) | collective-permute-done | bytes 131104 | tf_op jit(solution)/shard_map/ppermute | solution.py:55
  49.8 7.5 %all-to-all-start.1 = ((bf16[32,40,128]{2,1,0:T(8,128)(2,1)}), bf16[32,40,128]{2,1,0:T(8,128)(2,1)S(1)}, u32[]{:S(2)}, u32[]{:S(2)}) async-start(bf16[32,40,128]{2,1,0:T(8,128)(2,1)} %shard_map.134), calls=%async_computation.1 | async-start | bytes 655360 | tf_op jit(solution)/shard_map/all_to_all | solution.py:64
  57.3 1.8 %shard_map.136 = (f32[160,512]{1,0:T(8,128)S(1)}, bf16[160,512]{1,0:T(8,128)(2,1)}, bf16[160,512]{1,0:T(8,128)(2,1)}, bf16[160,512]{1,0:T(8,128)(2,1)S(1)}) custom-call(s32[1,2,4]{2,1,0:T(2,128)S(1)} %bitcast.5, f32[512,256]{1,0:T(8,128)S(1)} %get-tuple-element.74.start, f32[640,512]{1,0:T(8,128)S(1)} %get-tuple-element.75.part, ...), custom_call_target="tpu_custom_call" | custom-call | flops 300000000 | bytes 3000000 | tf_op jit(solution)/shard_map/pallas_call | solution.py:366
  59.1 1.3 %collective-permute-start.10 = (bf16[160,512]{1,0:T(8,128)(2,1)}, bf16[160,512]{1,0:T(8,128)(2,1)S(1)}, u32[]{:S(2)}, u32[]{:S(2)}) collective-permute-start(bf16[160,512]{1,0:T(8,128)(2,1)} %get-tuple-element.81), channel_id=1, source_target_pairs={{0,1},{1,0},{2,3},{3,2},{4,5},{5,4},{6,7},{7,6},{8,9},{9,8},{10,11... | collective-permute-start | bytes 491528 | tf_op jit(solution)/shard_map/ppermute | solution.py:59
  60.3 2.6 %collective-permute-start.11 = (bf16[160,512]{1,0:T(8,128)(2,1)}, bf16[160,512]{1,0:T(8,128)(2,1)S(1)}, u32[]{:S(2)}, u32[]{:S(2)}) collective-permute-start(bf16[160,512]{1,0:T(8,128)(2,1)} %get-tuple-element.82), channel_id=1, source_target_pairs={{0,2},{1,3},{2,0},{3,1},{4,6},{5,7},{6,4},{7,5},{8,10},{9,11},{10,... | collective-permute-start | bytes 491528 | tf_op jit(solution)/shard_map/ppermute | solution.py:59
  63.0 4.7 %all-to-all-done.1.mine = bf16[32,40,128]{2,1,0:T(8,128)(2,1)S(1)} async-done(((bf16[32,40,128]{2,1,0:T(8,128)(2,1)}), bf16[32,40,128]{2,1,0:T(8,128)(2,1)S(1)}, u32[]{:S(2)}, u32[]{:S(2)}) %all-to-all-start.1) | async-done | bytes 327712 | tf_op jit(solution)/shard_map/all_to_all | solution.py:64
  67.7 3.9 %collective-permute-start.9 = (bf16[32,40,128]{2,1,0:T(8,128)(2,1)S(1)}, bf16[32,40,128]{2,1,0:T(8,128)(2,1)S(1)}, u32[]{:S(2)}, u32[]{:S(2)}) collective-permute-start(bf16[32,40,128]{2,1,0:T(8,128)(2,1)S(1)} %all-to-all-done.1.mine), channel_id=1, source_target_pairs={{0,4},{4,0},{8,12},{12,8},{16,20},{20,16},{24,28},{28,24},{32,36},... | collective-permute-start | bytes 983048 | tf_op jit(solution)/shard_map/ppermute | solution.py:48
  71.6 1.3 %collective-permute-done.12 = bf16[160,512]{1,0:T(8,128)(2,1)S(1)} collective-permute-done((bf16[160,512]{1,0:T(8,128)(2,1)S(1)}, bf16[160,512]{1,0:T(8,128)(2,1)S(1)}, u32[]{:S(2)}, u32[]{:S(2)}) %collective-permute-start.12) | collective-permute-done | bytes 163872 | tf_op jit(solution)/shard_map/ppermute | solution.py:59
  72.9 0.7 fusion
  73.7 1.2 %shard_map.135 = (f32[640,256]{1,0:T(8,128)}, f32[640,256]{1,0:T(8,128)}) custom-call(bf16[32,40,128]{2,1,0:T(8,128)(2,1)S(1)} %all-to-all-done.1.mine, bf16[32,40,128]{2,1,0:T(8,128)(2,1)S(1)} %collective-permute-done.9.other), custom_call_target="tpu_custom_call" | custom-call | bytes 2000000 | tf_op jit(solution)/shard_map/pallas_call | solution.py:378
  (15 shorter events, 0.0 us)
Async XLA Ops:
  1.8 13.4 %collective-permute-start = (bf16[256,640]{1,0:T(8,128)(2,1)S(1)}, bf16[256,640]{1,0:T(8,128)(2,1)S(1)}, u32[]{:S(2)}, u32[]{:S(2)}) collective-permute-start(bf16[256,640]{1,0:T(8,128)(2,1)S(1)} %get-tuple-element.45), channel_id=1, source_target_pairs={{0,4},{4,0},{8,12},{12,8},{16,20},{20,16},{24,28},{28,24},{32,36},... | collective-permute-start | bytes 983048 | tf_op jit(solution)/shard_map/ppermute | solution.py:48
  5.2 10.1 %collective-permute-start.1 = (bf16[256,640]{1,0:T(8,128)(2,1)S(1)}, bf16[256,640]{1,0:T(8,128)(2,1)S(1)}, u32[]{:S(2)}, u32[]{:S(2)}) collective-permute-start(bf16[256,640]{1,0:T(8,128)(2,1)S(1)} %get-tuple-element.46), channel_id=1, source_target_pairs={{0,8},{4,12},{8,0},{12,4},{16,24},{20,28},{24,16},{28,20},{32,40},... | collective-permute-start | bytes 983048 | tf_op jit(solution)/shard_map/ppermute | solution.py:48
  5.2 14.6 %collective-permute-start.2 = (bf16[256,640]{1,0:T(8,128)(2,1)S(1)}, bf16[256,640]{1,0:T(8,128)(2,1)S(1)}, u32[]{:S(2)}, u32[]{:S(2)}) collective-permute-start(bf16[256,640]{1,0:T(8,128)(2,1)S(1)} %get-tuple-element.47), channel_id=1, source_target_pairs={{8,16},{12,20},{24,32},{28,36},{40,48},{44,52},{56,64},{60,68},{72... | collective-permute-start | bytes 983048 | tf_op jit(solution)/shard_map/ppermute | solution.py:55
  12.0 7.8 %collective-permute-start.3 = (bf16[256,640]{1,0:T(8,128)(2,1)S(1)}, bf16[256,640]{1,0:T(8,128)(2,1)S(1)}, u32[]{:S(2)}, u32[]{:S(2)}) collective-permute-start(bf16[256,640]{1,0:T(8,128)(2,1)S(1)} %get-tuple-element.48), channel_id=1, source_target_pairs={{4,8},{12,16},{20,24},{28,32},{36,40},{44,48},{52,56},{60,64},{68,... | collective-permute-start | bytes 983048 | tf_op jit(solution)/shard_map/ppermute | solution.py:55
  12.0 7.8 %copy-start = (bf16[640,256]{1,0:T(8,128)(2,1)S(1)}, bf16[640,256]{1,0:T(8,128)(2,1)}, u32[]{:S(2)}) copy-start(bf16[640,256]{1,0:T(8,128)(2,1)} %neigh_w.3) | copy-start | bytes 983044
  12.0 7.8 %copy-start.3 = (bf16[512,256]{1,0:T(8,128)(2,1)S(1)}, bf16[512,256]{1,0:T(8,128)(2,1)}, u32[]{:S(2)}) copy-start(bf16[512,256]{1,0:T(8,128)(2,1)} %cot.1) | copy-start | bytes 786436
  19.8 7.1 %copy-start.1 = (bf16[640,256]{1,0:T(8,128)(2,1)S(1)}, bf16[640,256]{1,0:T(8,128)(2,1)}, u32[]{:S(2)}) copy-start(bf16[640,256]{1,0:T(8,128)(2,1)} %self_w.3) | copy-start | bytes 983044
  22.4 5.9 %collective-permute-start.4 = (bf16[640,256]{1,0:T(8,128)(2,1)S(1)}, bf16[640,256]{1,0:T(8,128)(2,1)S(1)}, u32[]{:S(2)}, u32[]{:S(2)}) collective-permute-start(bf16[640,256]{1,0:T(8,128)(2,1)S(1)} %get-tuple-element.59), channel_id=1, source_target_pairs={{0,4},{4,0},{8,12},{12,8},{16,20},{20,16},{24,28},{28,24},{32,36},... | collective-permute-start | bytes 983048 | tf_op jit(solution)/shard_map/ppermute | solution.py:48
  29.1 28.2 %copy-start.2 = (s32[1,4,2]{1,2,0:T(2,128)S(1)}, s32[1,4,2]{1,2,0:T(2,128)}, u32[]{:S(2)}) copy-start(s32[1,4,2]{1,2,0:T(2,128)} %param.16) | copy-start | bytes 100
  29.1 16.7 %all-to-all-start = ((bf16[32,40,128]{2,1,0:T(8,128)(2,1)}), bf16[32,40,128]{2,1,0:T(8,128)(2,1)S(1)}, u32[]{:S(2)}, u32[]{:S(2)}) async-start(bf16[32,40,128]{2,1,0:T(8,128)(2,1)} %shard_map.133), calls=%async_computation | async-start | bytes 655360 | tf_op jit(solution)/shard_map/all_to_all | solution.py:64
  35.2 11.4 %collective-permute-start.5 = (bf16[256,256]{1,0:T(8,128)(2,1)}, bf16[256,256]{1,0:T(8,128)(2,1)S(1)}, u32[]{:S(2)}, u32[]{:S(2)}) collective-permute-start(bf16[256,256]{1,0:T(8,128)(2,1)} %get-tuple-element.67), channel_id=1, source_target_pairs={{0,4},{4,0},{8,12},{12,8},{16,20},{20,16},{24,28},{28,24},{32,36},... | collective-permute-start | bytes 393224 | tf_op jit(solution)/shard_map/ppermute | solution.py:48
  35.8 10.7 %collective-permute-start.6 = (bf16[256,256]{1,0:T(8,128)(2,1)S(1)}, bf16[256,256]{1,0:T(8,128)(2,1)S(1)}, u32[]{:S(2)}, u32[]{:S(2)}) collective-permute-start(bf16[256,256]{1,0:T(8,128)(2,1)S(1)} %get-tuple-element.68), channel_id=1, source_target_pairs={{0,8},{4,12},{8,0},{12,4},{16,24},{20,28},{24,16},{28,20},{32,40},... | collective-permute-start | bytes 393224 | tf_op jit(solution)/shard_map/ppermute | solution.py:48
  37.4 12.4 %collective-permute-start.7 = (bf16[256,256]{1,0:T(8,128)(2,1)S(1)}, bf16[256,256]{1,0:T(8,128)(2,1)S(1)}, u32[]{:S(2)}, u32[]{:S(2)}) collective-permute-start(bf16[256,256]{1,0:T(8,128)(2,1)S(1)} %get-tuple-element.69), channel_id=1, source_target_pairs={{8,16},{12,20},{24,32},{28,36},{40,48},{44,52},{56,64},{60,68},{72... | collective-permute-start | bytes 393224 | tf_op jit(solution)/shard_map/ppermute | solution.py:55
  42.0 7.8 %collective-permute-start.8 = (bf16[256,256]{1,0:T(8,128)(2,1)S(1)}, bf16[256,256]{1,0:T(8,128)(2,1)S(1)}, u32[]{:S(2)}, u32[]{:S(2)}) collective-permute-start(bf16[256,256]{1,0:T(8,128)(2,1)S(1)} %get-tuple-element.70), channel_id=1, source_target_pairs={{4,8},{12,16},{20,24},{28,32},{36,40},{44,48},{52,56},{60,64},{68,... | collective-permute-start | bytes 393224 | tf_op jit(solution)/shard_map/ppermute | solution.py:55
  49.8 17.9 %all-to-all-start.1 = ((bf16[32,40,128]{2,1,0:T(8,128)(2,1)}), bf16[32,40,128]{2,1,0:T(8,128)(2,1)S(1)}, u32[]{:S(2)}, u32[]{:S(2)}) async-start(bf16[32,40,128]{2,1,0:T(8,128)(2,1)} %shard_map.134), calls=%async_computation.1 | async-start | bytes 655360 | tf_op jit(solution)/shard_map/all_to_all | solution.py:64
  59.1 12.5 %collective-permute-start.10 = (bf16[160,512]{1,0:T(8,128)(2,1)}, bf16[160,512]{1,0:T(8,128)(2,1)S(1)}, u32[]{:S(2)}, u32[]{:S(2)}) collective-permute-start(bf16[160,512]{1,0:T(8,128)(2,1)} %get-tuple-element.81), channel_id=1, source_target_pairs={{0,1},{1,0},{2,3},{3,2},{4,5},{5,4},{6,7},{7,6},{8,9},{9,8},{10,11... | collective-permute-start | bytes 491528 | tf_op jit(solution)/shard_map/ppermute | solution.py:59
  60.3 11.3 %collective-permute-start.11 = (bf16[160,512]{1,0:T(8,128)(2,1)}, bf16[160,512]{1,0:T(8,128)(2,1)S(1)}, u32[]{:S(2)}, u32[]{:S(2)}) collective-permute-start(bf16[160,512]{1,0:T(8,128)(2,1)} %get-tuple-element.82), channel_id=1, source_target_pairs={{0,2},{1,3},{2,0},{3,1},{4,6},{5,7},{6,4},{7,5},{8,10},{9,11},{10,... | collective-permute-start | bytes 491528 | tf_op jit(solution)/shard_map/ppermute | solution.py:59
  63.0 10.0 %collective-permute-start.12 = (bf16[160,512]{1,0:T(8,128)(2,1)S(1)}, bf16[160,512]{1,0:T(8,128)(2,1)S(1)}, u32[]{:S(2)}, u32[]{:S(2)}) collective-permute-start(bf16[160,512]{1,0:T(8,128)(2,1)S(1)} %get-tuple-element.83), channel_id=1, source_target_pairs={{0,3},{1,2},{2,1},{3,0},{4,7},{5,6},{6,5},{7,4},{8,11},{9,10},{10,... | collective-permute-start | bytes 491528 | tf_op jit(solution)/shard_map/ppermute | solution.py:59
  67.7 6.0 %collective-permute-start.9 = (bf16[32,40,128]{2,1,0:T(8,128)(2,1)S(1)}, bf16[32,40,128]{2,1,0:T(8,128)(2,1)S(1)}, u32[]{:S(2)}, u32[]{:S(2)}) collective-permute-start(bf16[32,40,128]{2,1,0:T(8,128)(2,1)S(1)} %all-to-all-done.1.mine), channel_id=1, source_target_pairs={{0,4},{4,0},{8,12},{12,8},{16,20},{20,16},{24,28},{28,24},{32,36},... | collective-permute-start | bytes 983048 | tf_op jit(solution)/shard_map/ppermute | solution.py:48

commit v4 on v3

--- a/solution.py
+++ b/solution.py
@@ -19,6 +19,7 @@
 HID = 4
 CHIPS = X * Z
 PIECE = (40, 128)
+COVER_FLOPS = 60_000_000_000
 BF16 = jnp.bfloat16
 F32 = jnp.float32
 
@@ -31,7 +32,7 @@
     return lax.dot_general(a, b, (dims, ((), ())), preferred_element_type=F32)
 
 
-def call(kernel, outs, specs, flops=0, nbytes=0, limit=24, scratch=()):
+def call(kernel, outs, specs, flops=0, nbytes=0, limit=12, scratch=()):
     return pl.pallas_call(
         kernel,
         out_shape=[jax.ShapeDtypeStruct(shape, dtype) for shape, dtype in outs],
@@ -74,18 +75,18 @@
 
 def swaps(arrays):
     a, b, c, d = arrays
-    return [dom_swap(a, 1), dom_swap(b, 2), dom_pairs(c, 2), dom_pairs(d, 1)]
+    return [dom_pairs(a, 2), dom_pairs(b, 1), dom_swap(c, 2), dom_swap(d, 1)]
 
 
 def sent_rounds():
     me = lax.axis_index("dom")
     core, chip = lax.rem(me, CORES), lax.rem(me // CORES, 2)
-    return (core, 2 + chip, 3 - chip, 1 - core)
+    return (3 - chip, 1 - core, 2 + chip, core)
 
 
 def received_rounds():
     first, second, third, fourth = sent_rounds()
-    return (1 - first, 5 - second, 5 - third, 1 - fourth)
+    return (5 - first, 1 - second, 5 - third, 1 - fourth)
 
 
 def pack_kernel(send, feats, out0, out1, out2, out3, send_now, feats_now, sems):
@@ -251,8 +252,28 @@
 
 
 def back_own_kernel(
-    edge, spread, act, local, low, self_w, term0, term1, term2, term3, activated, back, part
+    send,
+    edge,
+    spread,
+    act,
+    local,
+    low,
+    self_w,
+    neigh_w,
+    term0,
+    term1,
+    term2,
+    term3,
+    activated,
+    back,
+    part,
+    neigh_w_out,
+    place,
+    send_now,
+    sem,
 ):
+    copy = pltpu.make_async_copy(send, send_now, sem.at[0])
+    copy.start()
     over_rows = ((0,), (0,))
     width = NB * BS
     for r, term in enumerate((term0, term1, term2, term3)):
@@ -261,24 +282,47 @@
     activated[...] = act[...]
     back[...] = dot(local[...], spread[...], over_rows)
     part[...] = dot(self_w[...], low[...], ((1,), (1,)))
-
-
-def back_kernel(send, start, part, got0, got1, got2, got3, neigh_w, own, give1, give2, give3, back):
-    back[...] = start[...]
-    for r, got in zip(sent_rounds(), (got0, got1, got2, got3)):
+    neigh_w_out[...] = neigh_w[...]
+    copy.wait()
+    for i, r in enumerate(sent_rounds()):
         for s in range(NB):
-            at = rows(send[0, s, r])
-            back[at, :] = back[at, :] + got[s * BS : (s + 1) * BS, :].astype(F32)
-    back_low = back[...].astype(BF16)
-    y = lax.axis_index("hid")
-    size = own.shape[0]
-    for k in range(HID):
-        at = rows(jnp.bitwise_xor(y, k), size)
-        total = part[at, :] + dot(neigh_w[at, :], back_low, ((1,), (1,)))
-        if k == 0:
-            own[...] = total
-        else:
-            (give1, give2, give3)[k - 1][...] = total.astype(BF16)
+            for b in range(BLK):
+                at = (i * NB + s) * BLK + b
+                hit = jnp.where(send_now[0, s, r] == b, 1.0, 0.0)
+                place[at : at + 1, :] = jnp.full((1, BS), hit, F32)
+
+
+def hid_part(k, size, part, neigh_w, back):
+    at = rows(jnp.bitwise_xor(lax.axis_index("hid"), k), size)
+    return part[at, :] + dot(neigh_w[at, :], back, ((1,), (1,)))
+
+
+def back_kernel(
+    place, start, part, got0, got1, got2, got3, neigh_w, own, far, give1, give3, got_now, sems
+):
+    size, hidden = own.shape[0], start.shape[1]
+    copies = [
+        pltpu.make_async_copy(got, got_now.at[i], sems.at[i])
+        for i, got in enumerate((got0, got1, got2, got3))
+    ]
+    for copy in copies:
+        copy.start()
+    for copy in copies:
+        copy.wait()
+    blocks = []
+    for b in range(BLK):
+        total = start[b * BS : (b + 1) * BS, :]
+        for i in range(ROUNDS):
+            for s in range(NB):
+                at = (i * NB + s) * BLK + b
+                hit = jnp.concatenate([place[at : at + 1, :]] * (hidden // BS), axis=1)
+                total = total + hit * got_now[i, s * BS : (s + 1) * BS, :].astype(F32)
+        blocks.append(total.astype(BF16))
+    back = jnp.concatenate(blocks, axis=0)
+    far[...] = hid_part(2, size, part, neigh_w, back).astype(BF16)
+    give1[...] = hid_part(1, size, part, neigh_w, back).astype(BF16)
+    give3[...] = hid_part(3, size, part, neigh_w, back).astype(BF16)
+    own[...] = hid_part(0, size, part, neigh_w, back)
 
 
 def on_device(
@@ -344,34 +388,36 @@
         [VMEM] * 11,
         flops=1_600_000_000,
         nbytes=8_000_000,
-        limit=32,
+        limit=16,
     )(edge, *received, local_sum, degree, own_pre, neigh_weight, cotangent, turned)
 
     got = dom_swap(give, 1)
-    *terms, activated, back, in_part = call(
+    *terms, activated, back, in_part, neigh_now, place = call(
         back_own_kernel,
         [((NB * BS, hidden), BF16)] * ROUNDS
-        + [((n, hidden), BF16), ((n, hidden), F32), ((width, n), F32)],
-        [VMEM] * 6,
+        + [((n, hidden), BF16), ((n, hidden), F32), ((width, n), F32), ((width, hidden), BF16)]
+        + [((ROUNDS * NB * BLK, BS), F32)],
+        [HBM] + [VMEM] * 7,
         flops=600_000_000,
         nbytes=3_000_000,
-    )(edge, spread, act, local, low, self_weight)
+        scratch=[pltpu.SMEM((1, NB, ROUNDS), jnp.int32), DMA((1,))],
+    )(in_hbm(send_blocks), edge, spread, act, local, low, self_weight, neigh_weight)
     got, back, *terms = lax.optimization_barrier((got, back, *terms))
     returned = swaps(terms)
     pieces = (CHIPS,) + PIECE
     (cut,) = call(cut_kernel, [(pieces, BF16)], [VMEM] * 2, nbytes=1_500_000)(keep, got)
     (summed,) = call(sum_kernel, [(pieces, BF16)], [VMEM], nbytes=700_000)(exchange(cut))
-    summed, back, *returned = lax.optimization_barrier((summed, back, *returned))
+    summed, back = lax.optimization_barrier((summed, back))
     shape = (width // HID, n)
-    in_own, *in_gives = call(
+    in_own, in_far, in_first, in_third = call(
         back_kernel,
-        [(shape, F32)] + [(shape, BF16)] * (HID - 1),
-        [pl.BlockSpec(memory_space=pltpu.SMEM)] + [VMEM] * 7,
-        flops=300_000_000,
+        [(shape, F32)] + [(shape, BF16)] * 3,
+        [VMEM] * 3 + [HBM] * 4 + [VMEM],
+        flops=COVER_FLOPS,
         nbytes=3_000_000,
-        scratch=[pltpu.VMEM((n, hidden), F32)],
-    )(send_blocks, back, in_part, *returned, neigh_weight)
-    in_parts = [hid_swap(in_gives[k - 1], k) for k in range(1, HID)]
+        scratch=[pltpu.VMEM((ROUNDS, NB * BS, hidden), BF16), DMA((ROUNDS,))],
+    )(place, back, in_part, *[in_hbm(a) for a in returned], neigh_now)
+    in_parts = [hid_swap(in_far, 2), hid_swap(in_first, 1), hid_swap(in_third, 3)]
     mine = exchange(summed)
     other = dom_swap(mine, 1)
     scale = 1.0 / math.sqrt(n * lax.axis_size("dom"))
@@ -381,7 +427,7 @@
         [VMEM] * 2,
         nbytes=2_000_000,
     )(mine, other)
-    grad_input = in_own
+    grad_self, grad_input = lax.optimization_barrier((grad_self, in_own))
     for part in in_parts:
         grad_input = grad_input + part.astype(F32)
     return activated, grad_self, grad_neigh, grad_input.astype(BF16).T

time: 75.2 us -> 81.7 us (1.086)
  blocking collectives: 0 us -> 14.8 us
  starting transfers between devices: 42.7 us -> 37.3 us
  waiting for transfers between devices: 17.6 us -> 14.5 us
    all_to_all x0 -> x1, blocking collectives: none -> 14.8 us  [exchange(): return lax.all_to_all(array, 'dom', 0, 0, axis_index_groups=groups)]
    all_to_all x2 -> x1, starting transfers between devices: 13.6 us -> 7.49 us  [exchange(): return lax.all_to_all(array, 'dom', 0, 0, axis_index_groups=groups)]
    all_to_all x2 -> x1, waiting for transfers between devices: 8.52 us -> 3.18 us  [exchange(): return lax.all_to_all(array, 'dom', 0, 0, axis_index_groups=groups)]
    ppermute x3, waiting for transfers between devices: 1.34 us -> 5.67 us  [hid_swap(): return lax.ppermute(array, 'hid', [(i, i ^ mask) for i in range(HID)])]
    ppermute x4, waiting for transfers between devices: 7.68 us -> 4.33 us  [dom_pairs(): return lax.ppermute(array, 'dom', pairs + [(j, i) for i, j in pairs])]
    ppermute x4, starting transfers between devices: 11.4 us -> 13.4 us  [dom_pairs(): return lax.ppermute(array, 'dom', pairs + [(j, i) for i, j in pairs])]
    ppermute x6, waiting for transfers between devices: 0.04 us -> 1.29 us  [dom_swap(): return lax.ppermute(array, 'dom', [(i, i ^ mask) for i in range(count)])]
    ppermute x6, starting transfers between devices: 13.9 us -> 12.7 us  [dom_swap(): return lax.ppermute(array, 'dom', [(i, i ^ mask) for i in range(count)])]
  transfers between devices with their start and end apart: 15 -> 14, of which waited for: 5 -> 7; matrix products, arithmetic and copies ran while one was open for 1% -> 0% of each run, Pallas kernels for 10% -> 10%
where the time goes in v4:
time: 81.7 us; the launch traced here: 81.4 us
  starting transfers between devices  37.3 us (46%)
  blocking collectives  14.8 us (18%)
  waiting for transfers between devices  14.5 us (18%)
  Pallas kernels  12.6 us (15%)
    all_to_all x1, blocking collectives, exchange(): return lax.all_to_all(array, 'dom', 0, 0, axis_index_groups=groups)  14.8 us
    ppermute x4, starting transfers between devices, dom_pairs(): return lax.ppermute(array, 'dom', pairs + [(j, i) for i, j in pairs])  13.4 us
    ppermute x6, starting transfers between devices, dom_swap(): return lax.ppermute(array, 'dom', [(i, i ^ mask) for i in range(count)])  12.7 us
    all_to_all x1, starting transfers between devices, exchange(): return lax.all_to_all(array, 'dom', 0, 0, axis_index_groups=groups)  7.49 us
    ppermute x3, waiting for transfers between devices, hid_swap(): return lax.ppermute(array, 'hid', [(i, i ^ mask) for i in range(HID)])  5.67 us
    ppermute x4, waiting for transfers between devices, dom_pairs(): return lax.ppermute(array, 'dom', pairs + [(j, i) for i, j in pairs])  4.33 us
    ppermute x3, starting transfers between devices, hid_swap(): return lax.ppermute(array, 'hid', [(i, i ^ mask) for i in range(HID)])  3.78 us
    pallas_call x1, Pallas kernels, on_device(): call(before_kernel, [((n, n), BF16), ((n, slots), BF16), ((n, width), F32...  3.28 us
  transfers between devices with their start and end apart: 14, of which 7 were waited for; matrix products, arithmetic and copies ran while one was open for 0% of the time, Pallas kernels for 10%

profile of v4, /device:TPU:1, one launch (start us, length us, event | category | flops | bytes accessed | tf_op | source)
XLA Modules:
  0.0 81.4 jit_solution(8718457817517036787)
XLA Ops:
  0.6 1.2 %shard_map.130 = (bf16[256,640]{1,0:T(8,128)(2,1)S(1)}, bf16[256,640]{1,0:T(8,128)(2,1)S(1)}, bf16[256,640]{1,0:T(8,128)(2,1)S(1)}, bf16[256,640]{1,0:T(8,128)(2,1)S(1)}) custom-call(s32[1,2,4]{2,1,0:T(2,128)} %bitcast.4, bf16[512,640]{1,0:T(8,128)(2,1)} %feats.3), custom_call_target="tpu_custom_call" | custom-call | bytes 2000000 | tf_op jit(solution)/shard_map/pallas_call | solution.py:345
  1.8 8.7 %collective-permute-start = (bf16[256,640]{1,0:T(8,128)(2,1)S(1)}, bf16[256,640]{1,0:T(8,128)(2,1)S(1)}, u32[]{:S(2)}, u32[]{:S(2)}) collective-permute-start(bf16[256,640]{1,0:T(8,128)(2,1)S(1)} %get-tuple-element.45), channel_id=1, source_target_pairs={{8,16},{12,20},{24,32},{28,36},{40,48},{44,52},{56,64},{60,68},{72... | collective-permute-start | bytes 983048 | tf_op jit(solution)/shard_map/ppermute | solution.py:56
  10.5 2.1 %collective-permute-start.3 = (bf16[256,640]{1,0:T(8,128)(2,1)S(1)}, bf16[256,640]{1,0:T(8,128)(2,1)S(1)}, u32[]{:S(2)}, u32[]{:S(2)}) collective-permute-start(bf16[256,640]{1,0:T(8,128)(2,1)S(1)} %get-tuple-element.48), channel_id=1, source_target_pairs={{0,4},{4,0},{8,12},{12,8},{16,20},{20,16},{24,28},{28,24},{32,36},... | collective-permute-start | bytes 983048 | tf_op jit(solution)/shard_map/ppermute | solution.py:49
  12.7 3.3 %shard_map.129 = (bf16[512,512]{1,0:T(8,128)(2,1)S(1)}, bf16[512,1024]{1,0:T(8,128)(2,1)S(1)}, f32[512,640]{1,0:T(8,128)S(1)}, f32[512,128]{1,0:T(8,128)S(1)}, f...) custom-call(s32[1,4,8]{2,1,0:T(4,128)} %neighbors.1, s32[1,2,4]{2,1,0:T(2,128)} %bitcast.6, s32[1,4]{1,0:T(1,128)} %live.1, ...), custom_call_target="tpu_custom_call" | custom-call | flops 1000000000 | bytes 6000000 | tf_op jit(solution)/shard_map/pallas_call | solution.py:353
  16.0 2.0 %collective-permute-done.got0 = bf16[256,640]{1,0:T(8,128)(2,1)S(1)} collective-permute-done((bf16[256,640]{1,0:T(8,128)(2,1)S(1)}, bf16[256,640]{1,0:T(8,128)(2,1)S(1)}, u32[]{:S(2)}, u32[]{:S(2)}) %collective-permute-start) | collective-permute-done | bytes 327712 | tf_op jit(solution)/shard_map/ppermute | solution.py:56
  18.0 2.3 %collective-permute-done.1.got1 = bf16[256,640]{1,0:T(8,128)(2,1)S(1)} collective-permute-done((bf16[256,640]{1,0:T(8,128)(2,1)S(1)}, bf16[256,640]{1,0:T(8,128)(2,1)S(1)}, u32[]{:S(2)}, u32[]{:S(2)}) %collective-permute-start.1) | collective-permute-done | bytes 327712 | tf_op jit(solution)/shard_map/ppermute | solution.py:56
  20.3 1.3 %collective-permute-done.2.got2 = bf16[256,640]{1,0:T(8,128)(2,1)S(1)} collective-permute-done((bf16[256,640]{1,0:T(8,128)(2,1)S(1)}, bf16[256,640]{1,0:T(8,128)(2,1)S(1)}, u32[]{:S(2)}, u32[]{:S(2)}) %collective-permute-start.2) | collective-permute-done | bytes 327712 | tf_op jit(solution)/shard_map/ppermute | solution.py:49
  21.6 2.6 %shard_map.131 = (bf16[512,256]{1,0:T(8,128)(2,1)S(1)}, bf16[512,256]{1,0:T(8,128)(2,1)S(1)}, bf16[512,256]{1,0:T(8,128)(2,1)S(1)}, f32[640,256]{1,0:T(8,128)S(1)}, bf16[640,256]{1,0:T(8,128)(2,1)S(1)}) custom-call(bf16[512,1024]{1,0:T(8,128)(2,1)S(1)} %get-tuple-element.44.edge, bf16[256,640]{1,0:T(8,128)(2,1)S(1)} %collective-permute-done.got0, ...), custom_call_target="tpu_custom_call" | custom-call | flops 1600000000 | bytes 8000000 | tf_op jit(solution)/shard_map/pallas_call | solution.py:385
  24.2 2.7 %collective-permute-start.4 = (bf16[640,256]{1,0:T(8,128)(2,1)S(1)}, bf16[640,256]{1,0:T(8,128)(2,1)S(1)}, u32[]{:S(2)}, u32[]{:S(2)}) collective-permute-start(bf16[640,256]{1,0:T(8,128)(2,1)S(1)} %get-tuple-element.59), channel_id=1, source_target_pairs={{0,4},{4,0},{8,12},{12,8},{16,20},{20,16},{24,28},{28,24},{32,36},... | collective-permute-start | bytes 983048 | tf_op jit(solution)/shard_map/ppermute | solution.py:49
  26.9 1.6 %shard_map.132 = (bf16[256,256]{1,0:T(8,128)(2,1)S(1)}, bf16[256,256]{1,0:T(8,128)(2,1)S(1)}, bf16[256,256]{1,0:T(8,128)(2,1)S(1)}, bf16[256,256]{1,0:T(8,128)(2...) custom-call(s32[1,2,4]{2,1,0:T(2,128)} %bitcast.5, ...), custom_call_target="tpu_custom_call" | custom-call | flops 600000000 | bytes 3000000 | tf_op jit(solution)/shard_map/pallas_call | solution.py:395
  28.5 0.1 shard_map.133
  28.6 14.8 %all_to_all.10.got = bf16[32,40,128]{2,1,0:T(8,128)(2,1)S(1)} all-to-all(bf16[32,40,128]{2,1,0:T(8,128)(2,1)S(1)} %shard_map.133), channel_id=1, replica_groups={{0,8,16,24,32,40,48,56,64,72,80,88,96,104,112,120,128,136,144,152,160,1..., dimensions={0} | all-to-all | bytes 655360 | tf_op jit(solution)/shard_map/all_to_all | solution.py:65
  43.4 0.8 shard_map.134
  44.2 7.5 %all-to-all-start.1 = ((bf16[32,40,128]{2,1,0:T(8,128)(2,1)}), bf16[32,40,128]{2,1,0:T(8,128)(2,1)S(1)}, u32[]{:S(2)}, u32[]{:S(2)}) async-start(bf16[32,40,128]{2,1,0:T(8,128)(2,1)} %shard_map.134), calls=%async_computation.1 | async-start | bytes 655360 | tf_op jit(solution)/shard_map/all_to_all | solution.py:65
  51.7 4.7 %collective-permute-start.6 = (bf16[256,256]{1,0:T(8,128)(2,1)S(1)}, bf16[256,256]{1,0:T(8,128)(2,1)S(1)}, u32[]{:S(2)}, u32[]{:S(2)}) collective-permute-start(bf16[256,256]{1,0:T(8,128)(2,1)S(1)} %get-tuple-element.72), channel_id=1, source_target_pairs={{8,16},{12,20},{24,32},{28,36},{40,48},{44,52},{56,64},{60,68},{72... | collective-permute-start | bytes 393224 | tf_op jit(solution)/shard_map/ppermute | solution.py:56
  56.4 2.1 %collective-permute-start.9 = (bf16[256,256]{1,0:T(8,128)(2,1)S(1)}, bf16[256,256]{1,0:T(8,128)(2,1)S(1)}, u32[]{:S(2)}, u32[]{:S(2)}) collective-permute-start(bf16[256,256]{1,0:T(8,128)(2,1)S(1)} %get-tuple-element.75), channel_id=1, source_target_pairs={{0,4},{4,0},{8,12},{12,8},{16,20},{20,16},{24,28},{28,24},{32,36},... | collective-permute-start | bytes 393224 | tf_op jit(solution)/shard_map/ppermute | solution.py:49
  58.6 3.2 %all-to-all-done.1.mine = bf16[32,40,128]{2,1,0:T(8,128)(2,1)S(1)} async-done(((bf16[32,40,128]{2,1,0:T(8,128)(2,1)}), bf16[32,40,128]{2,1,0:T(8,128)(2,1)S(1)}, u32[]{:S(2)}, u32[]{:S(2)}) %all-to-all-start.1) | async-done | bytes 327712 | tf_op jit(solution)/shard_map/all_to_all | solution.py:65
  61.7 5.6 %collective-permute-start.5 = (bf16[32,40,128]{2,1,0:T(8,128)(2,1)S(1)}, bf16[32,40,128]{2,1,0:T(8,128)(2,1)S(1)}, u32[]{:S(2)}, u32[]{:S(2)}) collective-permute-start(bf16[32,40,128]{2,1,0:T(8,128)(2,1)S(1)} %all-to-all-done.1.mine), channel_id=1, source_target_pairs={{0,4},{4,0},{8,12},{12,8},{16,20},{20,16},{24,28},{28,24},{32,36},... | collective-permute-start | bytes 983048 | tf_op jit(solution)/shard_map/ppermute | solution.py:49
  67.4 0.0 copy-start.4
  67.5 0.6 copy-done.3
  68.0 0.0 copy-done.4
  68.1 0.0 copy-done.5
  68.1 0.0 copy-done.6
  68.2 1.9 %shard_map.136 = (f32[160,512]{1,0:T(8,128)S(1)}, bf16[160,512]{1,0:T(8,128)(2,1)S(1)}, bf16[160,512]{1,0:T(8,128)(2,1)S(1)}, bf16[160,512]{1,0:T(8,128)(2,1)S(1)}) custom-call(f32[32,128]{1,0:T(8,128)S(1)} %get-tuple-element.69.place, f32[512,256]{1,0:T(8,128)S(1)} %get-tuple-element.70.start, f32[640,512]{1,0:T(8,128)S(1)} %get-tuple-element.71.part, ...), custom_call_target="tpu_custom_call" | custom-call | flops 60000002048 | bytes 3000000 | tf_op jit(solution)/shard_map/pallas_call | solution.py:412
  70.1 3.0 %collective-permute-start.10 = (bf16[160,512]{1,0:T(8,128)(2,1)S(1)}, bf16[160,512]{1,0:T(8,128)(2,1)S(1)}, u32[]{:S(2)}, u32[]{:S(2)}) collective-permute-start(bf16[160,512]{1,0:T(8,128)(2,1)S(1)} %get-tuple-element.81), channel_id=1, source_target_pairs={{0,2},{1,3},{2,0},{3,1},{4,6},{5,7},{6,4},{7,5},{8,10},{9,11},{10,... | collective-permute-start | bytes 491528 | tf_op jit(solution)/shard_map/ppermute | solution.py:60
  73.1 0.4 collective-permute-start.11
  73.4 0.4 collective-permute-start.12
  73.8 1.2 %shard_map.135 = (f32[640,256]{1,0:T(8,128)}, f32[640,256]{1,0:T(8,128)}) custom-call(bf16[32,40,128]{2,1,0:T(8,128)(2,1)S(1)} %all-to-all-done.1.mine, bf16[32,40,128]{2,1,0:T(8,128)(2,1)S(1)} %collective-permute-done.5.other), custom_call_target="tpu_custom_call" | custom-call | bytes 2000000 | tf_op jit(solution)/shard_map/pallas_call | solution.py:424
  75.0 0.8 %collective-permute-done.10 = bf16[160,512]{1,0:T(8,128)(2,1)S(1)} collective-permute-done((bf16[160,512]{1,0:T(8,128)(2,1)S(1)}, bf16[160,512]{1,0:T(8,128)(2,1)S(1)}, u32[]{:S(2)}, u32[]{:S(2)}) %collective-permute-start.10) | collective-permute-done | bytes 163872 | tf_op jit(solution)/shard_map/ppermute | solution.py:60
  75.8 3.5 %collective-permute-done.11 = bf16[160,512]{1,0:T(8,128)(2,1)S(1)} collective-permute-done((bf16[160,512]{1,0:T(8,128)(2,1)S(1)}, bf16[160,512]{1,0:T(8,128)(2,1)S(1)}, u32[]{:S(2)}, u32[]{:S(2)}) %collective-permute-start.11) | collective-permute-done | bytes 163872 | tf_op jit(solution)/shard_map/ppermute | solution.py:60
  79.3 1.3 %collective-permute-done.12 = bf16[160,512]{1,0:T(8,128)(2,1)S(1)} collective-permute-done((bf16[160,512]{1,0:T(8,128)(2,1)S(1)}, bf16[160,512]{1,0:T(8,128)(2,1)S(1)}, u32[]{:S(2)}, u32[]{:S(2)}) %collective-permute-start.12) | collective-permute-done | bytes 163872 | tf_op jit(solution)/shard_map/ppermute | solution.py:60
  80.7 0.8 fusion
  (20 shorter events, 0.0 us)
Async XLA Ops:
  1.8 16.1 %collective-permute-start = (bf16[256,640]{1,0:T(8,128)(2,1)S(1)}, bf16[256,640]{1,0:T(8,128)(2,1)S(1)}, u32[]{:S(2)}, u32[]{:S(2)}) collective-permute-start(bf16[256,640]{1,0:T(8,128)(2,1)S(1)} %get-tuple-element.45), channel_id=1, source_target_pairs={{8,16},{12,20},{24,32},{28,36},{40,48},{44,52},{56,64},{60,68},{72... | collective-permute-start | bytes 983048 | tf_op jit(solution)/shard_map/ppermute | solution.py:56
  10.5 9.8 %collective-permute-start.1 = (bf16[256,640]{1,0:T(8,128)(2,1)S(1)}, bf16[256,640]{1,0:T(8,128)(2,1)S(1)}, u32[]{:S(2)}, u32[]{:S(2)}) collective-permute-start(bf16[256,640]{1,0:T(8,128)(2,1)S(1)} %get-tuple-element.46), channel_id=1, source_target_pairs={{4,8},{12,16},{20,24},{28,32},{36,40},{44,48},{52,56},{60,64},{68,... | collective-permute-start | bytes 983048 | tf_op jit(solution)/shard_map/ppermute | solution.py:56
  10.5 11.0 %collective-permute-start.2 = (bf16[256,640]{1,0:T(8,128)(2,1)S(1)}, bf16[256,640]{1,0:T(8,128)(2,1)S(1)}, u32[]{:S(2)}, u32[]{:S(2)}) collective-permute-start(bf16[256,640]{1,0:T(8,128)(2,1)S(1)} %get-tuple-element.47), channel_id=1, source_target_pairs={{0,8},{4,12},{8,0},{12,4},{16,24},{20,28},{24,16},{28,20},{32,40},... | collective-permute-start | bytes 983048 | tf_op jit(solution)/shard_map/ppermute | solution.py:49
  10.5 11.0 %collective-permute-start.3 = (bf16[256,640]{1,0:T(8,128)(2,1)S(1)}, bf16[256,640]{1,0:T(8,128)(2,1)S(1)}, u32[]{:S(2)}, u32[]{:S(2)}) collective-permute-start(bf16[256,640]{1,0:T(8,128)(2,1)S(1)} %get-tuple-element.48), channel_id=1, source_target_pairs={{0,4},{4,0},{8,12},{12,8},{16,20},{20,16},{24,28},{28,24},{32,36},... | collective-permute-start | bytes 983048 | tf_op jit(solution)/shard_map/ppermute | solution.py:49
  12.7 8.9 %copy-start.1 = (bf16[640,256]{1,0:T(8,128)(2,1)S(1)}, bf16[640,256]{1,0:T(8,128)(2,1)}, u32[]{:S(2)}) copy-start(bf16[640,256]{1,0:T(8,128)(2,1)} %neigh_w.3) | copy-start | bytes 983044
  12.7 8.9 %copy-start.2 = (bf16[512,256]{1,0:T(8,128)(2,1)S(1)}, bf16[512,256]{1,0:T(8,128)(2,1)}, u32[]{:S(2)}) copy-start(bf16[512,256]{1,0:T(8,128)(2,1)} %cot.1) | copy-start | bytes 786436
  21.6 5.3 %copy-start = (bf16[640,256]{1,0:T(8,128)(2,1)S(1)}, bf16[640,256]{1,0:T(8,128)(2,1)}, u32[]{:S(2)}) copy-start(bf16[640,256]{1,0:T(8,128)(2,1)} %self_w.3) | copy-start | bytes 983044
  24.2 4.3 %collective-permute-start.4 = (bf16[640,256]{1,0:T(8,128)(2,1)S(1)}, bf16[640,256]{1,0:T(8,128)(2,1)S(1)}, u32[]{:S(2)}, u32[]{:S(2)}) collective-permute-start(bf16[640,256]{1,0:T(8,128)(2,1)S(1)} %get-tuple-element.59), channel_id=1, source_target_pairs={{0,4},{4,0},{8,12},{12,8},{16,20},{20,16},{24,28},{28,24},{32,36},... | collective-permute-start | bytes 983048 | tf_op jit(solution)/shard_map/ppermute | solution.py:49
  44.2 17.5 %all-to-all-start.1 = ((bf16[32,40,128]{2,1,0:T(8,128)(2,1)}), bf16[32,40,128]{2,1,0:T(8,128)(2,1)S(1)}, u32[]{:S(2)}, u32[]{:S(2)}) async-start(bf16[32,40,128]{2,1,0:T(8,128)(2,1)} %shard_map.134), calls=%async_computation.1 | async-start | bytes 655360 | tf_op jit(solution)/shard_map/all_to_all | solution.py:65
  51.7 15.7 %collective-permute-start.6 = (bf16[256,256]{1,0:T(8,128)(2,1)S(1)}, bf16[256,256]{1,0:T(8,128)(2,1)S(1)}, u32[]{:S(2)}, u32[]{:S(2)}) collective-permute-start(bf16[256,256]{1,0:T(8,128)(2,1)S(1)} %get-tuple-element.72), channel_id=1, source_target_pairs={{8,16},{12,20},{24,32},{28,36},{40,48},{44,52},{56,64},{60,68},{72... | collective-permute-start | bytes 393224 | tf_op jit(solution)/shard_map/ppermute | solution.py:56
  56.4 11.0 %collective-permute-start.7 = (bf16[256,256]{1,0:T(8,128)(2,1)S(1)}, bf16[256,256]{1,0:T(8,128)(2,1)S(1)}, u32[]{:S(2)}, u32[]{:S(2)}) collective-permute-start(bf16[256,256]{1,0:T(8,128)(2,1)S(1)} %get-tuple-element.73), channel_id=1, source_target_pairs={{4,8},{12,16},{20,24},{28,32},{36,40},{44,48},{52,56},{60,64},{68,... | collective-permute-start | bytes 393224 | tf_op jit(solution)/shard_map/ppermute | solution.py:56
  56.4 11.0 %collective-permute-start.8 = (bf16[256,256]{1,0:T(8,128)(2,1)S(1)}, bf16[256,256]{1,0:T(8,128)(2,1)S(1)}, u32[]{:S(2)}, u32[]{:S(2)}) collective-permute-start(bf16[256,256]{1,0:T(8,128)(2,1)S(1)} %get-tuple-element.74), channel_id=1, source_target_pairs={{0,8},{4,12},{8,0},{12,4},{16,24},{20,28},{24,16},{28,20},{32,40},... | collective-permute-start | bytes 393224 | tf_op jit(solution)/shard_map/ppermute | solution.py:49
  56.4 11.0 %collective-permute-start.9 = (bf16[256,256]{1,0:T(8,128)(2,1)S(1)}, bf16[256,256]{1,0:T(8,128)(2,1)S(1)}, u32[]{:S(2)}, u32[]{:S(2)}) collective-permute-start(bf16[256,256]{1,0:T(8,128)(2,1)S(1)} %get-tuple-element.75), channel_id=1, source_target_pairs={{0,4},{4,0},{8,12},{12,8},{16,20},{20,16},{24,28},{28,24},{32,36},... | collective-permute-start | bytes 393224 | tf_op jit(solution)/shard_map/ppermute | solution.py:49
  61.7 12.1 %collective-permute-start.5 = (bf16[32,40,128]{2,1,0:T(8,128)(2,1)S(1)}, bf16[32,40,128]{2,1,0:T(8,128)(2,1)S(1)}, u32[]{:S(2)}, u32[]{:S(2)}) collective-permute-start(bf16[32,40,128]{2,1,0:T(8,128)(2,1)S(1)} %all-to-all-done.1.mine), channel_id=1, source_target_pairs={{0,4},{4,0},{8,12},{12,8},{16,20},{20,16},{24,28},{28,24},{32,36},... | collective-permute-start | bytes 983048 | tf_op jit(solution)/shard_map/ppermute | solution.py:49
  67.4 0.7 copy-start.3
  67.4 0.7 copy-start.4
  67.4 0.7 copy-start.5
  67.4 0.7 copy-start.6
  70.1 5.8 %collective-permute-start.10 = (bf16[160,512]{1,0:T(8,128)(2,1)S(1)}, bf16[160,512]{1,0:T(8,128)(2,1)S(1)}, u32[]{:S(2)}, u32[]{:S(2)}) collective-permute-start(bf16[160,512]{1,0:T(8,128)(2,1)S(1)} %get-tuple-element.81), channel_id=1, source_target_pairs={{0,2},{1,3},{2,0},{3,1},{4,6},{5,7},{6,4},{7,5},{8,10},{9,11},{10,... | collective-permute-start | bytes 491528 | tf_op jit(solution)/shard_map/ppermute | solution.py:60
  73.1 6.3 %collective-permute-start.11 = (bf16[160,512]{1,0:T(8,128)(2,1)S(1)}, bf16[160,512]{1,0:T(8,128)(2,1)S(1)}, u32[]{:S(2)}, u32[]{:S(2)}) collective-permute-start(bf16[160,512]{1,0:T(8,128)(2,1)S(1)} %get-tuple-element.82), channel_id=1, source_target_pairs={{0,1},{1,0},{2,3},{3,2},{4,5},{5,4},{6,7},{7,6},{8,9},{9,8},{10,11... | collective-permute-start | bytes 491528 | tf_op jit(solution)/shard_map/ppermute | solution.py:60
  73.4 7.2 %collective-permute-start.12 = (bf16[160,512]{1,0:T(8,128)(2,1)S(1)}, bf16[160,512]{1,0:T(8,128)(2,1)S(1)}, u32[]{:S(2)}, u32[]{:S(2)}) collective-permute-start(bf16[160,512]{1,0:T(8,128)(2,1)S(1)} %get-tuple-element.83), channel_id=1, source_target_pairs={{0,3},{1,2},{2,1},{3,0},{4,7},{5,6},{6,5},{7,4},{8,11},{9,10},{10,... | collective-permute-start | bytes 491528 | tf_op jit(solution)/shard_map/ppermute | solution.py:60

commit v5 on v4

--- a/solution.py
+++ b/solution.py
@@ -75,13 +75,13 @@
 
 def swaps(arrays):
     a, b, c, d = arrays
-    return [dom_pairs(a, 2), dom_pairs(b, 1), dom_swap(c, 2), dom_swap(d, 1)]
+    return [dom_swap(a, 2), dom_pairs(b, 1), dom_pairs(c, 2), dom_swap(d, 1)]
 
 
 def sent_rounds():
     me = lax.axis_index("dom")
     core, chip = lax.rem(me, CORES), lax.rem(me // CORES, 2)
-    return (3 - chip, 1 - core, 2 + chip, core)
+    return (2 + chip, 1 - core, 3 - chip, core)
 
 
 def received_rounds():
@@ -98,7 +98,13 @@
         copy.start()
     for copy in copies:
         copy.wait()
+    y, size = lax.axis_index("hid"), out1.shape[0]
+    per_slot = HID // NB
     for r, out in zip(sent_rounds(), (out0, out1, out2, out3)):
+        if out is out1:
+            at = send_now[0, y // per_slot, r] * BS + lax.rem(y, per_slot) * size
+            out[...] = feats_now[pl.ds(pl.multiple_of(at, size), size), :]
+            continue
         for s in range(NB):
             out[s * BS : (s + 1) * BS, :] = feats_now[rows(send_now[0, s, r]), :]
 
@@ -127,20 +133,25 @@
     sems,
 ):
     pairs = (
+        (feats, feats_now),
+        (self_w, self_w_now),
         (neighbors, neighbors_now),
         (recv, recv_now),
         (live, live_now),
         (tiles, tiles_now),
         (edge_tiles, edge_tiles_now),
-        (feats, feats_now),
-        (self_w, self_w_now),
     )
     copies = [pltpu.make_async_copy(a, b, sems.at[i]) for i, (a, b) in enumerate(pairs)]
     for copy in copies:
         copy.start()
     local[...] = jnp.zeros_like(local)
     edge[...] = jnp.zeros_like(edge)
-    for copy in copies:
+    for copy in copies[:2]:
+        copy.wait()
+    mine = feats_now[...]
+    own_pre[...] = dot(mine, self_w_now[...])
+    turned[...] = mine.T
+    for copy in copies[2:]:
         copy.wait()
     for b in range(BLK):
         for k in range(K_IN):
@@ -155,9 +166,6 @@
             def _():
                 edge[rows(recv_now[0, s, r]), slot * BS : (slot + 1) * BS] = edge_tiles_now[0, r, s]
 
-    mine = feats_now[...]
-    own_pre[...] = dot(mine, self_w_now[...])
-    turned[...] = mine.T
     whole = local[...]
     local_sum[...] = dot(whole, mine)
     ones = jnp.ones((BS * BLK, BS), BF16)
@@ -168,9 +176,12 @@
 def middle_kernel(
     edge,
     got0,
-    got1,
     got2,
     got3,
+    share0,
+    share1,
+    share2,
+    share3,
     local_sum,
     degree,
     own_pre,
@@ -180,9 +191,13 @@
     activated,
     low_out,
     spread_out,
-    keep,
+    mean_out,
     give,
+    got1,
 ):
+    size = share0.shape[0]
+    for k, share in zip((0, 2, 1, 3), (share0, share1, share2, share3)):
+        got1[rows(jnp.bitwise_xor(lax.axis_index("hid"), k), size), :] = share[...]
     core = lax.rem(lax.axis_index("dom"), CORES)
     width = NB * BS
     total = local_sum[...]
@@ -201,18 +216,27 @@
     low_out[...] = low
     spread = (grad * jnp.concatenate([inverse] * (grad.shape[1] // BS), axis=1)).astype(BF16)
     spread_out[...] = spread
-    of_self = dot(turned[...], low)
-    of_neigh = dot(mean_high, low, ((0,), (0,)))
+    mean_out[...] = mean_high
 
     @pl.when(core == 0)
     def _():
-        keep[...] = of_self
-        give[...] = of_neigh.astype(BF16)
+        give[...] = dot(mean_high, low, ((0,), (0,))).astype(BF16)
 
     @pl.when(core == 1)
     def _():
-        keep[...] = of_neigh
-        give[...] = of_self.astype(BF16)
+        give[...] = dot(turned[...], low).astype(BF16)
+
+
+def keep_kernel(turned, mean, low, keep):
+    core = lax.rem(lax.axis_index("dom"), CORES)
+
+    @pl.when(core == 0)
+    def _():
+        keep[...] = dot(turned[...], low[...])
+
+    @pl.when(core == 1)
+    def _():
+        keep[...] = dot(mean[...], low[...], ((0,), (0,)))
 
 
 def piece_at(i):
@@ -257,7 +281,6 @@
     spread,
     act,
     local,
-    low,
     self_w,
     neigh_w,
     term0,
@@ -266,7 +289,7 @@
     term3,
     activated,
     back,
-    part,
+    self_w_out,
     neigh_w_out,
     place,
     send_now,
@@ -281,7 +304,7 @@
         term[...] = dot(of_round, spread[...], over_rows).astype(BF16)
     activated[...] = act[...]
     back[...] = dot(local[...], spread[...], over_rows)
-    part[...] = dot(self_w[...], low[...], ((1,), (1,)))
+    self_w_out[...] = self_w[...]
     neigh_w_out[...] = neigh_w[...]
     copy.wait()
     for i, r in enumerate(sent_rounds()):
@@ -292,37 +315,32 @@
                 place[at : at + 1, :] = jnp.full((1, BS), hit, F32)
 
 
-def hid_part(k, size, part, neigh_w, back):
+def hid_part(k, size, self_w, neigh_w, low, back):
     at = rows(jnp.bitwise_xor(lax.axis_index("hid"), k), size)
-    return part[at, :] + dot(neigh_w[at, :], back, ((1,), (1,)))
+    over_hidden = ((1,), (1,))
+    return dot(self_w[at, :], low, over_hidden) + dot(neigh_w[at, :], back, over_hidden)
 
 
 def back_kernel(
-    place, start, part, got0, got1, got2, got3, neigh_w, own, far, give1, give3, got_now, sems
+    place, start, low, self_w, neigh_w, got0, got1, got2, got3, own, far, give1, give3
 ):
     size, hidden = own.shape[0], start.shape[1]
-    copies = [
-        pltpu.make_async_copy(got, got_now.at[i], sems.at[i])
-        for i, got in enumerate((got0, got1, got2, got3))
-    ]
-    for copy in copies:
-        copy.start()
-    for copy in copies:
-        copy.wait()
     blocks = []
     for b in range(BLK):
         total = start[b * BS : (b + 1) * BS, :]
-        for i in range(ROUNDS):
+        for i, got in enumerate((got0, got1, got2, got3)):
             for s in range(NB):
                 at = (i * NB + s) * BLK + b
                 hit = jnp.concatenate([place[at : at + 1, :]] * (hidden // BS), axis=1)
-                total = total + hit * got_now[i, s * BS : (s + 1) * BS, :].astype(F32)
+                total = total + hit * got[s * BS : (s + 1) * BS, :].astype(F32)
         blocks.append(total.astype(BF16))
     back = jnp.concatenate(blocks, axis=0)
-    far[...] = hid_part(2, size, part, neigh_w, back).astype(BF16)
-    give1[...] = hid_part(1, size, part, neigh_w, back).astype(BF16)
-    give3[...] = hid_part(3, size, part, neigh_w, back).astype(BF16)
-    own[...] = hid_part(0, size, part, neigh_w, back)
+    part = functools.partial(hid_part, size=size, self_w=self_w, neigh_w=neigh_w)
+    low_now = low[...]
+    far[...] = part(2, low=low_now, back=back).astype(BF16)
+    give1[...] = part(1, low=low_now, back=back).astype(BF16)
+    give3[...] = part(3, low=low_now, back=back).astype(BF16)
+    own[...] = part(0, low=low_now, back=back)
 
 
 def on_device(
@@ -344,12 +362,14 @@
     recv_blocks = jnp.swapaxes(recv_blocks, 1, 2)
     packed = call(
         pack_kernel,
-        [((NB * BS, width), BF16)] * ROUNDS,
+        [((NB * BS // HID if r == 1 else NB * BS, width), BF16) for r in range(ROUNDS)],
         [HBM] * 2,
         nbytes=2_000_000,
         scratch=[pltpu.SMEM((1, NB, ROUNDS), jnp.int32), pltpu.VMEM((n, width), BF16), DMA((2,))],
     )(in_hbm(send_blocks), in_hbm(features))
-    received = swaps(packed)
+    got_c, share, got_d, got_a = swaps(packed)
+    share, got_a = lax.optimization_barrier((share, got_a))
+    shares = [share] + [hid_swap(share, k) for k in (2, 1, 3)]
     local, edge, local_sum, degree, own_pre, turned = call(
         before_kernel,
         [
@@ -361,7 +381,7 @@
             ((width, n), BF16),
         ],
         [HBM] * 7,
-        flops=1_000_000_000,
+        flops=COVER_FLOPS,
         nbytes=6_000_000,
         scratch=[
             pltpu.SMEM((1, BLK, K_IN), jnp.int32),
@@ -382,41 +402,46 @@
         in_hbm(local_tiles),
         in_hbm(boundary_tiles),
     )
-    act, low, spread, keep, give = call(
+    act, low, spread, mean, give = call(
         middle_kernel,
-        [((n, hidden), BF16)] * 3 + [((width, hidden), F32), ((width, hidden), BF16)],
-        [VMEM] * 11,
+        [((n, hidden), BF16)] * 3 + [((n, width), BF16), ((width, hidden), BF16)],
+        [VMEM] * 14,
         flops=1_600_000_000,
         nbytes=8_000_000,
+        scratch=[pltpu.VMEM((NB * BS, width), BF16)],
         limit=16,
-    )(edge, *received, local_sum, degree, own_pre, neigh_weight, cotangent, turned)
+    )(edge, got_c, got_d, got_a, *shares, local_sum, degree, own_pre, neigh_weight, cotangent, turned)
 
     got = dom_swap(give, 1)
-    *terms, activated, back, in_part, neigh_now, place = call(
+    (keep,) = call(
+        keep_kernel, [((width, hidden), F32)], [VMEM] * 3, flops=200_000_000, nbytes=2_000_000
+    )(turned, mean, low)
+    got, keep = lax.optimization_barrier((got, keep))
+    pieces = (CHIPS,) + PIECE
+    (cut,) = call(cut_kernel, [(pieces, BF16)], [VMEM] * 2, nbytes=1_500_000)(keep, got)
+    cut, spread, low = lax.optimization_barrier((cut, spread, low))
+    *terms, activated, back, self_now, neigh_now, place = call(
         back_own_kernel,
         [((NB * BS, hidden), BF16)] * ROUNDS
-        + [((n, hidden), BF16), ((n, hidden), F32), ((width, n), F32), ((width, hidden), BF16)]
+        + [((n, hidden), BF16), ((n, hidden), F32)]
+        + [((width, hidden), BF16)] * 2
         + [((ROUNDS * NB * BLK, BS), F32)],
-        [HBM] + [VMEM] * 7,
+        [HBM] + [VMEM] * 6,
         flops=600_000_000,
         nbytes=3_000_000,
         scratch=[pltpu.SMEM((1, NB, ROUNDS), jnp.int32), DMA((1,))],
-    )(in_hbm(send_blocks), edge, spread, act, local, low, self_weight, neigh_weight)
-    got, back, *terms = lax.optimization_barrier((got, back, *terms))
+    )(in_hbm(send_blocks), edge, spread, act, local, self_weight, neigh_weight)
     returned = swaps(terms)
-    pieces = (CHIPS,) + PIECE
-    (cut,) = call(cut_kernel, [(pieces, BF16)], [VMEM] * 2, nbytes=1_500_000)(keep, got)
     (summed,) = call(sum_kernel, [(pieces, BF16)], [VMEM], nbytes=700_000)(exchange(cut))
     summed, back = lax.optimization_barrier((summed, back))
     shape = (width // HID, n)
     in_own, in_far, in_first, in_third = call(
         back_kernel,
         [(shape, F32)] + [(shape, BF16)] * 3,
-        [VMEM] * 3 + [HBM] * 4 + [VMEM],
+        [VMEM] * 9,
         flops=COVER_FLOPS,
         nbytes=3_000_000,
-        scratch=[pltpu.VMEM((ROUNDS, NB * BS, hidden), BF16), DMA((ROUNDS,))],
-    )(place, back, in_part, *[in_hbm(a) for a in returned], neigh_now)
+    )(place, back, low, self_now, neigh_now, *returned)
     in_parts = [hid_swap(in_far, 2), hid_swap(in_first, 1), hid_swap(in_third, 3)]
     mine = exchange(summed)
     other = dom_swap(mine, 1)
@@ -427,7 +452,7 @@
         [VMEM] * 2,
         nbytes=2_000_000,
     )(mine, other)
-    grad_self, grad_input = lax.optimization_barrier((grad_self, in_own))
+    grad_input = in_own
     for part in in_parts:
         grad_input = grad_input + part.astype(F32)
     return activated, grad_self, grad_neigh, grad_input.astype(BF16).T

time: 81.7 us -> 69.3 us (0.85)
  blocking collectives: 14.8 us -> 0 us
  starting transfers between devices: 37.3 us -> 44.9 us
  waiting for transfers between devices: 14.5 us -> 7.19 us
  local copies, waits for them, and re-layouts: 0.74 us -> 2.26 us
    all_to_all x1 -> x0, blocking collectives: 14.8 us -> none  [exchange(): return lax.all_to_all(array, 'dom', 0, 0, axis_index_groups=groups)]
    all_to_all x1 -> x2, starting transfers between devices: 7.49 us -> 12.6 us  [exchange(): return lax.all_to_all(array, 'dom', 0, 0, axis_index_groups=groups)]
    ppermute x3 -> x6, waiting for transfers between devices: 5.67 us -> 1.15 us  [hid_swap(): return lax.ppermute(array, 'hid', [(i, i ^ mask) for i in range(HID)])]
    ppermute x4, waiting for transfers between devices: 4.33 us -> 0.01 us  [dom_pairs(): return lax.ppermute(array, 'dom', pairs + [(j, i) for i, j in pairs])]
    ppermute x3 -> x6, starting transfers between devices: 3.78 us -> 8.1 us  [hid_swap(): return lax.ppermute(array, 'hid', [(i, i ^ mask) for i in range(HID)])]
    ppermute x4, starting transfers between devices: 13.4 us -> 11.9 us  [dom_pairs(): return lax.ppermute(array, 'dom', pairs + [(j, i) for i, j in pairs])]
    unnamed x14 -> x18, local copies, waits for them, and re-layouts: 0.74 us -> 2.26 us
    all_to_all x1 -> x2, waiting for transfers between devices: 3.18 us -> 4.67 us  [exchange(): return lax.all_to_all(array, 'dom', 0, 0, axis_index_groups=groups)]
  transfers between devices with their start and end apart: 14 -> 18, of which waited for: 7 -> 4; matrix products, arithmetic and copies ran while one was open for 0% -> 1% of each run, Pallas kernels for 10% -> 11%
where the time goes in v5:
time: 69.3 us; the launch traced here: 68.9 us
  starting transfers between devices  44.9 us (65%)
  Pallas kernels  13 us (19%)
  waiting for transfers between devices  7.19 us (10%)
  local copies, waits for them, and re-layouts  2.26 us (3%)
  between operations  0.82 us (1%)
  other arithmetic  0.75 us (1%)
    all_to_all x2, starting transfers between devices, exchange(): return lax.all_to_all(array, 'dom', 0, 0, axis_index_groups=groups)  12.6 us
    ppermute x6, starting transfers between devices, dom_swap(): return lax.ppermute(array, 'dom', [(i, i ^ mask) for i in range(count)])  12.4 us
    ppermute x4, starting transfers between devices, dom_pairs(): return lax.ppermute(array, 'dom', pairs + [(j, i) for i, j in pairs])  11.9 us
    ppermute x6, starting transfers between devices, hid_swap(): return lax.ppermute(array, 'hid', [(i, i ^ mask) for i in range(HID)])  8.1 us
    all_to_all x2, waiting for transfers between devices, exchange(): return lax.all_to_all(array, 'dom', 0, 0, axis_index_groups=groups)  4.67 us
    pallas_call x1, Pallas kernels, on_device(): call(before_kernel, [((n, n), BF16), ((n, slots), BF16), ((n, width), F32...  3.46 us
    pallas_call x1, Pallas kernels, on_device(): call(middle_kernel, [((n, hidden), BF16)] * 3 + [((n, width), BF16), ((wi...  2.48 us
    unnamed x18, local copies, waits for them, and re-layouts  2.26 us
  transfers between devices with their start and end apart: 18, of which 4 were waited for; matrix products, arithmetic and copies ran while one was open for 1% of the time, Pallas kernels for 11%

profile of v5, /device:TPU:1, one launch (start us, length us, event | category | flops | bytes accessed | tf_op | source)
XLA Modules:
  0.0 68.9 jit_solution(16891994377931758586)
XLA Ops:
  0.6 1.2 %shard_map.130 = (bf16[256,640]{1,0:T(8,128)(2,1)S(1)}, bf16[64,640]{1,0:T(8,128)(2,1)S(1)}, bf16[256,640]{1,0:T(8,128)(2,1)S(1)}, bf16[256,640]{1,0:T(8,128)(2,1)S(1)}) custom-call(s32[1,2,4]{2,1,0:T(2,128)} %bitcast.4, bf16[512,640]{1,0:T(8,128)(2,1)} %feats.3), custom_call_target="tpu_custom_call" | custom-call | bytes 2000000 | tf_op jit(solution)/shard_map/pallas_call | solution.py:363
  1.8 3.3 %collective-permute-start.3 = (bf16[256,640]{1,0:T(8,128)(2,1)S(1)}, bf16[256,640]{1,0:T(8,128)(2,1)S(1)}, u32[]{:S(2)}, u32[]{:S(2)}) collective-permute-start(bf16[256,640]{1,0:T(8,128)(2,1)S(1)} %get-tuple-element.47), channel_id=1, source_target_pairs={{0,4},{4,0},{8,12},{12,8},{16,20},{20,16},{24,28},{28,24},{32,36},... | collective-permute-start | bytes 983048 | tf_op jit(solution)/shard_map/ppermute | solution.py:49
  5.2 1.5 %collective-permute-start = (bf16[256,640]{1,0:T(8,128)(2,1)S(1)}, bf16[256,640]{1,0:T(8,128)(2,1)S(1)}, u32[]{:S(2)}, u32[]{:S(2)}) collective-permute-start(bf16[256,640]{1,0:T(8,128)(2,1)S(1)} %get-tuple-element.44), channel_id=1, source_target_pairs={{0,8},{4,12},{8,0},{12,4},{16,24},{20,28},{24,16},{28,20},{32,40},... | collective-permute-start | bytes 983048 | tf_op jit(solution)/shard_map/ppermute | solution.py:49
  6.7 6.0 %collective-permute-start.1 = (bf16[256,640]{1,0:T(8,128)(2,1)S(1)}, bf16[256,640]{1,0:T(8,128)(2,1)S(1)}, u32[]{:S(2)}, u32[]{:S(2)}) collective-permute-start(bf16[256,640]{1,0:T(8,128)(2,1)S(1)} %get-tuple-element.45), channel_id=1, source_target_pairs={{8,16},{12,20},{24,32},{28,36},{40,48},{44,52},{56,64},{60,68},{72... | collective-permute-start | bytes 983048 | tf_op jit(solution)/shard_map/ppermute | solution.py:56
  12.7 2.7 %collective-permute-start.6 = (bf16[64,640]{1,0:T(8,128)(2,1)S(1)}, bf16[64,640]{1,0:T(8,128)(2,1)S(1)}, u32[]{:S(2)}, u32[]{:S(2)}) collective-permute-start(bf16[64,640]{1,0:T(8,128)(2,1)S(1)} %collective-permute-done.2.share0), channel_id=1, source_target_pairs={{0,3},{1,2},{2,1},{3,0},{4,7},{5,6},{6,5},{7,4},{8,11},{9,10},{10,... | collective-permute-start | bytes 245768 | tf_op jit(solution)/shard_map/ppermute | solution.py:60
  15.4 1.3 %collective-permute-start.4 = (bf16[64,640]{1,0:T(8,128)(2,1)S(1)}, bf16[64,640]{1,0:T(8,128)(2,1)S(1)}, u32[]{:S(2)}, u32[]{:S(2)}) collective-permute-start(bf16[64,640]{1,0:T(8,128)(2,1)S(1)} %collective-permute-done.2.share0), channel_id=1, source_target_pairs={{0,2},{1,3},{2,0},{3,1},{4,6},{5,7},{6,4},{7,5},{8,10},{9,11},{10,... | collective-permute-start | bytes 245768 | tf_op jit(solution)/shard_map/ppermute | solution.py:60
  16.7 3.5 %shard_map.129 = (bf16[512,512]{1,0:T(8,128)(2,1)S(1)}, bf16[512,1024]{1,0:T(8,128)(2,1)S(1)}, f32[512,640]{1,0:T(8,128)S(1)}, f32[512,128]{1,0:T(8,128)S(1)}, f...) custom-call(s32[1,4,8]{2,1,0:T(4,128)} %neighbors.1, s32[1,2,4]{2,1,0:T(2,128)} %bitcast.6, s32[1,4]{1,0:T(1,128)} %live.1, ...), custom_call_target="tpu_custom_call" | custom-call | flops 60000002048 | bytes 6000000 | tf_op jit(solution)/shard_map/pallas_call | solution.py:373
  20.2 1.1 %collective-permute-done.4.share1 = bf16[64,640]{1,0:T(8,128)(2,1)S(1)} collective-permute-done((bf16[64,640]{1,0:T(8,128)(2,1)S(1)}, bf16[64,640]{1,0:T(8,128)(2,1)S(1)}, u32[]{:S(2)}, u32[]{:S(2)}) %collective-permute-start.4) | collective-permute-done | bytes 81952 | tf_op jit(solution)/shard_map/ppermute | solution.py:60
  21.3 2.5 %shard_map.131 = (bf16[512,256]{1,0:T(8,128)(2,1)S(1)}, bf16[512,256]{1,0:T(8,128)(2,1)S(1)}, bf16[512,256]{1,0:T(8,128)(2,1)S(1)}, bf16[512,640]{1,0:T(8,128)(2,1)S(1)}, bf16[640,256]{1,0:T(8,128)(2,1)S(1)}) custom-call(bf16[512,1024]{1,0:T(8,128)(2,1)S(1)} %get-tuple-element.43.edge, bf16[256,640]{1,0:T(8,128)(2,1)S(1)} %collective-permute-done.got0, ...), custom_call_target="tpu_custom_call" | custom-call | flops 1600000000 | bytes 8000000 | tf_op jit(solution)/shard_map/pallas_call | solution.py:405
  23.8 1.6 %collective-permute-start.7 = (bf16[640,256]{1,0:T(8,128)(2,1)S(1)}, bf16[640,256]{1,0:T(8,128)(2,1)S(1)}, u32[]{:S(2)}, u32[]{:S(2)}) collective-permute-start(bf16[640,256]{1,0:T(8,128)(2,1)S(1)} %get-tuple-element.54), channel_id=1, source_target_pairs={{0,4},{4,0},{8,12},{12,8},{16,20},{20,16},{24,28},{28,24},{32,36},... | collective-permute-start | bytes 983048 | tf_op jit(solution)/shard_map/ppermute | solution.py:49
  25.4 0.4 shard_map.132.keep
  25.8 0.9 %collective-permute-done.7.got = bf16[640,256]{1,0:T(8,128)(2,1)S(1)} collective-permute-done((bf16[640,256]{1,0:T(8,128)(2,1)S(1)}, bf16[640,256]{1,0:T(8,128)(2,1)S(1)}, u32[]{:S(2)}, u32[]{:S(2)}) %collective-permute-start.7) | collective-permute-done | bytes 327712 | tf_op jit(solution)/shard_map/ppermute | solution.py:49
  26.7 0.8 %shard_map.133 = bf16[32,40,128]{2,1,0:T(8,128)(2,1)} custom-call(f32[640,256]{1,0:T(8,128)S(1)} %shard_map.132.keep, bf16[640,256]{1,0:T(8,128)(2,1)S(1)} %collective-permute-done.7.got), custom_call_target="tpu_custom_call" | custom-call | bytes 1500000 | tf_op jit(solution)/shard_map/pallas_call | solution.py:421
  27.5 5.9 %all-to-all-start = ((bf16[32,40,128]{2,1,0:T(8,128)(2,1)}), bf16[32,40,128]{2,1,0:T(8,128)(2,1)S(1)}, u32[]{:S(2)}, u32[]{:S(2)}) async-start(bf16[32,40,128]{2,1,0:T(8,128)(2,1)} %shard_map.133), calls=%async_computation | async-start | bytes 655360 | tf_op jit(solution)/shard_map/all_to_all | solution.py:65
  33.4 1.7 %shard_map.134 = (bf16[256,256]{1,0:T(8,128)(2,1)}, bf16[256,256]{1,0:T(8,128)(2,1)}, bf16[256,256]{1,0:T(8,128)(2,1)}, bf16[256,256]{1,0:T(8,128)(2,1)S(1)}, bf...) custom-call(s32[1,2,4]{2,1,0:T(2,128)} %bitcast.5, ...), custom_call_target="tpu_custom_call" | custom-call | flops 600000000 | bytes 3000000 | tf_op jit(solution)/shard_map/pallas_call | solution.py:423
  35.1 0.8 %copy-done.2 = f32[512,256]{1,0:T(8,128)} copy-done((f32[512,256]{1,0:T(8,128)}, f32[512,256]{1,0:T(8,128)S(1)}, u32[]{:S(2)}) %copy-start.2) | copy-done | bytes 524312
  35.9 0.7 %copy-done.4 = bf16[640,256]{1,0:T(8,128)(2,1)} copy-done((bf16[640,256]{1,0:T(8,128)(2,1)}, bf16[640,256]{1,0:T(8,128)(2,1)S(1)}, u32[]{:S(2)}) %copy-start.4) | copy-done | bytes 327704
  36.6 0.7 %copy-done.6 = bf16[640,256]{1,0:T(8,128)(2,1)} copy-done((bf16[640,256]{1,0:T(8,128)(2,1)}, bf16[640,256]{1,0:T(8,128)(2,1)S(1)}, u32[]{:S(2)}) %copy-start.6) | copy-done | bytes 327704
  37.3 1.2 %collective-permute-start.9 = (bf16[256,256]{1,0:T(8,128)(2,1)}, bf16[256,256]{1,0:T(8,128)(2,1)S(1)}, u32[]{:S(2)}, u32[]{:S(2)}) collective-permute-start(bf16[256,256]{1,0:T(8,128)(2,1)} %get-tuple-element.74), channel_id=1, source_target_pairs={{0,8},{4,12},{8,0},{12,4},{16,24},{20,28},{24,16},{28,20},{32,40},... | collective-permute-start | bytes 393224 | tf_op jit(solution)/shard_map/ppermute | solution.py:49
  38.6 1.1 %collective-permute-start.10 = (bf16[256,256]{1,0:T(8,128)(2,1)}, bf16[256,256]{1,0:T(8,128)(2,1)S(1)}, u32[]{:S(2)}, u32[]{:S(2)}) collective-permute-start(bf16[256,256]{1,0:T(8,128)(2,1)} %get-tuple-element.75), channel_id=1, source_target_pairs={{4,8},{12,16},{20,24},{28,32},{36,40},{44,48},{52,56},{60,64},{68,... | collective-permute-start | bytes 393224 | tf_op jit(solution)/shard_map/ppermute | solution.py:56
  39.6 4.8 %collective-permute-start.11 = (bf16[256,256]{1,0:T(8,128)(2,1)}, bf16[256,256]{1,0:T(8,128)(2,1)S(1)}, u32[]{:S(2)}, u32[]{:S(2)}) collective-permute-start(bf16[256,256]{1,0:T(8,128)(2,1)} %get-tuple-element.76), channel_id=1, source_target_pairs={{8,16},{12,20},{24,32},{28,36},{40,48},{44,52},{56,64},{60,68},{72... | collective-permute-start | bytes 393224 | tf_op jit(solution)/shard_map/ppermute | solution.py:56
  44.7 0.8 %shard_map.135 = bf16[32,40,128]{2,1,0:T(8,128)(2,1)} custom-call(bf16[32,40,128]{2,1,0:T(8,128)(2,1)S(1)} %all-to-all-done.got), custom_call_target="tpu_custom_call" | custom-call | bytes 700000 | tf_op jit(solution)/shard_map/pallas_call | solution.py:435
  45.5 6.7 %all-to-all-start.1 = ((bf16[32,40,128]{2,1,0:T(8,128)(2,1)}), bf16[32,40,128]{2,1,0:T(8,128)(2,1)S(1)}, u32[]{:S(2)}, u32[]{:S(2)}) async-start(bf16[32,40,128]{2,1,0:T(8,128)(2,1)} %shard_map.135), calls=%async_computation.1 | async-start | bytes 655360 | tf_op jit(solution)/shard_map/all_to_all | solution.py:65
  52.2 1.1 %shard_map.137 = (f32[160,512]{1,0:T(8,128)S(1)}, bf16[160,512]{1,0:T(8,128)(2,1)S(1)}, bf16[160,512]{1,0:T(8,128)(2,1)S(1)}, bf16[160,512]{1,0:T(8,128)(2,1)S(1)}) custom-call(f32[32,128]{1,0:T(8,128)S(1)} %get-tuple-element.69.place, f32[512,256]{1,0:T(8,128)S(1)} %copy-done.3, bf16[512,256]{1,0:T(8,128)(2,1)S(1)} %get-tuple-element.71.low, ...), custom_call_target="tpu_custom_call" | custom-call | flops 60000002048 | bytes 3000000 | tf_op jit(solution)/shard_map/pallas_call | solution.py:438
  53.3 2.0 %collective-permute-start.13 = (bf16[160,512]{1,0:T(8,128)(2,1)S(1)}, bf16[160,512]{1,0:T(8,128)(2,1)S(1)}, u32[]{:S(2)}, u32[]{:S(2)}) collective-permute-start(bf16[160,512]{1,0:T(8,128)(2,1)S(1)} %get-tuple-element.79), channel_id=1, source_target_pairs={{0,2},{1,3},{2,0},{3,1},{4,6},{5,7},{6,4},{7,5},{8,10},{9,11},{10,... | collective-permute-start | bytes 491528 | tf_op jit(solution)/shard_map/ppermute | solution.py:60
  55.4 0.9 %collective-permute-start.14 = (bf16[160,512]{1,0:T(8,128)(2,1)S(1)}, bf16[160,512]{1,0:T(8,128)(2,1)S(1)}, u32[]{:S(2)}, u32[]{:S(2)}) collective-permute-start(bf16[160,512]{1,0:T(8,128)(2,1)S(1)} %get-tuple-element.80), channel_id=1, source_target_pairs={{0,1},{1,0},{2,3},{3,2},{4,5},{5,4},{6,7},{7,6},{8,9},{9,8},{10,11... | collective-permute-start | bytes 491528 | tf_op jit(solution)/shard_map/ppermute | solution.py:60
  56.2 1.2 %collective-permute-start.15 = (bf16[160,512]{1,0:T(8,128)(2,1)S(1)}, bf16[160,512]{1,0:T(8,128)(2,1)S(1)}, u32[]{:S(2)}, u32[]{:S(2)}) collective-permute-start(bf16[160,512]{1,0:T(8,128)(2,1)S(1)} %get-tuple-element.81), channel_id=1, source_target_pairs={{0,3},{1,2},{2,1},{3,0},{4,7},{5,6},{6,5},{7,4},{8,11},{9,10},{10,... | collective-permute-start | bytes 491528 | tf_op jit(solution)/shard_map/ppermute | solution.py:60
  57.4 4.7 %all-to-all-done.1.mine = bf16[32,40,128]{2,1,0:T(8,128)(2,1)S(1)} async-done(((bf16[32,40,128]{2,1,0:T(8,128)(2,1)}), bf16[32,40,128]{2,1,0:T(8,128)(2,1)S(1)}, u32[]{:S(2)}, u32[]{:S(2)}) %all-to-all-start.1) | async-done | bytes 327712 | tf_op jit(solution)/shard_map/all_to_all | solution.py:65
  62.1 4.5 %collective-permute-start.8 = (bf16[32,40,128]{2,1,0:T(8,128)(2,1)S(1)}, bf16[32,40,128]{2,1,0:T(8,128)(2,1)S(1)}, u32[]{:S(2)}, u32[]{:S(2)}) collective-permute-start(bf16[32,40,128]{2,1,0:T(8,128)(2,1)S(1)} %all-to-all-done.1.mine), channel_id=1, source_target_pairs={{0,4},{4,0},{8,12},{12,8},{16,20},{20,16},{24,28},{28,24},{32,36},... | collective-permute-start | bytes 983048 | tf_op jit(solution)/shard_map/ppermute | solution.py:49
  66.5 0.7 %fusion = bf16[512,160]{0,1:T(8,128)(2,1)} fusion(bf16[160,512]{1,0:T(8,128)(2,1)S(1)} %collective-permute-done.15, bf16[160,512]{1,0:T(8,128)(2,1)S(1)} %collective-permute-done.14, f32[160,512]{1,0:T(8,128)S(1)} %get-tuple-element.78, bf16[160,512]{1,0:T(8,128)(2,1)S(1)} %collective-permute-done.13), kind=kLoop, calls=%fused_computation.1 | loop fusion | flops 573440 | bytes 983040 | tf_op jit(solution)/shard_map/transpose | solution.py:458
  67.3 0.5 collective-permute-done.8.other
  67.8 1.2 %shard_map.136 = (f32[640,256]{1,0:T(8,128)}, f32[640,256]{1,0:T(8,128)}) custom-call(bf16[32,40,128]{2,1,0:T(8,128)(2,1)S(1)} %all-to-all-done.1.mine, bf16[32,40,128]{2,1,0:T(8,128)(2,1)S(1)} %collective-permute-done.8.other), custom_call_target="tpu_custom_call" | custom-call | bytes 2000000 | tf_op jit(solution)/shard_map/pallas_call | solution.py:449
  (32 shorter events, 0.3 us)
Async XLA Ops:
  1.8 10.8 %collective-permute-start.3 = (bf16[256,640]{1,0:T(8,128)(2,1)S(1)}, bf16[256,640]{1,0:T(8,128)(2,1)S(1)}, u32[]{:S(2)}, u32[]{:S(2)}) collective-permute-start(bf16[256,640]{1,0:T(8,128)(2,1)S(1)} %get-tuple-element.47), channel_id=1, source_target_pairs={{0,4},{4,0},{8,12},{12,8},{16,20},{20,16},{24,28},{28,24},{32,36},... | collective-permute-start | bytes 983048 | tf_op jit(solution)/shard_map/ppermute | solution.py:49
  5.2 7.5 %collective-permute-start.2 = (bf16[64,640]{1,0:T(8,128)(2,1)S(1)}, bf16[64,640]{1,0:T(8,128)(2,1)S(1)}, u32[]{:S(2)}, u32[]{:S(2)}) collective-permute-start(bf16[64,640]{1,0:T(8,128)(2,1)S(1)} %get-tuple-element.46), channel_id=1, source_target_pairs={{4,8},{12,16},{20,24},{28,32},{36,40},{44,48},{52,56},{60,64},{68,... | collective-permute-start | bytes 245768 | tf_op jit(solution)/shard_map/ppermute | solution.py:56
  5.2 15.0 %collective-permute-start = (bf16[256,640]{1,0:T(8,128)(2,1)S(1)}, bf16[256,640]{1,0:T(8,128)(2,1)S(1)}, u32[]{:S(2)}, u32[]{:S(2)}) collective-permute-start(bf16[256,640]{1,0:T(8,128)(2,1)S(1)} %get-tuple-element.44), channel_id=1, source_target_pairs={{0,8},{4,12},{8,0},{12,4},{16,24},{20,28},{24,16},{28,20},{32,40},... | collective-permute-start | bytes 983048 | tf_op jit(solution)/shard_map/ppermute | solution.py:49
  6.7 13.5 %collective-permute-start.1 = (bf16[256,640]{1,0:T(8,128)(2,1)S(1)}, bf16[256,640]{1,0:T(8,128)(2,1)S(1)}, u32[]{:S(2)}, u32[]{:S(2)}) collective-permute-start(bf16[256,640]{1,0:T(8,128)(2,1)S(1)} %get-tuple-element.45), channel_id=1, source_target_pairs={{8,16},{12,20},{24,32},{28,36},{40,48},{44,52},{56,64},{60,68},{72... | collective-permute-start | bytes 983048 | tf_op jit(solution)/shard_map/ppermute | solution.py:56
  12.7 7.5 %collective-permute-start.6 = (bf16[64,640]{1,0:T(8,128)(2,1)S(1)}, bf16[64,640]{1,0:T(8,128)(2,1)S(1)}, u32[]{:S(2)}, u32[]{:S(2)}) collective-permute-start(bf16[64,640]{1,0:T(8,128)(2,1)S(1)} %collective-permute-done.2.share0), channel_id=1, source_target_pairs={{0,3},{1,2},{2,1},{3,0},{4,7},{5,6},{6,5},{7,4},{8,11},{9,10},{10,... | collective-permute-start | bytes 245768 | tf_op jit(solution)/shard_map/ppermute | solution.py:60
  15.4 4.8 %collective-permute-start.5 = (bf16[64,640]{1,0:T(8,128)(2,1)S(1)}, bf16[64,640]{1,0:T(8,128)(2,1)S(1)}, u32[]{:S(2)}, u32[]{:S(2)}) collective-permute-start(bf16[64,640]{1,0:T(8,128)(2,1)S(1)} %collective-permute-done.2.share0), channel_id=1, source_target_pairs={{0,1},{1,0},{2,3},{3,2},{4,5},{5,4},{6,7},{7,6},{8,9},{9,8},{10,11... | collective-permute-start | bytes 245768 | tf_op jit(solution)/shard_map/ppermute | solution.py:60
  15.4 5.9 %collective-permute-start.4 = (bf16[64,640]{1,0:T(8,128)(2,1)S(1)}, bf16[64,640]{1,0:T(8,128)(2,1)S(1)}, u32[]{:S(2)}, u32[]{:S(2)}) collective-permute-start(bf16[64,640]{1,0:T(8,128)(2,1)S(1)} %collective-permute-done.2.share0), channel_id=1, source_target_pairs={{0,2},{1,3},{2,0},{3,1},{4,6},{5,7},{6,4},{7,5},{8,10},{9,11},{10,... | collective-permute-start | bytes 245768 | tf_op jit(solution)/shard_map/ppermute | solution.py:60
  16.7 4.7 %copy-start.1 = (bf16[640,256]{1,0:T(8,128)(2,1)S(1)}, bf16[640,256]{1,0:T(8,128)(2,1)}, u32[]{:S(2)}) copy-start(bf16[640,256]{1,0:T(8,128)(2,1)} %neigh_w.3) | copy-start | bytes 983044
  16.7 4.7 %copy-start.8 = (bf16[512,256]{1,0:T(8,128)(2,1)S(1)}, bf16[512,256]{1,0:T(8,128)(2,1)}, u32[]{:S(2)}) copy-start(bf16[512,256]{1,0:T(8,128)(2,1)} %cot.1) | copy-start | bytes 786436
  23.8 2.9 %collective-permute-start.7 = (bf16[640,256]{1,0:T(8,128)(2,1)S(1)}, bf16[640,256]{1,0:T(8,128)(2,1)S(1)}, u32[]{:S(2)}, u32[]{:S(2)}) collective-permute-start(bf16[640,256]{1,0:T(8,128)(2,1)S(1)} %get-tuple-element.54), channel_id=1, source_target_pairs={{0,4},{4,0},{8,12},{12,8},{16,20},{20,16},{24,28},{28,24},{32,36},... | collective-permute-start | bytes 983048 | tf_op jit(solution)/shard_map/ppermute | solution.py:49
  25.8 7.6 %copy-start = (bf16[640,256]{1,0:T(8,128)(2,1)S(1)}, bf16[640,256]{1,0:T(8,128)(2,1)}, u32[]{:S(2)}) copy-start(bf16[640,256]{1,0:T(8,128)(2,1)} %self_w.3) | copy-start | bytes 983044
  27.5 17.2 %all-to-all-start = ((bf16[32,40,128]{2,1,0:T(8,128)(2,1)}), bf16[32,40,128]{2,1,0:T(8,128)(2,1)S(1)}, u32[]{:S(2)}, u32[]{:S(2)}) async-start(bf16[32,40,128]{2,1,0:T(8,128)(2,1)} %shard_map.133), calls=%async_computation | async-start | bytes 655360 | tf_op jit(solution)/shard_map/all_to_all | solution.py:65
  35.1 0.8 %copy-start.2 = (f32[512,256]{1,0:T(8,128)}, f32[512,256]{1,0:T(8,128)S(1)}, u32[]{:S(2)}) copy-start(f32[512,256]{1,0:T(8,128)S(1)} %get-tuple-element.70.start) | copy-start | bytes 1572868
  35.9 0.7 %copy-start.4 = (bf16[640,256]{1,0:T(8,128)(2,1)}, bf16[640,256]{1,0:T(8,128)(2,1)S(1)}, u32[]{:S(2)}) copy-start(bf16[640,256]{1,0:T(8,128)(2,1)S(1)} %get-tuple-element.72.self_w) | copy-start | bytes 983044
  36.6 0.7 %copy-start.6 = (bf16[640,256]{1,0:T(8,128)(2,1)}, bf16[640,256]{1,0:T(8,128)(2,1)S(1)}, u32[]{:S(2)}) copy-start(bf16[640,256]{1,0:T(8,128)(2,1)S(1)} %get-tuple-element.73.neigh_w) | copy-start | bytes 983044
  37.3 14.8 %copy-start.3 = (f32[512,256]{1,0:T(8,128)S(1)}, f32[512,256]{1,0:T(8,128)}, u32[]{:S(2)}) copy-start(f32[512,256]{1,0:T(8,128)} %copy-done.2) | copy-start | bytes 1572868
  37.3 14.9 %copy-start.5 = (bf16[640,256]{1,0:T(8,128)(2,1)S(1)}, bf16[640,256]{1,0:T(8,128)(2,1)}, u32[]{:S(2)}) copy-start(bf16[640,256]{1,0:T(8,128)(2,1)} %copy-done.4) | copy-start | bytes 983044
  37.3 14.9 %copy-start.7 = (bf16[640,256]{1,0:T(8,128)(2,1)S(1)}, bf16[640,256]{1,0:T(8,128)(2,1)}, u32[]{:S(2)}) copy-start(bf16[640,256]{1,0:T(8,128)(2,1)} %copy-done.6) | copy-start | bytes 983044
  37.3 14.8 %collective-permute-start.9 = (bf16[256,256]{1,0:T(8,128)(2,1)}, bf16[256,256]{1,0:T(8,128)(2,1)S(1)}, u32[]{:S(2)}, u32[]{:S(2)}) collective-permute-start(bf16[256,256]{1,0:T(8,128)(2,1)} %get-tuple-element.74), channel_id=1, source_target_pairs={{0,8},{4,12},{8,0},{12,4},{16,24},{20,28},{24,16},{28,20},{32,40},... | collective-permute-start | bytes 393224 | tf_op jit(solution)/shard_map/ppermute | solution.py:49
  38.6 13.6 %collective-permute-start.10 = (bf16[256,256]{1,0:T(8,128)(2,1)}, bf16[256,256]{1,0:T(8,128)(2,1)S(1)}, u32[]{:S(2)}, u32[]{:S(2)}) collective-permute-start(bf16[256,256]{1,0:T(8,128)(2,1)} %get-tuple-element.75), channel_id=1, source_target_pairs={{4,8},{12,16},{20,24},{28,32},{36,40},{44,48},{52,56},{60,64},{68,... | collective-permute-start | bytes 393224 | tf_op jit(solution)/shard_map/ppermute | solution.py:56
  39.6 12.5 %collective-permute-start.11 = (bf16[256,256]{1,0:T(8,128)(2,1)}, bf16[256,256]{1,0:T(8,128)(2,1)S(1)}, u32[]{:S(2)}, u32[]{:S(2)}) collective-permute-start(bf16[256,256]{1,0:T(8,128)(2,1)} %get-tuple-element.76), channel_id=1, source_target_pairs={{8,16},{12,20},{24,32},{28,36},{40,48},{44,52},{56,64},{60,68},{72... | collective-permute-start | bytes 393224 | tf_op jit(solution)/shard_map/ppermute | solution.py:56
  44.5 7.7 %collective-permute-start.12 = (bf16[256,256]{1,0:T(8,128)(2,1)S(1)}, bf16[256,256]{1,0:T(8,128)(2,1)S(1)}, u32[]{:S(2)}, u32[]{:S(2)}) collective-permute-start(bf16[256,256]{1,0:T(8,128)(2,1)S(1)} %get-tuple-element.77), channel_id=1, source_target_pairs={{0,4},{4,0},{8,12},{12,8},{16,20},{20,16},{24,28},{28,24},{32,36},... | collective-permute-start | bytes 393224 | tf_op jit(solution)/shard_map/ppermute | solution.py:49
  45.5 16.6 %all-to-all-start.1 = ((bf16[32,40,128]{2,1,0:T(8,128)(2,1)}), bf16[32,40,128]{2,1,0:T(8,128)(2,1)S(1)}, u32[]{:S(2)}, u32[]{:S(2)}) async-start(bf16[32,40,128]{2,1,0:T(8,128)(2,1)} %shard_map.135), calls=%async_computation.1 | async-start | bytes 655360 | tf_op jit(solution)/shard_map/all_to_all | solution.py:65
  53.3 13.2 %collective-permute-start.13 = (bf16[160,512]{1,0:T(8,128)(2,1)S(1)}, bf16[160,512]{1,0:T(8,128)(2,1)S(1)}, u32[]{:S(2)}, u32[]{:S(2)}) collective-permute-start(bf16[160,512]{1,0:T(8,128)(2,1)S(1)} %get-tuple-element.79), channel_id=1, source_target_pairs={{0,2},{1,3},{2,0},{3,1},{4,6},{5,7},{6,4},{7,5},{8,10},{9,11},{10,... | collective-permute-start | bytes 491528 | tf_op jit(solution)/shard_map/ppermute | solution.py:60
  55.4 11.2 %collective-permute-start.14 = (bf16[160,512]{1,0:T(8,128)(2,1)S(1)}, bf16[160,512]{1,0:T(8,128)(2,1)S(1)}, u32[]{:S(2)}, u32[]{:S(2)}) collective-permute-start(bf16[160,512]{1,0:T(8,128)(2,1)S(1)} %get-tuple-element.80), channel_id=1, source_target_pairs={{0,1},{1,0},{2,3},{3,2},{4,5},{5,4},{6,7},{7,6},{8,9},{9,8},{10,11... | collective-permute-start | bytes 491528 | tf_op jit(solution)/shard_map/ppermute | solution.py:60
  56.2 10.3 %collective-permute-start.15 = (bf16[160,512]{1,0:T(8,128)(2,1)S(1)}, bf16[160,512]{1,0:T(8,128)(2,1)S(1)}, u32[]{:S(2)}, u32[]{:S(2)}) collective-permute-start(bf16[160,512]{1,0:T(8,128)(2,1)S(1)} %get-tuple-element.81), channel_id=1, source_target_pairs={{0,3},{1,2},{2,1},{3,0},{4,7},{5,6},{6,5},{7,4},{8,11},{9,10},{10,... | collective-permute-start | bytes 491528 | tf_op jit(solution)/shard_map/ppermute | solution.py:60
  62.1 5.7 %collective-permute-start.8 = (bf16[32,40,128]{2,1,0:T(8,128)(2,1)S(1)}, bf16[32,40,128]{2,1,0:T(8,128)(2,1)S(1)}, u32[]{:S(2)}, u32[]{:S(2)}) collective-permute-start(bf16[32,40,128]{2,1,0:T(8,128)(2,1)S(1)} %all-to-all-done.1.mine), channel_id=1, source_target_pairs={{0,4},{4,0},{8,12},{12,8},{16,20},{20,16},{24,28},{28,24},{32,36},... | collective-permute-start | bytes 983048 | tf_op jit(solution)/shard_map/ppermute | solution.py:49

commit v6 on v5

--- a/solution.py
+++ b/solution.py
@@ -61,7 +61,8 @@
 
 
 def exchange(array):
-    groups = [[CORES * chip + core for chip in range(CHIPS)] for core in range(CORES)]
+    chips = list(reversed(range(CHIPS)))
+    groups = [[CORES * chip + core for chip in chips] for core in range(CORES)]
     return lax.all_to_all(array, "dom", 0, 0, axis_index_groups=groups)
 
 
@@ -75,13 +76,13 @@
 
 def swaps(arrays):
     a, b, c, d = arrays
-    return [dom_swap(a, 2), dom_pairs(b, 1), dom_pairs(c, 2), dom_swap(d, 1)]
+    return [dom_pairs(a, 2), dom_pairs(b, 1), dom_swap(c, 2), dom_swap(d, 1)]
 
 
 def sent_rounds():
     me = lax.axis_index("dom")
     core, chip = lax.rem(me, CORES), lax.rem(me // CORES, 2)
-    return (2 + chip, 1 - core, 3 - chip, core)
+    return (3 - chip, 1 - core, 2 + chip, core)
 
 
 def received_rounds():
@@ -89,7 +90,7 @@
     return (5 - first, 1 - second, 5 - third, 1 - fourth)
 
 
-def pack_kernel(send, feats, out0, out1, out2, out3, send_now, feats_now, sems):
+def pack_kernel(send, feats, out0, out1, out2, out3, feats_now, send_now, sems):
     copies = [
         pltpu.make_async_copy(send, send_now, sems.at[0]),
         pltpu.make_async_copy(feats, feats_now, sems.at[1]),
@@ -109,31 +110,33 @@
             out[s * BS : (s + 1) * BS, :] = feats_now[rows(send_now[0, s, r]), :]
 
 
+def turn_kernel(feats, turned):
+    turned[...] = feats[...].T
+
+
 def before_kernel(
     neighbors,
     recv,
     live,
-    feats,
     self_w,
     tiles,
     edge_tiles,
+    feats,
+    got,
     local,
     edge,
     local_sum,
-    degree,
+    inverse,
     own_pre,
-    turned,
     neighbors_now,
     recv_now,
     live_now,
-    feats_now,
     self_w_now,
     tiles_now,
     edge_tiles_now,
     sems,
 ):
     pairs = (
-        (feats, feats_now),
         (self_w, self_w_now),
         (neighbors, neighbors_now),
         (recv, recv_now),
@@ -146,12 +149,10 @@
         copy.start()
     local[...] = jnp.zeros_like(local)
     edge[...] = jnp.zeros_like(edge)
-    for copy in copies[:2]:
-        copy.wait()
-    mine = feats_now[...]
+    copies[0].wait()
+    mine = feats[...]
     own_pre[...] = dot(mine, self_w_now[...])
-    turned[...] = mine.T
-    for copy in copies[2:]:
+    for copy in copies[1:]:
         copy.wait()
     for b in range(BLK):
         for k in range(K_IN):
@@ -167,23 +168,23 @@
                 edge[rows(recv_now[0, s, r]), slot * BS : (slot + 1) * BS] = edge_tiles_now[0, r, s]
 
     whole = local[...]
-    local_sum[...] = dot(whole, mine)
+    of_pair = (ROUNDS - 1) * NB * BS
+    local_sum[...] = dot(whole, mine) + dot(edge[:, of_pair:], got[...])
     ones = jnp.ones((BS * BLK, BS), BF16)
     edge_ones = jnp.ones((BS * NB * ROUNDS, BS), BF16)
-    degree[...] = dot(whole, ones) + dot(edge[...], edge_ones)
+    inverse[...] = 1.0 / (dot(whole, ones) + dot(edge[...], edge_ones))
 
 
 def middle_kernel(
     edge,
     got0,
     got2,
-    got3,
     share0,
     share1,
     share2,
     share3,
     local_sum,
-    degree,
+    inverse_in,
     own_pre,
     neigh_w,
     cot,
@@ -196,14 +197,14 @@
     got1,
 ):
     size = share0.shape[0]
-    for k, share in zip((0, 2, 1, 3), (share0, share1, share2, share3)):
+    for k, share in zip((0, 3, 1, 2), (share0, share1, share2, share3)):
         got1[rows(jnp.bitwise_xor(lax.axis_index("hid"), k), size), :] = share[...]
     core = lax.rem(lax.axis_index("dom"), CORES)
     width = NB * BS
     total = local_sum[...]
-    for r, got in enumerate((got0, got1, got2, got3)):
+    for r, got in enumerate((got0, got1, got2)):
         total = total + dot(edge[:, r * width : (r + 1) * width], got[...])
-    inverse = 1.0 / degree[...]
+    inverse = inverse_in[...]
     mean = total * jnp.concatenate([inverse] * (total.shape[1] // BS), axis=1)
     mean_high = mean.astype(BF16)
     mean_rest = (mean - mean_high.astype(F32)).astype(BF16)
@@ -360,17 +361,21 @@
     slots = ROUNDS * NB * BS
     send_blocks = jnp.swapaxes(send_blocks, 1, 2)
     recv_blocks = jnp.swapaxes(recv_blocks, 1, 2)
-    packed = call(
+    *packed, feats_now = call(
         pack_kernel,
-        [((NB * BS // HID if r == 1 else NB * BS, width), BF16) for r in range(ROUNDS)],
+        [((NB * BS // HID if r == 1 else NB * BS, width), BF16) for r in range(ROUNDS)]
+        + [((n, width), BF16)],
         [HBM] * 2,
         nbytes=2_000_000,
-        scratch=[pltpu.SMEM((1, NB, ROUNDS), jnp.int32), pltpu.VMEM((n, width), BF16), DMA((2,))],
+        scratch=[pltpu.SMEM((1, NB, ROUNDS), jnp.int32), DMA((2,))],
     )(in_hbm(send_blocks), in_hbm(features))
     got_c, share, got_d, got_a = swaps(packed)
-    share, got_a = lax.optimization_barrier((share, got_a))
-    shares = [share] + [hid_swap(share, k) for k in (2, 1, 3)]
-    local, edge, local_sum, degree, own_pre, turned = call(
+    (turned,) = call(
+        turn_kernel, [((width, n), BF16)], [VMEM], flops=COVER_FLOPS, nbytes=2_000_000
+    )(feats_now)
+    share, got_a, turned = lax.optimization_barrier((share, got_a, turned))
+    shares = [share] + [hid_swap(share, k) for k in (3, 1, 2)]
+    local, edge, local_sum, inverse, own_pre = call(
         before_kernel,
         [
             ((n, n), BF16),
@@ -378,39 +383,38 @@
             ((n, width), F32),
             ((n, BS), F32),
             ((n, hidden), F32),
-            ((width, n), BF16),
         ],
-        [HBM] * 7,
+        [HBM] * 6 + [VMEM] * 2,
         flops=COVER_FLOPS,
         nbytes=6_000_000,
         scratch=[
             pltpu.SMEM((1, BLK, K_IN), jnp.int32),
             pltpu.SMEM((1, NB, ROUNDS), jnp.int32),
             pltpu.SMEM((1, ROUNDS), jnp.int32),
-            pltpu.VMEM((n, width), BF16),
             pltpu.VMEM((width, hidden), BF16),
             pltpu.VMEM((1, BLK, K_IN, BS, BS), BF16),
             pltpu.VMEM((1, ROUNDS, NB, BS, BS), BF16),
-            DMA((7,)),
+            DMA((6,)),
         ],
     )(
         in_hbm(neighbor_blocks),
         in_hbm(recv_blocks),
         in_hbm(live_slots),
-        in_hbm(features),
         in_hbm(self_weight),
         in_hbm(local_tiles),
         in_hbm(boundary_tiles),
+        feats_now,
+        got_a,
     )
     act, low, spread, mean, give = call(
         middle_kernel,
         [((n, hidden), BF16)] * 3 + [((n, width), BF16), ((width, hidden), BF16)],
-        [VMEM] * 14,
+        [VMEM] * 13,
         flops=1_600_000_000,
         nbytes=8_000_000,
         scratch=[pltpu.VMEM((NB * BS, width), BF16)],
         limit=16,
-    )(edge, got_c, got_d, got_a, *shares, local_sum, degree, own_pre, neigh_weight, cotangent, turned)
+    )(edge, got_c, got_d, *shares, local_sum, inverse, own_pre, neigh_weight, cotangent, turned)
 
     got = dom_swap(give, 1)
     (keep,) = call(

time: 69.3 us -> 68.1 us (0.983)
  starting transfers between devices: 44.9 us -> 40.6 us
  waiting for transfers between devices: 7.19 us -> 10.3 us
    ppermute x4, starting transfers between devices: 11.9 us -> 7.29 us  [dom_pairs(): return lax.ppermute(array, 'dom', pairs + [(j, i) for i, j in pairs])]
    ppermute x4, waiting for transfers between devices: 0.01 us -> 4.23 us  [dom_pairs(): return lax.ppermute(array, 'dom', pairs + [(j, i) for i, j in pairs])]
    all_to_all x2, starting transfers between devices: 12.6 us -> 14.4 us  [exchange(): return lax.all_to_all(array, 'dom', 0, 0, axis_index_groups=groups)]
    ppermute x6, waiting for transfers between devices: 1.15 us -> 0.02 us  [hid_swap(): return lax.ppermute(array, 'hid', [(i, i ^ mask) for i in range(HID)])]
    ppermute x6, starting transfers between devices: 12.4 us -> 11.4 us  [dom_swap(): return lax.ppermute(array, 'dom', [(i, i ^ mask) for i in range(count)])]
  transfers between devices with their start and end apart: 18 -> 18, of which waited for: 4 -> 6; matrix products, arithmetic and copies ran while one was open for 1% -> 1% of each run, Pallas kernels for 11% -> 11%
where the time goes in v6:
time: 68.1 us; the launch traced here: 67.7 us
  starting transfers between devices  40.6 us (60%)
  Pallas kernels  13 us (19%)
  waiting for transfers between devices  10.3 us (15%)
  local copies, waits for them, and re-layouts  2.26 us (3%)
  between operations  0.83 us (1%)
  other arithmetic  0.75 us (1%)
    all_to_all x2, starting transfers between devices, exchange(): return lax.all_to_all(array, 'dom', 0, 0, axis_index_groups=groups)  14.4 us
    ppermute x6, starting transfers between devices, dom_swap(): return lax.ppermute(array, 'dom', [(i, i ^ mask) for i in range(count)])  11.4 us
    ppermute x6, starting transfers between devices, hid_swap(): return lax.ppermute(array, 'hid', [(i, i ^ mask) for i in range(HID)])  7.48 us
    ppermute x4, starting transfers between devices, dom_pairs(): return lax.ppermute(array, 'dom', pairs + [(j, i) for i, j in pairs])  7.29 us
    all_to_all x2, waiting for transfers between devices, exchange(): return lax.all_to_all(array, 'dom', 0, 0, axis_index_groups=groups)  4.37 us
    ppermute x4, waiting for transfers between devices, dom_pairs(): return lax.ppermute(array, 'dom', pairs + [(j, i) for i, j in pairs])  4.23 us
    pallas_call x1, Pallas kernels, on_device(): call(before_kernel, [((n, n), BF16), ((n, slots), BF16), ((n, width), F32...  3.47 us
    pallas_call x1, Pallas kernels, on_device(): call(middle_kernel, [((n, hidden), BF16)] * 3 + [((n, width), BF16), ((wi...  2.28 us
  transfers between devices with their start and end apart: 18, of which 6 were waited for; matrix products, arithmetic and copies ran while one was open for 1% of the time, Pallas kernels for 11%

profile of v6, /device:TPU:1, one launch (start us, length us, event | category | flops | bytes accessed | tf_op | source)
XLA Modules:
  0.0 67.7 jit_solution(12522573079307209728)
XLA Ops:
  0.6 1.2 %shard_map.129 = (bf16[256,640]{1,0:T(8,128)(2,1)S(1)}, bf16[64,640]{1,0:T(8,128)(2,1)S(1)}, bf16[256,640]{1,0:T(8,128)(2,1)S(1)}, bf16[256,640]{1,0:T(8,128)(2,1)S(1)}, bf16[512,640]{1,0:T(8,128)(2,1)S(1)}) custom-call(s32[1,2,4]{2,1,0:T(2,128)} %bitcast.4, bf16[512,640]{1,0:T(8,128)(2,1)} %feats.1), custom_call_target="tpu_custom_call" | custom-call | bytes 2000000 | tf_op jit(solution)/shard_map/pallas_call | solution.py:364
  1.8 3.1 %collective-permute-start = (bf16[64,640]{1,0:T(8,128)(2,1)S(1)}, bf16[64,640]{1,0:T(8,128)(2,1)S(1)}, u32[]{:S(2)}, u32[]{:S(2)}) collective-permute-start(bf16[64,640]{1,0:T(8,128)(2,1)S(1)} %get-tuple-element.45), channel_id=1, source_target_pairs={{4,8},{12,16},{20,24},{28,32},{36,40},{44,48},{52,56},{60,64},{68,... | collective-permute-start | bytes 245768 | tf_op jit(solution)/shard_map/ppermute | solution.py:56
  4.9 6.0 %collective-permute-start.1 = (bf16[256,640]{1,0:T(8,128)(2,1)S(1)}, bf16[256,640]{1,0:T(8,128)(2,1)S(1)}, u32[]{:S(2)}, u32[]{:S(2)}) collective-permute-start(bf16[256,640]{1,0:T(8,128)(2,1)S(1)} %get-tuple-element.46), channel_id=1, source_target_pairs={{0,4},{4,0},{8,12},{12,8},{16,20},{20,16},{24,28},{28,24},{32,36},... | collective-permute-start | bytes 983048 | tf_op jit(solution)/shard_map/ppermute | solution.py:49
  10.9 0.7 %collective-permute-start.2 = (bf16[256,640]{1,0:T(8,128)(2,1)S(1)}, bf16[256,640]{1,0:T(8,128)(2,1)S(1)}, u32[]{:S(2)}, u32[]{:S(2)}) collective-permute-start(bf16[256,640]{1,0:T(8,128)(2,1)S(1)} %get-tuple-element.49), channel_id=1, source_target_pairs={{8,16},{12,20},{24,32},{28,36},{40,48},{44,52},{56,64},{60,68},{72... | collective-permute-start | bytes 983048 | tf_op jit(solution)/shard_map/ppermute | solution.py:56
  12.2 2.9 %collective-permute-start.6 = (bf16[64,640]{1,0:T(8,128)(2,1)S(1)}, bf16[64,640]{1,0:T(8,128)(2,1)S(1)}, u32[]{:S(2)}, u32[]{:S(2)}) collective-permute-start(bf16[64,640]{1,0:T(8,128)(2,1)S(1)} %collective-permute-done.share0), channel_id=1, source_target_pairs={{0,2},{1,3},{2,0},{3,1},{4,6},{5,7},{6,4},{7,5},{8,10},{9,11},{10,... | collective-permute-start | bytes 245768 | tf_op jit(solution)/shard_map/ppermute | solution.py:60
  15.1 0.4 collective-permute-start.5
  15.5 0.4 collective-permute-start.4
  15.9 3.5 %shard_map.131 = (bf16[512,512]{1,0:T(8,128)(2,1)S(1)}, bf16[512,1024]{1,0:T(8,128)(2,1)S(1)}, f32[512,640]{1,0:T(8,128)S(1)}, f32[512,128]{1,0:T(8,128)S(1)}, f32[512,256]{1,0:T(8,128)S(1)}) custom-call(s32[1,4,8]{2,1,0:T(4,128)} %neighbors.1, s32[1,2,4]{2,1,0:T(2,128)} %bitcast.6, s32[1,4]{1,0:T(1,128)} %live.1, bf16[640,256]{1,0:T(8,128)(2,1)} %self_w.3, ...), custom_call_target="tpu_custom_call" | custom-call | flops 60000002048 | bytes 6000000 | tf_op jit(solution)/shard_map/pallas_call | solution.py:378
  19.3 4.2 %collective-permute-done.2.got0 = bf16[256,640]{1,0:T(8,128)(2,1)S(1)} collective-permute-done((bf16[256,640]{1,0:T(8,128)(2,1)S(1)}, bf16[256,640]{1,0:T(8,128)(2,1)S(1)}, u32[]{:S(2)}, u32[]{:S(2)}) %collective-permute-start.2) | collective-permute-done | bytes 327712 | tf_op jit(solution)/shard_map/ppermute | solution.py:56
  23.6 2.3 %shard_map.132 = (bf16[512,256]{1,0:T(8,128)(2,1)S(1)}, bf16[512,256]{1,0:T(8,128)(2,1)S(1)}, bf16[512,256]{1,0:T(8,128)(2,1)S(1)}, bf16[512,640]{1,0:T(8,128)(2,1)S(1)}, bf16[640,256]{1,0:T(8,128)(2,1)S(1)}) custom-call(bf16[512,1024]{1,0:T(8,128)(2,1)S(1)} %get-tuple-element.48.edge, bf16[256,640]{1,0:T(8,128)(2,1)S(1)} %collective-permute-done.2.got0, ...), custom_call_target="tpu_custom_call" | custom-call | flops 1600000000 | bytes 8000000 | tf_op jit(solution)/shard_map/pallas_call | solution.py:409
  25.9 0.9 %collective-permute-start.7 = (bf16[640,256]{1,0:T(8,128)(2,1)S(1)}, bf16[640,256]{1,0:T(8,128)(2,1)S(1)}, u32[]{:S(2)}, u32[]{:S(2)}) collective-permute-start(bf16[640,256]{1,0:T(8,128)(2,1)S(1)} %get-tuple-element.56), channel_id=1, source_target_pairs={{0,4},{4,0},{8,12},{12,8},{16,20},{20,16},{24,28},{28,24},{32,36},... | collective-permute-start | bytes 983048 | tf_op jit(solution)/shard_map/ppermute | solution.py:49
  27.2 0.9 %collective-permute-done.7.got = bf16[640,256]{1,0:T(8,128)(2,1)S(1)} collective-permute-done((bf16[640,256]{1,0:T(8,128)(2,1)S(1)}, bf16[640,256]{1,0:T(8,128)(2,1)S(1)}, u32[]{:S(2)}, u32[]{:S(2)}) %collective-permute-start.7) | collective-permute-done | bytes 327712 | tf_op jit(solution)/shard_map/ppermute | solution.py:49
  28.1 0.8 %shard_map.134 = bf16[32,40,128]{2,1,0:T(8,128)(2,1)} custom-call(f32[640,256]{1,0:T(8,128)S(1)} %shard_map.133.keep, bf16[640,256]{1,0:T(8,128)(2,1)S(1)} %collective-permute-done.7.got), custom_call_target="tpu_custom_call" | custom-call | bytes 1500000 | tf_op jit(solution)/shard_map/pallas_call | solution.py:425
  28.9 6.3 %all-to-all-start = ((bf16[32,40,128]{2,1,0:T(8,128)(2,1)}), bf16[32,40,128]{2,1,0:T(8,128)(2,1)S(1)}, u32[]{:S(2)}, u32[]{:S(2)}) async-start(bf16[32,40,128]{2,1,0:T(8,128)(2,1)} %shard_map.134), calls=%async_computation | async-start | bytes 655360 | tf_op jit(solution)/shard_map/all_to_all | solution.py:66
  35.2 1.7 %shard_map.135 = (bf16[256,256]{1,0:T(8,128)(2,1)}, bf16[256,256]{1,0:T(8,128)(2,1)}, bf16[256,256]{1,0:T(8,128)(2,1)}, bf16[256,256]{1,0:T(8,128)(2,1)S(1)}, bf...) custom-call(s32[1,2,4]{2,1,0:T(2,128)} %bitcast.5, ...), custom_call_target="tpu_custom_call" | custom-call | flops 600000000 | bytes 3000000 | tf_op jit(solution)/shard_map/pallas_call | solution.py:427
  36.9 0.8 %copy-done.2 = f32[512,256]{1,0:T(8,128)} copy-done((f32[512,256]{1,0:T(8,128)}, f32[512,256]{1,0:T(8,128)S(1)}, u32[]{:S(2)}) %copy-start.2) | copy-done | bytes 524312
  37.7 0.7 %copy-done.4 = bf16[640,256]{1,0:T(8,128)(2,1)} copy-done((bf16[640,256]{1,0:T(8,128)(2,1)}, bf16[640,256]{1,0:T(8,128)(2,1)S(1)}, u32[]{:S(2)}) %copy-start.4) | copy-done | bytes 327704
  38.4 0.7 %copy-done.6 = bf16[640,256]{1,0:T(8,128)(2,1)} copy-done((bf16[640,256]{1,0:T(8,128)(2,1)}, bf16[640,256]{1,0:T(8,128)(2,1)S(1)}, u32[]{:S(2)}) %copy-start.6) | copy-done | bytes 327704
  39.3 3.3 %collective-permute-start.10 = (bf16[256,256]{1,0:T(8,128)(2,1)}, bf16[256,256]{1,0:T(8,128)(2,1)S(1)}, u32[]{:S(2)}, u32[]{:S(2)}) collective-permute-start(bf16[256,256]{1,0:T(8,128)(2,1)} %get-tuple-element.77), channel_id=1, source_target_pairs={{4,8},{12,16},{20,24},{28,32},{36,40},{44,48},{52,56},{60,64},{68,... | collective-permute-start | bytes 393224 | tf_op jit(solution)/shard_map/ppermute | solution.py:56
  42.9 1.4 %collective-permute-start.12 = (bf16[256,256]{1,0:T(8,128)(2,1)S(1)}, bf16[256,256]{1,0:T(8,128)(2,1)S(1)}, u32[]{:S(2)}, u32[]{:S(2)}) collective-permute-start(bf16[256,256]{1,0:T(8,128)(2,1)S(1)} %get-tuple-element.79), channel_id=1, source_target_pairs={{0,4},{4,0},{8,12},{12,8},{16,20},{20,16},{24,28},{28,24},{32,36},... | collective-permute-start | bytes 393224 | tf_op jit(solution)/shard_map/ppermute | solution.py:49
  44.3 0.6 all-to-all-done.got
  44.8 0.8 %shard_map.136 = bf16[32,40,128]{2,1,0:T(8,128)(2,1)} custom-call(bf16[32,40,128]{2,1,0:T(8,128)(2,1)S(1)} %all-to-all-done.got), custom_call_target="tpu_custom_call" | custom-call | bytes 700000 | tf_op jit(solution)/shard_map/pallas_call | solution.py:439
  45.6 8.1 %all-to-all-start.1 = ((bf16[32,40,128]{2,1,0:T(8,128)(2,1)}), bf16[32,40,128]{2,1,0:T(8,128)(2,1)S(1)}, u32[]{:S(2)}, u32[]{:S(2)}) async-start(bf16[32,40,128]{2,1,0:T(8,128)(2,1)} %shard_map.136), calls=%async_computation.1 | async-start | bytes 655360 | tf_op jit(solution)/shard_map/all_to_all | solution.py:66
  53.8 1.1 %shard_map.138 = (f32[160,512]{1,0:T(8,128)S(1)}, bf16[160,512]{1,0:T(8,128)(2,1)S(1)}, bf16[160,512]{1,0:T(8,128)(2,1)S(1)}, bf16[160,512]{1,0:T(8,128)(2,1)S(1)}) custom-call(f32[32,128]{1,0:T(8,128)S(1)} %get-tuple-element.71.place, f32[512,256]{1,0:T(8,128)S(1)} %copy-done.3, bf16[512,256]{1,0:T(8,128)(2,1)S(1)} %get-tuple-element.73.low, ...), custom_call_target="tpu_custom_call" | custom-call | flops 60000002048 | bytes 3000000 | tf_op jit(solution)/shard_map/pallas_call | solution.py:442
  54.9 3.0 %collective-permute-start.13 = (bf16[160,512]{1,0:T(8,128)(2,1)S(1)}, bf16[160,512]{1,0:T(8,128)(2,1)S(1)}, u32[]{:S(2)}, u32[]{:S(2)}) collective-permute-start(bf16[160,512]{1,0:T(8,128)(2,1)S(1)} %get-tuple-element.81), channel_id=1, source_target_pairs={{0,2},{1,3},{2,0},{3,1},{4,6},{5,7},{6,4},{7,5},{8,10},{9,11},{10,... | collective-permute-start | bytes 491528 | tf_op jit(solution)/shard_map/ppermute | solution.py:60
  57.9 0.4 collective-permute-start.14
  58.3 0.4 collective-permute-start.15
  58.7 3.8 %all-to-all-done.1.mine = bf16[32,40,128]{2,1,0:T(8,128)(2,1)S(1)} async-done(((bf16[32,40,128]{2,1,0:T(8,128)(2,1)}), bf16[32,40,128]{2,1,0:T(8,128)(2,1)S(1)}, u32[]{:S(2)}, u32[]{:S(2)}) %all-to-all-start.1) | async-done | bytes 327712 | tf_op jit(solution)/shard_map/all_to_all | solution.py:66
  62.5 2.8 %collective-permute-start.8 = (bf16[32,40,128]{2,1,0:T(8,128)(2,1)S(1)}, bf16[32,40,128]{2,1,0:T(8,128)(2,1)S(1)}, u32[]{:S(2)}, u32[]{:S(2)}) collective-permute-start(bf16[32,40,128]{2,1,0:T(8,128)(2,1)S(1)} %all-to-all-done.1.mine), channel_id=1, source_target_pairs={{0,4},{4,0},{8,12},{12,8},{16,20},{20,16},{24,28},{28,24},{32,36},... | collective-permute-start | bytes 983048 | tf_op jit(solution)/shard_map/ppermute | solution.py:49
  65.3 0.7 %fusion = bf16[512,160]{0,1:T(8,128)(2,1)} fusion(bf16[160,512]{1,0:T(8,128)(2,1)S(1)} %collective-permute-done.15, bf16[160,512]{1,0:T(8,128)(2,1)S(1)} %collective-permute-done.14, f32[160,512]{1,0:T(8,128)S(1)} %get-tuple-element.80, bf16[160,512]{1,0:T(8,128)(2,1)S(1)} %collective-permute-done.13), kind=kLoop, calls=%fused_computation.1 | loop fusion | flops 573440 | bytes 983040 | tf_op jit(solution)/shard_map/transpose | solution.py:462
  66.1 0.5 collective-permute-done.8.other
  66.6 1.2 %shard_map.137 = (f32[640,256]{1,0:T(8,128)}, f32[640,256]{1,0:T(8,128)}) custom-call(bf16[32,40,128]{2,1,0:T(8,128)(2,1)S(1)} %all-to-all-done.1.mine, bf16[32,40,128]{2,1,0:T(8,128)(2,1)S(1)} %collective-permute-done.8.other), custom_call_target="tpu_custom_call" | custom-call | bytes 2000000 | tf_op jit(solution)/shard_map/pallas_call | solution.py:453
  (33 shorter events, 1.4 us)
Async XLA Ops:
  1.8 10.0 %collective-permute-start = (bf16[64,640]{1,0:T(8,128)(2,1)S(1)}, bf16[64,640]{1,0:T(8,128)(2,1)S(1)}, u32[]{:S(2)}, u32[]{:S(2)}) collective-permute-start(bf16[64,640]{1,0:T(8,128)(2,1)S(1)} %get-tuple-element.45), channel_id=1, source_target_pairs={{4,8},{12,16},{20,24},{28,32},{36,40},{44,48},{52,56},{60,64},{68,... | collective-permute-start | bytes 245768 | tf_op jit(solution)/shard_map/ppermute | solution.py:56
  4.9 7.2 %collective-permute-start.1 = (bf16[256,640]{1,0:T(8,128)(2,1)S(1)}, bf16[256,640]{1,0:T(8,128)(2,1)S(1)}, u32[]{:S(2)}, u32[]{:S(2)}) collective-permute-start(bf16[256,640]{1,0:T(8,128)(2,1)S(1)} %get-tuple-element.46), channel_id=1, source_target_pairs={{0,4},{4,0},{8,12},{12,8},{16,20},{20,16},{24,28},{28,24},{32,36},... | collective-permute-start | bytes 983048 | tf_op jit(solution)/shard_map/ppermute | solution.py:49
  10.9 12.7 %collective-permute-start.2 = (bf16[256,640]{1,0:T(8,128)(2,1)S(1)}, bf16[256,640]{1,0:T(8,128)(2,1)S(1)}, u32[]{:S(2)}, u32[]{:S(2)}) collective-permute-start(bf16[256,640]{1,0:T(8,128)(2,1)S(1)} %get-tuple-element.49), channel_id=1, source_target_pairs={{8,16},{12,20},{24,32},{28,36},{40,48},{44,52},{56,64},{60,68},{72... | collective-permute-start | bytes 983048 | tf_op jit(solution)/shard_map/ppermute | solution.py:56
  11.6 11.9 %collective-permute-start.3 = (bf16[256,640]{1,0:T(8,128)(2,1)S(1)}, bf16[256,640]{1,0:T(8,128)(2,1)S(1)}, u32[]{:S(2)}, u32[]{:S(2)}) collective-permute-start(bf16[256,640]{1,0:T(8,128)(2,1)S(1)} %get-tuple-element.50), channel_id=1, source_target_pairs={{0,8},{4,12},{8,0},{12,4},{16,24},{20,28},{24,16},{28,20},{32,40},... | collective-permute-start | bytes 983048 | tf_op jit(solution)/shard_map/ppermute | solution.py:49
  12.2 11.4 %collective-permute-start.6 = (bf16[64,640]{1,0:T(8,128)(2,1)S(1)}, bf16[64,640]{1,0:T(8,128)(2,1)S(1)}, u32[]{:S(2)}, u32[]{:S(2)}) collective-permute-start(bf16[64,640]{1,0:T(8,128)(2,1)S(1)} %collective-permute-done.share0), channel_id=1, source_target_pairs={{0,2},{1,3},{2,0},{3,1},{4,6},{5,7},{6,4},{7,5},{8,10},{9,11},{10,... | collective-permute-start | bytes 245768 | tf_op jit(solution)/shard_map/ppermute | solution.py:60
  15.1 8.5 %collective-permute-start.5 = (bf16[64,640]{1,0:T(8,128)(2,1)S(1)}, bf16[64,640]{1,0:T(8,128)(2,1)S(1)}, u32[]{:S(2)}, u32[]{:S(2)}) collective-permute-start(bf16[64,640]{1,0:T(8,128)(2,1)S(1)} %collective-permute-done.share0), channel_id=1, source_target_pairs={{0,1},{1,0},{2,3},{3,2},{4,5},{5,4},{6,7},{7,6},{8,9},{9,8},{10,11... | collective-permute-start | bytes 245768 | tf_op jit(solution)/shard_map/ppermute | solution.py:60
  15.5 8.1 %collective-permute-start.4 = (bf16[64,640]{1,0:T(8,128)(2,1)S(1)}, bf16[64,640]{1,0:T(8,128)(2,1)S(1)}, u32[]{:S(2)}, u32[]{:S(2)}) collective-permute-start(bf16[64,640]{1,0:T(8,128)(2,1)S(1)} %collective-permute-done.share0), channel_id=1, source_target_pairs={{0,3},{1,2},{2,1},{3,0},{4,7},{5,6},{6,5},{7,4},{8,11},{9,10},{10,... | collective-permute-start | bytes 245768 | tf_op jit(solution)/shard_map/ppermute | solution.py:60
  15.9 7.7 %copy-start.1 = (bf16[640,256]{1,0:T(8,128)(2,1)S(1)}, bf16[640,256]{1,0:T(8,128)(2,1)}, u32[]{:S(2)}) copy-start(bf16[640,256]{1,0:T(8,128)(2,1)} %neigh_w.3) | copy-start | bytes 983044
  15.9 7.7 %copy-start.8 = (bf16[512,256]{1,0:T(8,128)(2,1)S(1)}, bf16[512,256]{1,0:T(8,128)(2,1)}, u32[]{:S(2)}) copy-start(bf16[512,256]{1,0:T(8,128)(2,1)} %cot.1) | copy-start | bytes 786436
  25.9 2.2 %collective-permute-start.7 = (bf16[640,256]{1,0:T(8,128)(2,1)S(1)}, bf16[640,256]{1,0:T(8,128)(2,1)S(1)}, u32[]{:S(2)}, u32[]{:S(2)}) collective-permute-start(bf16[640,256]{1,0:T(8,128)(2,1)S(1)} %get-tuple-element.56), channel_id=1, source_target_pairs={{0,4},{4,0},{8,12},{12,8},{16,20},{20,16},{24,28},{28,24},{32,36},... | collective-permute-start | bytes 983048 | tf_op jit(solution)/shard_map/ppermute | solution.py:49
  27.2 8.0 %copy-start = (bf16[640,256]{1,0:T(8,128)(2,1)S(1)}, bf16[640,256]{1,0:T(8,128)(2,1)}, u32[]{:S(2)}) copy-start(bf16[640,256]{1,0:T(8,128)(2,1)} %self_w.3) | copy-start | bytes 983044
  28.9 16.0 %all-to-all-start = ((bf16[32,40,128]{2,1,0:T(8,128)(2,1)}), bf16[32,40,128]{2,1,0:T(8,128)(2,1)S(1)}, u32[]{:S(2)}, u32[]{:S(2)}) async-start(bf16[32,40,128]{2,1,0:T(8,128)(2,1)} %shard_map.134), calls=%async_computation | async-start | bytes 655360 | tf_op jit(solution)/shard_map/all_to_all | solution.py:66
  36.9 0.8 %copy-start.2 = (f32[512,256]{1,0:T(8,128)}, f32[512,256]{1,0:T(8,128)S(1)}, u32[]{:S(2)}) copy-start(f32[512,256]{1,0:T(8,128)S(1)} %get-tuple-element.72.start) | copy-start | bytes 1572868
  37.6 0.7 %copy-start.4 = (bf16[640,256]{1,0:T(8,128)(2,1)}, bf16[640,256]{1,0:T(8,128)(2,1)S(1)}, u32[]{:S(2)}) copy-start(bf16[640,256]{1,0:T(8,128)(2,1)S(1)} %get-tuple-element.74.self_w) | copy-start | bytes 983044
  38.4 0.7 %copy-start.6 = (bf16[640,256]{1,0:T(8,128)(2,1)}, bf16[640,256]{1,0:T(8,128)(2,1)S(1)}, u32[]{:S(2)}) copy-start(bf16[640,256]{1,0:T(8,128)(2,1)S(1)} %get-tuple-element.75.neigh_w) | copy-start | bytes 983044
  39.1 14.7 %copy-start.3 = (f32[512,256]{1,0:T(8,128)S(1)}, f32[512,256]{1,0:T(8,128)}, u32[]{:S(2)}) copy-start(f32[512,256]{1,0:T(8,128)} %copy-done.2) | copy-start | bytes 1572868
  39.1 14.7 %copy-start.5 = (bf16[640,256]{1,0:T(8,128)(2,1)S(1)}, bf16[640,256]{1,0:T(8,128)(2,1)}, u32[]{:S(2)}) copy-start(bf16[640,256]{1,0:T(8,128)(2,1)} %copy-done.4) | copy-start | bytes 983044
  39.1 14.7 %copy-start.7 = (bf16[640,256]{1,0:T(8,128)(2,1)S(1)}, bf16[640,256]{1,0:T(8,128)(2,1)}, u32[]{:S(2)}) copy-start(bf16[640,256]{1,0:T(8,128)(2,1)} %copy-done.6) | copy-start | bytes 983044
  39.1 14.6 %collective-permute-start.9 = (bf16[256,256]{1,0:T(8,128)(2,1)}, bf16[256,256]{1,0:T(8,128)(2,1)S(1)}, u32[]{:S(2)}, u32[]{:S(2)}) collective-permute-start(bf16[256,256]{1,0:T(8,128)(2,1)} %get-tuple-element.76), channel_id=1, source_target_pairs={{8,16},{12,20},{24,32},{28,36},{40,48},{44,52},{56,64},{60,68},{72... | collective-permute-start | bytes 393224 | tf_op jit(solution)/shard_map/ppermute | solution.py:56
  39.3 14.5 %collective-permute-start.10 = (bf16[256,256]{1,0:T(8,128)(2,1)}, bf16[256,256]{1,0:T(8,128)(2,1)S(1)}, u32[]{:S(2)}, u32[]{:S(2)}) collective-permute-start(bf16[256,256]{1,0:T(8,128)(2,1)} %get-tuple-element.77), channel_id=1, source_target_pairs={{4,8},{12,16},{20,24},{28,32},{36,40},{44,48},{52,56},{60,64},{68,... | collective-permute-start | bytes 393224 | tf_op jit(solution)/shard_map/ppermute | solution.py:56
  42.6 11.2 %collective-permute-start.11 = (bf16[256,256]{1,0:T(8,128)(2,1)}, bf16[256,256]{1,0:T(8,128)(2,1)S(1)}, u32[]{:S(2)}, u32[]{:S(2)}) collective-permute-start(bf16[256,256]{1,0:T(8,128)(2,1)} %get-tuple-element.78), channel_id=1, source_target_pairs={{0,8},{4,12},{8,0},{12,4},{16,24},{20,28},{24,16},{28,20},{32,40},... | collective-permute-start | bytes 393224 | tf_op jit(solution)/shard_map/ppermute | solution.py:49
  42.9 10.9 %collective-permute-start.12 = (bf16[256,256]{1,0:T(8,128)(2,1)S(1)}, bf16[256,256]{1,0:T(8,128)(2,1)S(1)}, u32[]{:S(2)}, u32[]{:S(2)}) collective-permute-start(bf16[256,256]{1,0:T(8,128)(2,1)S(1)} %get-tuple-element.79), channel_id=1, source_target_pairs={{0,4},{4,0},{8,12},{12,8},{16,20},{20,16},{24,28},{28,24},{32,36},... | collective-permute-start | bytes 393224 | tf_op jit(solution)/shard_map/ppermute | solution.py:49
  45.6 16.9 %all-to-all-start.1 = ((bf16[32,40,128]{2,1,0:T(8,128)(2,1)}), bf16[32,40,128]{2,1,0:T(8,128)(2,1)S(1)}, u32[]{:S(2)}, u32[]{:S(2)}) async-start(bf16[32,40,128]{2,1,0:T(8,128)(2,1)} %shard_map.136), calls=%async_computation.1 | async-start | bytes 655360 | tf_op jit(solution)/shard_map/all_to_all | solution.py:66
  54.9 10.4 %collective-permute-start.13 = (bf16[160,512]{1,0:T(8,128)(2,1)S(1)}, bf16[160,512]{1,0:T(8,128)(2,1)S(1)}, u32[]{:S(2)}, u32[]{:S(2)}) collective-permute-start(bf16[160,512]{1,0:T(8,128)(2,1)S(1)} %get-tuple-element.81), channel_id=1, source_target_pairs={{0,2},{1,3},{2,0},{3,1},{4,6},{5,7},{6,4},{7,5},{8,10},{9,11},{10,... | collective-permute-start | bytes 491528 | tf_op jit(solution)/shard_map/ppermute | solution.py:60
  57.9 7.4 %collective-permute-start.14 = (bf16[160,512]{1,0:T(8,128)(2,1)S(1)}, bf16[160,512]{1,0:T(8,128)(2,1)S(1)}, u32[]{:S(2)}, u32[]{:S(2)}) collective-permute-start(bf16[160,512]{1,0:T(8,128)(2,1)S(1)} %get-tuple-element.82), channel_id=1, source_target_pairs={{0,1},{1,0},{2,3},{3,2},{4,5},{5,4},{6,7},{7,6},{8,9},{9,8},{10,11... | collective-permute-start | bytes 491528 | tf_op jit(solution)/shard_map/ppermute | solution.py:60
  58.3 7.0 %collective-permute-start.15 = (bf16[160,512]{1,0:T(8,128)(2,1)S(1)}, bf16[160,512]{1,0:T(8,128)(2,1)S(1)}, u32[]{:S(2)}, u32[]{:S(2)}) collective-permute-start(bf16[160,512]{1,0:T(8,128)(2,1)S(1)} %get-tuple-element.83), channel_id=1, source_target_pairs={{0,3},{1,2},{2,1},{3,0},{4,7},{5,6},{6,5},{7,4},{8,11},{9,10},{10,... | collective-permute-start | bytes 491528 | tf_op jit(solution)/shard_map/ppermute | solution.py:60
  62.5 4.1 %collective-permute-start.8 = (bf16[32,40,128]{2,1,0:T(8,128)(2,1)S(1)}, bf16[32,40,128]{2,1,0:T(8,128)(2,1)S(1)}, u32[]{:S(2)}, u32[]{:S(2)}) collective-permute-start(bf16[32,40,128]{2,1,0:T(8,128)(2,1)S(1)} %all-to-all-done.1.mine), channel_id=1, source_target_pairs={{0,4},{4,0},{8,12},{12,8},{16,20},{20,16},{24,28},{28,24},{32,36},... | collective-permute-start | bytes 983048 | tf_op jit(solution)/shard_map/ppermute | solution.py:49

commit v7 on v6

--- a/solution.py
+++ b/solution.py
@@ -61,7 +61,7 @@
 
 
 def exchange(array):
-    chips = list(reversed(range(CHIPS)))
+    chips = [x * Z + z for x in (1, 2, 3, 0) for z in reversed(range(Z))]
     groups = [[CORES * chip + core for chip in chips] for core in range(CORES)]
     return lax.all_to_all(array, "dom", 0, 0, axis_index_groups=groups)
 

time: 68.1 us -> 66.6 us (0.978)
  starting transfers between devices: 40.6 us -> 39 us
    all_to_all x2, starting transfers between devices: 14.4 us -> 12.8 us  [exchange(): return lax.all_to_all(array, 'dom', 0, 0, axis_index_groups=groups)]
  transfers between devices with their start and end apart: 18 -> 18, of which waited for: 6 -> 7; matrix products, arithmetic and copies ran while one was open for 1% -> 1% of each run, Pallas kernels for 11% -> 11%
where the time goes in v7:
time: 66.6 us; the launch traced here: 66.2 us
  starting transfers between devices  39 us (59%)
  Pallas kernels  13 us (20%)
  waiting for transfers between devices  10.3 us (15%)
  local copies, waits for them, and re-layouts  2.26 us (3%)
  between operations  0.83 us (1%)
  other arithmetic  0.74 us (1%)
    all_to_all x2, starting transfers between devices, exchange(): return lax.all_to_all(array, 'dom', 0, 0, axis_index_groups=groups)  12.8 us
    ppermute x6, starting transfers between devices, dom_swap(): return lax.ppermute(array, 'dom', [(i, i ^ mask) for i in range(count)])  11.4 us
    ppermute x6, starting transfers between devices, hid_swap(): return lax.ppermute(array, 'hid', [(i, i ^ mask) for i in range(HID)])  7.47 us
    ppermute x4, starting transfers between devices, dom_pairs(): return lax.ppermute(array, 'dom', pairs + [(j, i) for i, j in pairs])  7.29 us
    all_to_all x2, waiting for transfers between devices, exchange(): return lax.all_to_all(array, 'dom', 0, 0, axis_index_groups=groups)  4.44 us
    ppermute x4, waiting for transfers between devices, dom_pairs(): return lax.ppermute(array, 'dom', pairs + [(j, i) for i, j in pairs])  4.24 us
    pallas_call x1, Pallas kernels, on_device(): call(before_kernel, [((n, n), BF16), ((n, slots), BF16), ((n, width), F32...  3.47 us
    pallas_call x1, Pallas kernels, on_device(): call(middle_kernel, [((n, hidden), BF16)] * 3 + [((n, width), BF16), ((wi...  2.28 us
  transfers between devices with their start and end apart: 18, of which 7 were waited for; matrix products, arithmetic and copies ran while one was open for 1% of the time, Pallas kernels for 11%

profile of v7, /device:TPU:1, one launch (start us, length us, event | category | flops | bytes accessed | tf_op | source)
XLA Modules:
  0.0 66.2 jit_solution(12480858761023405388)
XLA Ops:
  0.6 1.2 %shard_map.129 = (bf16[256,640]{1,0:T(8,128)(2,1)S(1)}, bf16[64,640]{1,0:T(8,128)(2,1)S(1)}, bf16[256,640]{1,0:T(8,128)(2,1)S(1)}, bf16[256,640]{1,0:T(8,128)(2,1)S(1)}, bf16[512,640]{1,0:T(8,128)(2,1)S(1)}) custom-call(s32[1,2,4]{2,1,0:T(2,128)} %bitcast.4, bf16[512,640]{1,0:T(8,128)(2,1)} %feats.1), custom_call_target="tpu_custom_call" | custom-call | bytes 2000000 | tf_op jit(solution)/shard_map/pallas_call | solution.py:364
  1.8 3.1 %collective-permute-start = (bf16[64,640]{1,0:T(8,128)(2,1)S(1)}, bf16[64,640]{1,0:T(8,128)(2,1)S(1)}, u32[]{:S(2)}, u32[]{:S(2)}) collective-permute-start(bf16[64,640]{1,0:T(8,128)(2,1)S(1)} %get-tuple-element.45), channel_id=1, source_target_pairs={{4,8},{12,16},{20,24},{28,32},{36,40},{44,48},{52,56},{60,64},{68,... | collective-permute-start | bytes 245768 | tf_op jit(solution)/shard_map/ppermute | solution.py:56
  4.9 6.0 %collective-permute-start.1 = (bf16[256,640]{1,0:T(8,128)(2,1)S(1)}, bf16[256,640]{1,0:T(8,128)(2,1)S(1)}, u32[]{:S(2)}, u32[]{:S(2)}) collective-permute-start(bf16[256,640]{1,0:T(8,128)(2,1)S(1)} %get-tuple-element.46), channel_id=1, source_target_pairs={{0,4},{4,0},{8,12},{12,8},{16,20},{20,16},{24,28},{28,24},{32,36},... | collective-permute-start | bytes 983048 | tf_op jit(solution)/shard_map/ppermute | solution.py:49
  10.9 0.7 %collective-permute-start.2 = (bf16[256,640]{1,0:T(8,128)(2,1)S(1)}, bf16[256,640]{1,0:T(8,128)(2,1)S(1)}, u32[]{:S(2)}, u32[]{:S(2)}) collective-permute-start(bf16[256,640]{1,0:T(8,128)(2,1)S(1)} %get-tuple-element.49), channel_id=1, source_target_pairs={{8,16},{12,20},{24,32},{28,36},{40,48},{44,52},{56,64},{60,68},{72... | collective-permute-start | bytes 983048 | tf_op jit(solution)/shard_map/ppermute | solution.py:56
  12.2 2.9 %collective-permute-start.6 = (bf16[64,640]{1,0:T(8,128)(2,1)S(1)}, bf16[64,640]{1,0:T(8,128)(2,1)S(1)}, u32[]{:S(2)}, u32[]{:S(2)}) collective-permute-start(bf16[64,640]{1,0:T(8,128)(2,1)S(1)} %collective-permute-done.share0), channel_id=1, source_target_pairs={{0,2},{1,3},{2,0},{3,1},{4,6},{5,7},{6,4},{7,5},{8,10},{9,11},{10,... | collective-permute-start | bytes 245768 | tf_op jit(solution)/shard_map/ppermute | solution.py:60
  15.1 0.4 collective-permute-start.5
  15.5 0.4 collective-permute-start.4
  15.9 3.5 %shard_map.131 = (bf16[512,512]{1,0:T(8,128)(2,1)S(1)}, bf16[512,1024]{1,0:T(8,128)(2,1)S(1)}, f32[512,640]{1,0:T(8,128)S(1)}, f32[512,128]{1,0:T(8,128)S(1)}, f32[512,256]{1,0:T(8,128)S(1)}) custom-call(s32[1,4,8]{2,1,0:T(4,128)} %neighbors.1, s32[1,2,4]{2,1,0:T(2,128)} %bitcast.6, s32[1,4]{1,0:T(1,128)} %live.1, bf16[640,256]{1,0:T(8,128)(2,1)} %self_w.3, ...), custom_call_target="tpu_custom_call" | custom-call | flops 60000002048 | bytes 6000000 | tf_op jit(solution)/shard_map/pallas_call | solution.py:378
  19.3 4.2 %collective-permute-done.2.got0 = bf16[256,640]{1,0:T(8,128)(2,1)S(1)} collective-permute-done((bf16[256,640]{1,0:T(8,128)(2,1)S(1)}, bf16[256,640]{1,0:T(8,128)(2,1)S(1)}, u32[]{:S(2)}, u32[]{:S(2)}) %collective-permute-start.2) | collective-permute-done | bytes 327712 | tf_op jit(solution)/shard_map/ppermute | solution.py:56
  23.6 2.3 %shard_map.132 = (bf16[512,256]{1,0:T(8,128)(2,1)S(1)}, bf16[512,256]{1,0:T(8,128)(2,1)S(1)}, bf16[512,256]{1,0:T(8,128)(2,1)S(1)}, bf16[512,640]{1,0:T(8,128)(2,1)S(1)}, bf16[640,256]{1,0:T(8,128)(2,1)S(1)}) custom-call(bf16[512,1024]{1,0:T(8,128)(2,1)S(1)} %get-tuple-element.48.edge, bf16[256,640]{1,0:T(8,128)(2,1)S(1)} %collective-permute-done.2.got0, ...), custom_call_target="tpu_custom_call" | custom-call | flops 1600000000 | bytes 8000000 | tf_op jit(solution)/shard_map/pallas_call | solution.py:409
  25.9 0.9 %collective-permute-start.7 = (bf16[640,256]{1,0:T(8,128)(2,1)S(1)}, bf16[640,256]{1,0:T(8,128)(2,1)S(1)}, u32[]{:S(2)}, u32[]{:S(2)}) collective-permute-start(bf16[640,256]{1,0:T(8,128)(2,1)S(1)} %get-tuple-element.56), channel_id=1, source_target_pairs={{0,4},{4,0},{8,12},{12,8},{16,20},{20,16},{24,28},{28,24},{32,36},... | collective-permute-start | bytes 983048 | tf_op jit(solution)/shard_map/ppermute | solution.py:49
  27.2 0.9 %collective-permute-done.7.got = bf16[640,256]{1,0:T(8,128)(2,1)S(1)} collective-permute-done((bf16[640,256]{1,0:T(8,128)(2,1)S(1)}, bf16[640,256]{1,0:T(8,128)(2,1)S(1)}, u32[]{:S(2)}, u32[]{:S(2)}) %collective-permute-start.7) | collective-permute-done | bytes 327712 | tf_op jit(solution)/shard_map/ppermute | solution.py:49
  28.1 0.8 %shard_map.134 = bf16[32,40,128]{2,1,0:T(8,128)(2,1)} custom-call(f32[640,256]{1,0:T(8,128)S(1)} %shard_map.133.keep, bf16[640,256]{1,0:T(8,128)(2,1)S(1)} %collective-permute-done.7.got), custom_call_target="tpu_custom_call" | custom-call | bytes 1500000 | tf_op jit(solution)/shard_map/pallas_call | solution.py:425
  28.9 5.1 %all-to-all-start = ((bf16[32,40,128]{2,1,0:T(8,128)(2,1)}), bf16[32,40,128]{2,1,0:T(8,128)(2,1)S(1)}, u32[]{:S(2)}, u32[]{:S(2)}) async-start(bf16[32,40,128]{2,1,0:T(8,128)(2,1)} %shard_map.134), calls=%async_computation | async-start | bytes 655360 | tf_op jit(solution)/shard_map/all_to_all | solution.py:66
  34.0 1.7 %shard_map.135 = (bf16[256,256]{1,0:T(8,128)(2,1)}, bf16[256,256]{1,0:T(8,128)(2,1)}, bf16[256,256]{1,0:T(8,128)(2,1)}, bf16[256,256]{1,0:T(8,128)(2,1)S(1)}, bf...) custom-call(s32[1,2,4]{2,1,0:T(2,128)} %bitcast.5, ...), custom_call_target="tpu_custom_call" | custom-call | flops 600000000 | bytes 3000000 | tf_op jit(solution)/shard_map/pallas_call | solution.py:427
  35.7 0.8 %copy-done.2 = f32[512,256]{1,0:T(8,128)} copy-done((f32[512,256]{1,0:T(8,128)}, f32[512,256]{1,0:T(8,128)S(1)}, u32[]{:S(2)}) %copy-start.2) | copy-done | bytes 524312
  36.4 0.7 %copy-done.4 = bf16[640,256]{1,0:T(8,128)(2,1)} copy-done((bf16[640,256]{1,0:T(8,128)(2,1)}, bf16[640,256]{1,0:T(8,128)(2,1)S(1)}, u32[]{:S(2)}) %copy-start.4) | copy-done | bytes 327704
  37.2 0.7 %copy-done.6 = bf16[640,256]{1,0:T(8,128)(2,1)} copy-done((bf16[640,256]{1,0:T(8,128)(2,1)}, bf16[640,256]{1,0:T(8,128)(2,1)S(1)}, u32[]{:S(2)}) %copy-start.6) | copy-done | bytes 327704
  37.9 2.3 %collective-permute-start.9 = (bf16[256,256]{1,0:T(8,128)(2,1)}, bf16[256,256]{1,0:T(8,128)(2,1)S(1)}, u32[]{:S(2)}, u32[]{:S(2)}) collective-permute-start(bf16[256,256]{1,0:T(8,128)(2,1)} %get-tuple-element.76), channel_id=1, source_target_pairs={{8,16},{12,20},{24,32},{28,36},{40,48},{44,52},{56,64},{60,68},{72... | collective-permute-start | bytes 393224 | tf_op jit(solution)/shard_map/ppermute | solution.py:56
  40.2 1.1 %collective-permute-start.10 = (bf16[256,256]{1,0:T(8,128)(2,1)}, bf16[256,256]{1,0:T(8,128)(2,1)S(1)}, u32[]{:S(2)}, u32[]{:S(2)}) collective-permute-start(bf16[256,256]{1,0:T(8,128)(2,1)} %get-tuple-element.77), channel_id=1, source_target_pairs={{4,8},{12,16},{20,24},{28,32},{36,40},{44,48},{52,56},{60,64},{68,... | collective-permute-start | bytes 393224 | tf_op jit(solution)/shard_map/ppermute | solution.py:56
  41.6 1.4 %collective-permute-start.12 = (bf16[256,256]{1,0:T(8,128)(2,1)S(1)}, bf16[256,256]{1,0:T(8,128)(2,1)S(1)}, u32[]{:S(2)}, u32[]{:S(2)}) collective-permute-start(bf16[256,256]{1,0:T(8,128)(2,1)S(1)} %get-tuple-element.79), channel_id=1, source_target_pairs={{0,4},{4,0},{8,12},{12,8},{16,20},{20,16},{24,28},{28,24},{32,36},... | collective-permute-start | bytes 393224 | tf_op jit(solution)/shard_map/ppermute | solution.py:49
  43.1 0.6 all-to-all-done.got
  43.6 0.8 %shard_map.136 = bf16[32,40,128]{2,1,0:T(8,128)(2,1)} custom-call(bf16[32,40,128]{2,1,0:T(8,128)(2,1)S(1)} %all-to-all-done.got), custom_call_target="tpu_custom_call" | custom-call | bytes 700000 | tf_op jit(solution)/shard_map/pallas_call | solution.py:439
  44.4 7.7 %all-to-all-start.1 = ((bf16[32,40,128]{2,1,0:T(8,128)(2,1)}), bf16[32,40,128]{2,1,0:T(8,128)(2,1)S(1)}, u32[]{:S(2)}, u32[]{:S(2)}) async-start(bf16[32,40,128]{2,1,0:T(8,128)(2,1)} %shard_map.136), calls=%async_computation.1 | async-start | bytes 655360 | tf_op jit(solution)/shard_map/all_to_all | solution.py:66
  52.2 1.1 %shard_map.138 = (f32[160,512]{1,0:T(8,128)S(1)}, bf16[160,512]{1,0:T(8,128)(2,1)S(1)}, bf16[160,512]{1,0:T(8,128)(2,1)S(1)}, bf16[160,512]{1,0:T(8,128)(2,1)S(1)}) custom-call(f32[32,128]{1,0:T(8,128)S(1)} %get-tuple-element.71.place, f32[512,256]{1,0:T(8,128)S(1)} %copy-done.3, bf16[512,256]{1,0:T(8,128)(2,1)S(1)} %get-tuple-element.73.low, ...), custom_call_target="tpu_custom_call" | custom-call | flops 60000002048 | bytes 3000000 | tf_op jit(solution)/shard_map/pallas_call | solution.py:442
  53.3 3.0 %collective-permute-start.13 = (bf16[160,512]{1,0:T(8,128)(2,1)S(1)}, bf16[160,512]{1,0:T(8,128)(2,1)S(1)}, u32[]{:S(2)}, u32[]{:S(2)}) collective-permute-start(bf16[160,512]{1,0:T(8,128)(2,1)S(1)} %get-tuple-element.81), channel_id=1, source_target_pairs={{0,2},{1,3},{2,0},{3,1},{4,6},{5,7},{6,4},{7,5},{8,10},{9,11},{10,... | collective-permute-start | bytes 491528 | tf_op jit(solution)/shard_map/ppermute | solution.py:60
  56.3 0.4 collective-permute-start.14
  56.7 0.4 collective-permute-start.15
  57.1 3.9 %all-to-all-done.1.mine = bf16[32,40,128]{2,1,0:T(8,128)(2,1)S(1)} async-done(((bf16[32,40,128]{2,1,0:T(8,128)(2,1)}), bf16[32,40,128]{2,1,0:T(8,128)(2,1)S(1)}, u32[]{:S(2)}, u32[]{:S(2)}) %all-to-all-start.1) | async-done | bytes 327712 | tf_op jit(solution)/shard_map/all_to_all | solution.py:66
  61.0 2.7 %collective-permute-start.8 = (bf16[32,40,128]{2,1,0:T(8,128)(2,1)S(1)}, bf16[32,40,128]{2,1,0:T(8,128)(2,1)S(1)}, u32[]{:S(2)}, u32[]{:S(2)}) collective-permute-start(bf16[32,40,128]{2,1,0:T(8,128)(2,1)S(1)} %all-to-all-done.1.mine), channel_id=1, source_target_pairs={{0,4},{4,0},{8,12},{12,8},{16,20},{20,16},{24,28},{28,24},{32,36},... | collective-permute-start | bytes 983048 | tf_op jit(solution)/shard_map/ppermute | solution.py:49
  64.0 0.7 %fusion = bf16[512,160]{0,1:T(8,128)(2,1)} fusion(bf16[160,512]{1,0:T(8,128)(2,1)S(1)} %collective-permute-done.15, bf16[160,512]{1,0:T(8,128)(2,1)S(1)} %collective-permute-done.14, f32[160,512]{1,0:T(8,128)S(1)} %get-tuple-element.80, bf16[160,512]{1,0:T(8,128)(2,1)S(1)} %collective-permute-done.13), kind=kLoop, calls=%fused_computation.1 | loop fusion | flops 573440 | bytes 983040 | tf_op jit(solution)/shard_map/transpose | solution.py:462
  65.0 1.2 %shard_map.137 = (f32[640,256]{1,0:T(8,128)}, f32[640,256]{1,0:T(8,128)}) custom-call(bf16[32,40,128]{2,1,0:T(8,128)(2,1)S(1)} %all-to-all-done.1.mine, bf16[32,40,128]{2,1,0:T(8,128)(2,1)S(1)} %collective-permute-done.8.other), custom_call_target="tpu_custom_call" | custom-call | bytes 2000000 | tf_op jit(solution)/shard_map/pallas_call | solution.py:453
  (33 shorter events, 1.7 us)
Async XLA Ops:
  1.8 10.0 %collective-permute-start = (bf16[64,640]{1,0:T(8,128)(2,1)S(1)}, bf16[64,640]{1,0:T(8,128)(2,1)S(1)}, u32[]{:S(2)}, u32[]{:S(2)}) collective-permute-start(bf16[64,640]{1,0:T(8,128)(2,1)S(1)} %get-tuple-element.45), channel_id=1, source_target_pairs={{4,8},{12,16},{20,24},{28,32},{36,40},{44,48},{52,56},{60,64},{68,... | collective-permute-start | bytes 245768 | tf_op jit(solution)/shard_map/ppermute | solution.py:56
  4.9 7.2 %collective-permute-start.1 = (bf16[256,640]{1,0:T(8,128)(2,1)S(1)}, bf16[256,640]{1,0:T(8,128)(2,1)S(1)}, u32[]{:S(2)}, u32[]{:S(2)}) collective-permute-start(bf16[256,640]{1,0:T(8,128)(2,1)S(1)} %get-tuple-element.46), channel_id=1, source_target_pairs={{0,4},{4,0},{8,12},{12,8},{16,20},{20,16},{24,28},{28,24},{32,36},... | collective-permute-start | bytes 983048 | tf_op jit(solution)/shard_map/ppermute | solution.py:49
  10.9 12.7 %collective-permute-start.2 = (bf16[256,640]{1,0:T(8,128)(2,1)S(1)}, bf16[256,640]{1,0:T(8,128)(2,1)S(1)}, u32[]{:S(2)}, u32[]{:S(2)}) collective-permute-start(bf16[256,640]{1,0:T(8,128)(2,1)S(1)} %get-tuple-element.49), channel_id=1, source_target_pairs={{8,16},{12,20},{24,32},{28,36},{40,48},{44,52},{56,64},{60,68},{72... | collective-permute-start | bytes 983048 | tf_op jit(solution)/shard_map/ppermute | solution.py:56
  11.6 11.9 %collective-permute-start.3 = (bf16[256,640]{1,0:T(8,128)(2,1)S(1)}, bf16[256,640]{1,0:T(8,128)(2,1)S(1)}, u32[]{:S(2)}, u32[]{:S(2)}) collective-permute-start(bf16[256,640]{1,0:T(8,128)(2,1)S(1)} %get-tuple-element.50), channel_id=1, source_target_pairs={{0,8},{4,12},{8,0},{12,4},{16,24},{20,28},{24,16},{28,20},{32,40},... | collective-permute-start | bytes 983048 | tf_op jit(solution)/shard_map/ppermute | solution.py:49
  12.2 11.4 %collective-permute-start.6 = (bf16[64,640]{1,0:T(8,128)(2,1)S(1)}, bf16[64,640]{1,0:T(8,128)(2,1)S(1)}, u32[]{:S(2)}, u32[]{:S(2)}) collective-permute-start(bf16[64,640]{1,0:T(8,128)(2,1)S(1)} %collective-permute-done.share0), channel_id=1, source_target_pairs={{0,2},{1,3},{2,0},{3,1},{4,6},{5,7},{6,4},{7,5},{8,10},{9,11},{10,... | collective-permute-start | bytes 245768 | tf_op jit(solution)/shard_map/ppermute | solution.py:60
  15.1 8.5 %collective-permute-start.5 = (bf16[64,640]{1,0:T(8,128)(2,1)S(1)}, bf16[64,640]{1,0:T(8,128)(2,1)S(1)}, u32[]{:S(2)}, u32[]{:S(2)}) collective-permute-start(bf16[64,640]{1,0:T(8,128)(2,1)S(1)} %collective-permute-done.share0), channel_id=1, source_target_pairs={{0,1},{1,0},{2,3},{3,2},{4,5},{5,4},{6,7},{7,6},{8,9},{9,8},{10,11... | collective-permute-start | bytes 245768 | tf_op jit(solution)/shard_map/ppermute | solution.py:60
  15.5 8.1 %collective-permute-start.4 = (bf16[64,640]{1,0:T(8,128)(2,1)S(1)}, bf16[64,640]{1,0:T(8,128)(2,1)S(1)}, u32[]{:S(2)}, u32[]{:S(2)}) collective-permute-start(bf16[64,640]{1,0:T(8,128)(2,1)S(1)} %collective-permute-done.share0), channel_id=1, source_target_pairs={{0,3},{1,2},{2,1},{3,0},{4,7},{5,6},{6,5},{7,4},{8,11},{9,10},{10,... | collective-permute-start | bytes 245768 | tf_op jit(solution)/shard_map/ppermute | solution.py:60
  15.9 7.7 %copy-start.1 = (bf16[640,256]{1,0:T(8,128)(2,1)S(1)}, bf16[640,256]{1,0:T(8,128)(2,1)}, u32[]{:S(2)}) copy-start(bf16[640,256]{1,0:T(8,128)(2,1)} %neigh_w.3) | copy-start | bytes 983044
  15.9 7.7 %copy-start.8 = (bf16[512,256]{1,0:T(8,128)(2,1)S(1)}, bf16[512,256]{1,0:T(8,128)(2,1)}, u32[]{:S(2)}) copy-start(bf16[512,256]{1,0:T(8,128)(2,1)} %cot.1) | copy-start | bytes 786436
  25.9 2.2 %collective-permute-start.7 = (bf16[640,256]{1,0:T(8,128)(2,1)S(1)}, bf16[640,256]{1,0:T(8,128)(2,1)S(1)}, u32[]{:S(2)}, u32[]{:S(2)}) collective-permute-start(bf16[640,256]{1,0:T(8,128)(2,1)S(1)} %get-tuple-element.56), channel_id=1, source_target_pairs={{0,4},{4,0},{8,12},{12,8},{16,20},{20,16},{24,28},{28,24},{32,36},... | collective-permute-start | bytes 983048 | tf_op jit(solution)/shard_map/ppermute | solution.py:49
  27.2 6.8 %copy-start = (bf16[640,256]{1,0:T(8,128)(2,1)S(1)}, bf16[640,256]{1,0:T(8,128)(2,1)}, u32[]{:S(2)}) copy-start(bf16[640,256]{1,0:T(8,128)(2,1)} %self_w.3) | copy-start | bytes 983044
  28.9 14.8 %all-to-all-start = ((bf16[32,40,128]{2,1,0:T(8,128)(2,1)}), bf16[32,40,128]{2,1,0:T(8,128)(2,1)S(1)}, u32[]{:S(2)}, u32[]{:S(2)}) async-start(bf16[32,40,128]{2,1,0:T(8,128)(2,1)} %shard_map.134), calls=%async_computation | async-start | bytes 655360 | tf_op jit(solution)/shard_map/all_to_all | solution.py:66
  35.6 0.8 %copy-start.2 = (f32[512,256]{1,0:T(8,128)}, f32[512,256]{1,0:T(8,128)S(1)}, u32[]{:S(2)}) copy-start(f32[512,256]{1,0:T(8,128)S(1)} %get-tuple-element.72.start) | copy-start | bytes 1572868
  36.4 0.7 %copy-start.4 = (bf16[640,256]{1,0:T(8,128)(2,1)}, bf16[640,256]{1,0:T(8,128)(2,1)S(1)}, u32[]{:S(2)}) copy-start(bf16[640,256]{1,0:T(8,128)(2,1)S(1)} %get-tuple-element.74.self_w) | copy-start | bytes 983044
  37.2 0.7 %copy-start.6 = (bf16[640,256]{1,0:T(8,128)(2,1)}, bf16[640,256]{1,0:T(8,128)(2,1)S(1)}, u32[]{:S(2)}) copy-start(bf16[640,256]{1,0:T(8,128)(2,1)S(1)} %get-tuple-element.75.neigh_w) | copy-start | bytes 983044
  37.9 14.3 %copy-start.3 = (f32[512,256]{1,0:T(8,128)S(1)}, f32[512,256]{1,0:T(8,128)}, u32[]{:S(2)}) copy-start(f32[512,256]{1,0:T(8,128)} %copy-done.2) | copy-start | bytes 1572868
  37.9 14.3 %copy-start.5 = (bf16[640,256]{1,0:T(8,128)(2,1)S(1)}, bf16[640,256]{1,0:T(8,128)(2,1)}, u32[]{:S(2)}) copy-start(bf16[640,256]{1,0:T(8,128)(2,1)} %copy-done.4) | copy-start | bytes 983044
  37.9 14.3 %copy-start.7 = (bf16[640,256]{1,0:T(8,128)(2,1)S(1)}, bf16[640,256]{1,0:T(8,128)(2,1)}, u32[]{:S(2)}) copy-start(bf16[640,256]{1,0:T(8,128)(2,1)} %copy-done.6) | copy-start | bytes 983044
  37.9 14.3 %collective-permute-start.9 = (bf16[256,256]{1,0:T(8,128)(2,1)}, bf16[256,256]{1,0:T(8,128)(2,1)S(1)}, u32[]{:S(2)}, u32[]{:S(2)}) collective-permute-start(bf16[256,256]{1,0:T(8,128)(2,1)} %get-tuple-element.76), channel_id=1, source_target_pairs={{8,16},{12,20},{24,32},{28,36},{40,48},{44,52},{56,64},{60,68},{72... | collective-permute-start | bytes 393224 | tf_op jit(solution)/shard_map/ppermute | solution.py:56
  40.2 12.0 %collective-permute-start.10 = (bf16[256,256]{1,0:T(8,128)(2,1)}, bf16[256,256]{1,0:T(8,128)(2,1)S(1)}, u32[]{:S(2)}, u32[]{:S(2)}) collective-permute-start(bf16[256,256]{1,0:T(8,128)(2,1)} %get-tuple-element.77), channel_id=1, source_target_pairs={{4,8},{12,16},{20,24},{28,32},{36,40},{44,48},{52,56},{60,64},{68,... | collective-permute-start | bytes 393224 | tf_op jit(solution)/shard_map/ppermute | solution.py:56
  41.3 10.9 %collective-permute-start.11 = (bf16[256,256]{1,0:T(8,128)(2,1)}, bf16[256,256]{1,0:T(8,128)(2,1)S(1)}, u32[]{:S(2)}, u32[]{:S(2)}) collective-permute-start(bf16[256,256]{1,0:T(8,128)(2,1)} %get-tuple-element.78), channel_id=1, source_target_pairs={{0,8},{4,12},{8,0},{12,4},{16,24},{20,28},{24,16},{28,20},{32,40},... | collective-permute-start | bytes 393224 | tf_op jit(solution)/shard_map/ppermute | solution.py:49
  41.6 10.6 %collective-permute-start.12 = (bf16[256,256]{1,0:T(8,128)(2,1)S(1)}, bf16[256,256]{1,0:T(8,128)(2,1)S(1)}, u32[]{:S(2)}, u32[]{:S(2)}) collective-permute-start(bf16[256,256]{1,0:T(8,128)(2,1)S(1)} %get-tuple-element.79), channel_id=1, source_target_pairs={{0,4},{4,0},{8,12},{12,8},{16,20},{20,16},{24,28},{28,24},{32,36},... | collective-permute-start | bytes 393224 | tf_op jit(solution)/shard_map/ppermute | solution.py:49
  44.4 16.6 %all-to-all-start.1 = ((bf16[32,40,128]{2,1,0:T(8,128)(2,1)}), bf16[32,40,128]{2,1,0:T(8,128)(2,1)S(1)}, u32[]{:S(2)}, u32[]{:S(2)}) async-start(bf16[32,40,128]{2,1,0:T(8,128)(2,1)} %shard_map.136), calls=%async_computation.1 | async-start | bytes 655360 | tf_op jit(solution)/shard_map/all_to_all | solution.py:66
  53.3 10.4 %collective-permute-start.13 = (bf16[160,512]{1,0:T(8,128)(2,1)S(1)}, bf16[160,512]{1,0:T(8,128)(2,1)S(1)}, u32[]{:S(2)}, u32[]{:S(2)}) collective-permute-start(bf16[160,512]{1,0:T(8,128)(2,1)S(1)} %get-tuple-element.81), channel_id=1, source_target_pairs={{0,2},{1,3},{2,0},{3,1},{4,6},{5,7},{6,4},{7,5},{8,10},{9,11},{10,... | collective-permute-start | bytes 491528 | tf_op jit(solution)/shard_map/ppermute | solution.py:60
  56.3 7.4 %collective-permute-start.14 = (bf16[160,512]{1,0:T(8,128)(2,1)S(1)}, bf16[160,512]{1,0:T(8,128)(2,1)S(1)}, u32[]{:S(2)}, u32[]{:S(2)}) collective-permute-start(bf16[160,512]{1,0:T(8,128)(2,1)S(1)} %get-tuple-element.82), channel_id=1, source_target_pairs={{0,1},{1,0},{2,3},{3,2},{4,5},{5,4},{6,7},{7,6},{8,9},{9,8},{10,11... | collective-permute-start | bytes 491528 | tf_op jit(solution)/shard_map/ppermute | solution.py:60
  56.7 7.2 %collective-permute-start.15 = (bf16[160,512]{1,0:T(8,128)(2,1)S(1)}, bf16[160,512]{1,0:T(8,128)(2,1)S(1)}, u32[]{:S(2)}, u32[]{:S(2)}) collective-permute-start(bf16[160,512]{1,0:T(8,128)(2,1)S(1)} %get-tuple-element.83), channel_id=1, source_target_pairs={{0,3},{1,2},{2,1},{3,0},{4,7},{5,6},{6,5},{7,4},{8,11},{9,10},{10,... | collective-permute-start | bytes 491528 | tf_op jit(solution)/shard_map/ppermute | solution.py:60
  61.0 4.0 %collective-permute-start.8 = (bf16[32,40,128]{2,1,0:T(8,128)(2,1)S(1)}, bf16[32,40,128]{2,1,0:T(8,128)(2,1)S(1)}, u32[]{:S(2)}, u32[]{:S(2)}) collective-permute-start(bf16[32,40,128]{2,1,0:T(8,128)(2,1)S(1)} %all-to-all-done.1.mine), channel_id=1, source_target_pairs={{0,4},{4,0},{8,12},{12,8},{16,20},{20,16},{24,28},{28,24},{32,36},... | collective-permute-start | bytes 983048 | tf_op jit(solution)/shard_map/ppermute | solution.py:49

commit v8 on v7

--- a/solution.py
+++ b/solution.py
@@ -19,6 +19,7 @@
 HID = 4
 CHIPS = X * Z
 PIECE = (40, 128)
+GROUPS = 4
 COVER_FLOPS = 60_000_000_000
 BF16 = jnp.bfloat16
 F32 = jnp.float32
@@ -32,12 +33,12 @@
     return lax.dot_general(a, b, (dims, ((), ())), preferred_element_type=F32)
 
 
-def call(kernel, outs, specs, flops=0, nbytes=0, limit=12, scratch=()):
+def call(kernel, outs, specs, flops=0, nbytes=0, limit=12, scratch=(), out_specs=None):
     return pl.pallas_call(
         kernel,
         out_shape=[jax.ShapeDtypeStruct(shape, dtype) for shape, dtype in outs],
         in_specs=specs,
-        out_specs=[VMEM] * len(outs),
+        out_specs=out_specs or [VMEM] * len(outs),
         scratch_shapes=list(scratch),
         compiler_params=pltpu.CompilerParams(vmem_limit_bytes=limit * 1024 * 1024),
         cost_estimate=pl.CostEstimate(flops=flops, bytes_accessed=nbytes, transcendentals=0),
@@ -244,17 +245,45 @@
     return (i % 16) * PIECE[0], (i // 16) * PIECE[1]
 
 
-def cut_kernel(keep, got, out):
+def cut_kernel(keep, got, out, buffer, sems):
     total = keep[...] + got[...].astype(F32)
-    for i in range(CHIPS):
-        at, lane = piece_at(i)
-        out[i] = total[at : at + PIECE[0], lane : lane + PIECE[1]].astype(BF16)
-
-
-def sum_kernel(got, out):
-    done = jnp.sum(got[...].astype(F32), axis=0).astype(BF16)
-    for i in range(CHIPS):
-        out[i] = done
+    copies = []
+    span = CHIPS // GROUPS
+    for group in range(GROUPS):
+        for i in range(group * span, (group + 1) * span):
+            at, lane = piece_at(i)
+            buffer[i] = total[at : at + PIECE[0], lane : lane + PIECE[1]].astype(BF16)
+        here = pl.ds(group * span, span)
+        copies.append(pltpu.make_async_copy(buffer.at[here], out.at[here], sems.at[group]))
+        copies[-1].start()
+    for copy in copies:
+        copy.wait()
+
+
+def sum_kernel(got, out, got_now, buffer, sems):
+    span = CHIPS // GROUPS
+    parts = [pl.ds(group * span, span) for group in range(GROUPS)]
+    copies = [
+        pltpu.make_async_copy(got.at[part], got_now.at[part], sems.at[group])
+        for group, part in enumerate(parts)
+    ]
+    for copy in copies:
+        copy.start()
+    total = jnp.zeros(PIECE, F32)
+    for part, copy in zip(parts, copies):
+        copy.wait()
+        total = total + jnp.sum(got_now[part].astype(F32), axis=0)
+    done = total.astype(BF16)
+    for i in range(span):
+        buffer[i] = done
+    copies = [
+        pltpu.make_async_copy(buffer, out.at[part], sems.at[GROUPS + group])
+        for group, part in enumerate(parts)
+    ]
+    for copy in copies:
+        copy.start()
+    for copy in copies:
+        copy.wait()
 
 
 def last_kernel(scale, mine, other, of_self, of_neigh):
@@ -422,7 +451,14 @@
     )(turned, mean, low)
     got, keep = lax.optimization_barrier((got, keep))
     pieces = (CHIPS,) + PIECE
-    (cut,) = call(cut_kernel, [(pieces, BF16)], [VMEM] * 2, nbytes=1_500_000)(keep, got)
+    (cut,) = call(
+        cut_kernel,
+        [(pieces, BF16)],
+        [VMEM] * 2,
+        nbytes=1_500_000,
+        scratch=[pltpu.VMEM(pieces, BF16), DMA((GROUPS,))],
+        out_specs=[HBM],
+    )(keep, got)
     cut, spread, low = lax.optimization_barrier((cut, spread, low))
     *terms, activated, back, self_now, neigh_now, place = call(
         back_own_kernel,
@@ -436,7 +472,18 @@
         scratch=[pltpu.SMEM((1, NB, ROUNDS), jnp.int32), DMA((1,))],
     )(in_hbm(send_blocks), edge, spread, act, local, self_weight, neigh_weight)
     returned = swaps(terms)
-    (summed,) = call(sum_kernel, [(pieces, BF16)], [VMEM], nbytes=700_000)(exchange(cut))
+    (summed,) = call(
+        sum_kernel,
+        [(pieces, BF16)],
+        [HBM],
+        nbytes=700_000,
+        scratch=[
+            pltpu.VMEM(pieces, BF16),
+            pltpu.VMEM((CHIPS // GROUPS,) + PIECE, BF16),
+            DMA((2 * GROUPS,)),
+        ],
+        out_specs=[HBM],
+    )(in_hbm(exchange(cut)))
     summed, back = lax.optimization_barrier((summed, back))
     shape = (width // HID, n)
     in_own, in_far, in_first, in_third = call(

time: 66.6 us -> 67.9 us (1.020)
  Pallas kernels: 13 us -> 14.1 us
  waiting for transfers between devices: 10.3 us -> 11.2 us
  local copies, waits for them, and re-layouts: 2.26 us -> 1.46 us
    pallas_call x2, Pallas kernels: 1.58 us -> 2.58 us  [the longest x1 1.81 us: on_device(): call(sum_kernel, [(pieces, BF16)], [HBM], nbytes=700000, scratch=[pltpu.V...]
    all_to_all x2, waiting for transfers between devices: 4.44 us -> 5.32 us  [exchange(): return lax.all_to_all(array, 'dom', 0, 0, axis_index_groups=groups)]
    unnamed x18 -> x14, local copies, waits for them, and re-layouts: 2.26 us -> 1.46 us
  transfers between devices with their start and end apart: 18 -> 18, of which waited for: 7 -> 7; matrix products, arithmetic and copies ran while one was open for 1% -> 1% of each run, Pallas kernels for 11% -> 13%
where the time goes in v8:
time: 67.9 us; the launch traced here: 67.6 us
  starting transfers between devices  39.3 us (58%)
  Pallas kernels  14.1 us (21%)
  waiting for transfers between devices  11.2 us (16%)
  local copies, waits for them, and re-layouts  1.46 us (2%)
  between operations  0.83 us (1%)
  other arithmetic  0.74 us (1%)
    all_to_all x2, starting transfers between devices, exchange(): return lax.all_to_all(array, 'dom', 0, 0, axis_index_groups=groups)  13.2 us
    ppermute x6, starting transfers between devices, dom_swap(): return lax.ppermute(array, 'dom', [(i, i ^ mask) for i in range(count)])  11.3 us
    ppermute x6, starting transfers between devices, hid_swap(): return lax.ppermute(array, 'hid', [(i, i ^ mask) for i in range(HID)])  7.47 us
    ppermute x4, starting transfers between devices, dom_pairs(): return lax.ppermute(array, 'dom', pairs + [(j, i) for i, j in pairs])  7.29 us
    all_to_all x2, waiting for transfers between devices, exchange(): return lax.all_to_all(array, 'dom', 0, 0, axis_index_groups=groups)  5.32 us
    ppermute x4, waiting for transfers between devices, dom_pairs(): return lax.ppermute(array, 'dom', pairs + [(j, i) for i, j in pairs])  4.22 us
    pallas_call x1, Pallas kernels, on_device(): call(before_kernel, [((n, n), BF16), ((n, slots), BF16), ((n, width), F32...  3.49 us
    pallas_call x1, Pallas kernels, on_device(): call(middle_kernel, [((n, hidden), BF16)] * 3 + [((n, width), BF16), ((wi...  2.28 us
  transfers between devices with their start and end apart: 18, of which 7 were waited for; matrix products, arithmetic and copies ran while one was open for 1% of the time, Pallas kernels for 13%

profile of v8, /device:TPU:1, one launch (start us, length us, event | category | flops | bytes accessed | tf_op | source)
XLA Modules:
  0.0 67.6 jit_solution(11332621823111079920)
XLA Ops:
  0.6 1.2 %shard_map.129 = (bf16[256,640]{1,0:T(8,128)(2,1)S(1)}, bf16[64,640]{1,0:T(8,128)(2,1)S(1)}, bf16[256,640]{1,0:T(8,128)(2,1)S(1)}, bf16[256,640]{1,0:T(8,128)(2,1)S(1)}, bf16[512,640]{1,0:T(8,128)(2,1)S(1)}) custom-call(s32[1,2,4]{2,1,0:T(2,128)} %bitcast.4, bf16[512,640]{1,0:T(8,128)(2,1)} %feats.1), custom_call_target="tpu_custom_call" | custom-call | bytes 2000000 | tf_op jit(solution)/shard_map/pallas_call | solution.py:393
  1.8 3.1 %collective-permute-start = (bf16[64,640]{1,0:T(8,128)(2,1)S(1)}, bf16[64,640]{1,0:T(8,128)(2,1)S(1)}, u32[]{:S(2)}, u32[]{:S(2)}) collective-permute-start(bf16[64,640]{1,0:T(8,128)(2,1)S(1)} %get-tuple-element.45), channel_id=1, source_target_pairs={{4,8},{12,16},{20,24},{28,32},{36,40},{44,48},{52,56},{60,64},{68,... | collective-permute-start | bytes 245768 | tf_op jit(solution)/shard_map/ppermute | solution.py:57
  4.9 6.0 %collective-permute-start.1 = (bf16[256,640]{1,0:T(8,128)(2,1)S(1)}, bf16[256,640]{1,0:T(8,128)(2,1)S(1)}, u32[]{:S(2)}, u32[]{:S(2)}) collective-permute-start(bf16[256,640]{1,0:T(8,128)(2,1)S(1)} %get-tuple-element.46), channel_id=1, source_target_pairs={{0,4},{4,0},{8,12},{12,8},{16,20},{20,16},{24,28},{28,24},{32,36},... | collective-permute-start | bytes 983048 | tf_op jit(solution)/shard_map/ppermute | solution.py:50
  10.9 0.7 %collective-permute-start.2 = (bf16[256,640]{1,0:T(8,128)(2,1)S(1)}, bf16[256,640]{1,0:T(8,128)(2,1)S(1)}, u32[]{:S(2)}, u32[]{:S(2)}) collective-permute-start(bf16[256,640]{1,0:T(8,128)(2,1)S(1)} %get-tuple-element.49), channel_id=1, source_target_pairs={{8,16},{12,20},{24,32},{28,36},{40,48},{44,52},{56,64},{60,68},{72... | collective-permute-start | bytes 983048 | tf_op jit(solution)/shard_map/ppermute | solution.py:57
  12.2 2.9 %collective-permute-start.6 = (bf16[64,640]{1,0:T(8,128)(2,1)S(1)}, bf16[64,640]{1,0:T(8,128)(2,1)S(1)}, u32[]{:S(2)}, u32[]{:S(2)}) collective-permute-start(bf16[64,640]{1,0:T(8,128)(2,1)S(1)} %collective-permute-done.share0), channel_id=1, source_target_pairs={{0,2},{1,3},{2,0},{3,1},{4,6},{5,7},{6,4},{7,5},{8,10},{9,11},{10,... | collective-permute-start | bytes 245768 | tf_op jit(solution)/shard_map/ppermute | solution.py:61
  15.1 0.4 collective-permute-start.5
  15.5 0.4 collective-permute-start.4
  15.9 3.5 %shard_map.131 = (bf16[512,512]{1,0:T(8,128)(2,1)S(1)}, bf16[512,1024]{1,0:T(8,128)(2,1)S(1)}, f32[512,640]{1,0:T(8,128)S(1)}, f32[512,128]{1,0:T(8,128)S(1)}, f32[512,256]{1,0:T(8,128)S(1)}) custom-call(s32[1,4,8]{2,1,0:T(4,128)} %neighbors.1, s32[1,2,4]{2,1,0:T(2,128)} %bitcast.6, s32[1,4]{1,0:T(1,128)} %live.1, bf16[640,256]{1,0:T(8,128)(2,1)} %self_w.3, ...), custom_call_target="tpu_custom_call" | custom-call | flops 60000002048 | bytes 6000000 | tf_op jit(solution)/shard_map/pallas_call | solution.py:407
  19.4 4.2 %collective-permute-done.2.got0 = bf16[256,640]{1,0:T(8,128)(2,1)S(1)} collective-permute-done((bf16[256,640]{1,0:T(8,128)(2,1)S(1)}, bf16[256,640]{1,0:T(8,128)(2,1)S(1)}, u32[]{:S(2)}, u32[]{:S(2)}) %collective-permute-start.2) | collective-permute-done | bytes 327712 | tf_op jit(solution)/shard_map/ppermute | solution.py:57
  23.6 2.3 %shard_map.132 = (bf16[512,256]{1,0:T(8,128)(2,1)S(1)}, bf16[512,256]{1,0:T(8,128)(2,1)S(1)}, bf16[512,256]{1,0:T(8,128)(2,1)S(1)}, bf16[512,640]{1,0:T(8,128)(2,1)S(1)}, bf16[640,256]{1,0:T(8,128)(2,1)S(1)}) custom-call(bf16[512,1024]{1,0:T(8,128)(2,1)S(1)} %get-tuple-element.48.edge, bf16[256,640]{1,0:T(8,128)(2,1)S(1)} %collective-permute-done.2.got0, ...), custom_call_target="tpu_custom_call" | custom-call | flops 1600000000 | bytes 8000000 | tf_op jit(solution)/shard_map/pallas_call | solution.py:438
  25.9 0.9 %collective-permute-start.7 = (bf16[640,256]{1,0:T(8,128)(2,1)S(1)}, bf16[640,256]{1,0:T(8,128)(2,1)S(1)}, u32[]{:S(2)}, u32[]{:S(2)}) collective-permute-start(bf16[640,256]{1,0:T(8,128)(2,1)S(1)} %get-tuple-element.56), channel_id=1, source_target_pairs={{0,4},{4,0},{8,12},{12,8},{16,20},{20,16},{24,28},{28,24},{32,36},... | collective-permute-start | bytes 983048 | tf_op jit(solution)/shard_map/ppermute | solution.py:50
  26.8 0.4 shard_map.133.keep
  27.2 0.9 %collective-permute-done.7.got = bf16[640,256]{1,0:T(8,128)(2,1)S(1)} collective-permute-done((bf16[640,256]{1,0:T(8,128)(2,1)S(1)}, bf16[640,256]{1,0:T(8,128)(2,1)S(1)}, u32[]{:S(2)}, u32[]{:S(2)}) %collective-permute-start.7) | collective-permute-done | bytes 327712 | tf_op jit(solution)/shard_map/ppermute | solution.py:50
  28.1 0.8 %shard_map.134 = bf16[32,40,128]{2,1,0:T(8,128)(2,1)} custom-call(f32[640,256]{1,0:T(8,128)S(1)} %shard_map.133.keep, bf16[640,256]{1,0:T(8,128)(2,1)S(1)} %collective-permute-done.7.got), custom_call_target="tpu_custom_call" | custom-call | bytes 1500000 | tf_op jit(solution)/shard_map/pallas_call | solution.py:454
  28.9 5.2 %all-to-all-start = ((bf16[32,40,128]{2,1,0:T(8,128)(2,1)}), bf16[32,40,128]{2,1,0:T(8,128)(2,1)}, u32[]{:S(2)}, u32[]{:S(2)}) async-start(bf16[32,40,128]{2,1,0:T(8,128)(2,1)} %shard_map.134), calls=%async_computation | async-start | bytes 655360 | tf_op jit(solution)/shard_map/all_to_all | solution.py:67
  34.0 1.7 %shard_map.135 = (bf16[256,256]{1,0:T(8,128)(2,1)}, bf16[256,256]{1,0:T(8,128)(2,1)}, bf16[256,256]{1,0:T(8,128)(2,1)}, bf16[256,256]{1,0:T(8,128)(2,1)}, bf16[5...) custom-call(s32[1,2,4]{2,1,0:T(2,128)} %bitcast.5, ...), custom_call_target="tpu_custom_call" | custom-call | flops 600000000 | bytes 3000000 | tf_op jit(solution)/shard_map/pallas_call | solution.py:463
  35.7 0.7 %copy-done.2 = bf16[640,256]{1,0:T(8,128)(2,1)} copy-done((bf16[640,256]{1,0:T(8,128)(2,1)}, bf16[640,256]{1,0:T(8,128)(2,1)S(1)}, u32[]{:S(2)}) %copy-start.2) | copy-done | bytes 327704
  36.5 0.7 %copy-done.4 = bf16[640,256]{1,0:T(8,128)(2,1)} copy-done((bf16[640,256]{1,0:T(8,128)(2,1)}, bf16[640,256]{1,0:T(8,128)(2,1)S(1)}, u32[]{:S(2)}) %copy-start.4) | copy-done | bytes 327704
  37.2 2.3 %collective-permute-start.9 = (bf16[256,256]{1,0:T(8,128)(2,1)}, bf16[256,256]{1,0:T(8,128)(2,1)S(1)}, u32[]{:S(2)}, u32[]{:S(2)}) collective-permute-start(bf16[256,256]{1,0:T(8,128)(2,1)} %get-tuple-element.76), channel_id=1, source_target_pairs={{8,16},{12,20},{24,32},{28,36},{40,48},{44,52},{56,64},{60,68},{72... | collective-permute-start | bytes 393224 | tf_op jit(solution)/shard_map/ppermute | solution.py:57
  39.5 1.1 %collective-permute-start.10 = (bf16[256,256]{1,0:T(8,128)(2,1)}, bf16[256,256]{1,0:T(8,128)(2,1)S(1)}, u32[]{:S(2)}, u32[]{:S(2)}) collective-permute-start(bf16[256,256]{1,0:T(8,128)(2,1)} %get-tuple-element.77), channel_id=1, source_target_pairs={{4,8},{12,16},{20,24},{28,32},{36,40},{44,48},{52,56},{60,64},{68,... | collective-permute-start | bytes 393224 | tf_op jit(solution)/shard_map/ppermute | solution.py:57
  40.9 1.4 %collective-permute-start.12 = (bf16[256,256]{1,0:T(8,128)(2,1)}, bf16[256,256]{1,0:T(8,128)(2,1)S(1)}, u32[]{:S(2)}, u32[]{:S(2)}) collective-permute-start(bf16[256,256]{1,0:T(8,128)(2,1)} %get-tuple-element.79), channel_id=1, source_target_pairs={{0,4},{4,0},{8,12},{12,8},{16,20},{20,16},{24,28},{28,24},{32,36},... | collective-permute-start | bytes 393224 | tf_op jit(solution)/shard_map/ppermute | solution.py:50
  42.4 1.4 %all-to-all-done.got = bf16[32,40,128]{2,1,0:T(8,128)(2,1)} async-done(((bf16[32,40,128]{2,1,0:T(8,128)(2,1)}), bf16[32,40,128]{2,1,0:T(8,128)(2,1)}, u32[]{:S(2)}, u32[]{:S(2)}) %all-to-all-start) | async-done | bytes 327712 | tf_op jit(solution)/shard_map/all_to_all | solution.py:67
  43.7 1.8 %shard_map.136 = bf16[32,40,128]{2,1,0:T(8,128)(2,1)} custom-call(bf16[32,40,128]{2,1,0:T(8,128)(2,1)} %all-to-all-done.got), custom_call_target="tpu_custom_call" | custom-call | bytes 700000 | tf_op jit(solution)/shard_map/pallas_call | solution.py:475
  45.5 8.0 %all-to-all-start.1 = ((bf16[32,40,128]{2,1,0:T(8,128)(2,1)}), bf16[32,40,128]{2,1,0:T(8,128)(2,1)S(1)}, u32[]{:S(2)}, u32[]{:S(2)}) async-start(bf16[32,40,128]{2,1,0:T(8,128)(2,1)} %shard_map.136), calls=%async_computation.1 | async-start | bytes 655360 | tf_op jit(solution)/shard_map/all_to_all | solution.py:67
  53.7 1.1 %shard_map.138 = (f32[160,512]{1,0:T(8,128)S(1)}, bf16[160,512]{1,0:T(8,128)(2,1)S(1)}, bf16[160,512]{1,0:T(8,128)(2,1)S(1)}, bf16[160,512]{1,0:T(8,128)(2,1)S(1)}) custom-call(f32[32,128]{1,0:T(8,128)S(1)} %get-tuple-element.71.place, f32[512,256]{1,0:T(8,128)S(1)} %get-tuple-element.72.start, bf16[512,256]{1,0:T(8,128)(2,1)S(1)} %get-tuple-element.73.low, ...), custom_call_target="tpu_custom_call" | custom-call | flops 60000002048 | bytes 3000000 | tf_op jit(solution)/shard_map/pallas_call | solution.py:489
  54.8 3.0 %collective-permute-start.13 = (bf16[160,512]{1,0:T(8,128)(2,1)S(1)}, bf16[160,512]{1,0:T(8,128)(2,1)S(1)}, u32[]{:S(2)}, u32[]{:S(2)}) collective-permute-start(bf16[160,512]{1,0:T(8,128)(2,1)S(1)} %get-tuple-element.81), channel_id=1, source_target_pairs={{0,2},{1,3},{2,0},{3,1},{4,6},{5,7},{6,4},{7,5},{8,10},{9,11},{10,... | collective-permute-start | bytes 491528 | tf_op jit(solution)/shard_map/ppermute | solution.py:61
  57.8 0.4 collective-permute-start.14
  58.2 0.4 collective-permute-start.15
  58.5 4.0 %all-to-all-done.1.mine = bf16[32,40,128]{2,1,0:T(8,128)(2,1)S(1)} async-done(((bf16[32,40,128]{2,1,0:T(8,128)(2,1)}), bf16[32,40,128]{2,1,0:T(8,128)(2,1)S(1)}, u32[]{:S(2)}, u32[]{:S(2)}) %all-to-all-start.1) | async-done | bytes 327712 | tf_op jit(solution)/shard_map/all_to_all | solution.py:67
  62.5 2.7 %collective-permute-start.8 = (bf16[32,40,128]{2,1,0:T(8,128)(2,1)S(1)}, bf16[32,40,128]{2,1,0:T(8,128)(2,1)S(1)}, u32[]{:S(2)}, u32[]{:S(2)}) collective-permute-start(bf16[32,40,128]{2,1,0:T(8,128)(2,1)S(1)} %all-to-all-done.1.mine), channel_id=1, source_target_pairs={{0,4},{4,0},{8,12},{12,8},{16,20},{20,16},{24,28},{28,24},{32,36},... | collective-permute-start | bytes 983048 | tf_op jit(solution)/shard_map/ppermute | solution.py:50
  65.5 0.7 %fusion = bf16[512,160]{0,1:T(8,128)(2,1)} fusion(bf16[160,512]{1,0:T(8,128)(2,1)S(1)} %collective-permute-done.15, bf16[160,512]{1,0:T(8,128)(2,1)S(1)} %collective-permute-done.14, f32[160,512]{1,0:T(8,128)S(1)} %get-tuple-element.80, bf16[160,512]{1,0:T(8,128)(2,1)S(1)} %collective-permute-done.13), kind=kLoop, calls=%fused_computation.1 | loop fusion | flops 573440 | bytes 983040 | tf_op jit(solution)/shard_map/transpose | solution.py:509
  66.4 1.2 %shard_map.137 = (f32[640,256]{1,0:T(8,128)}, f32[640,256]{1,0:T(8,128)}) custom-call(bf16[32,40,128]{2,1,0:T(8,128)(2,1)S(1)} %all-to-all-done.1.mine, bf16[32,40,128]{2,1,0:T(8,128)(2,1)S(1)} %collective-permute-done.8.other), custom_call_target="tpu_custom_call" | custom-call | bytes 2000000 | tf_op jit(solution)/shard_map/pallas_call | solution.py:500
  (29 shorter events, 1.4 us)
Async XLA Ops:
  1.8 10.0 %collective-permute-start = (bf16[64,640]{1,0:T(8,128)(2,1)S(1)}, bf16[64,640]{1,0:T(8,128)(2,1)S(1)}, u32[]{:S(2)}, u32[]{:S(2)}) collective-permute-start(bf16[64,640]{1,0:T(8,128)(2,1)S(1)} %get-tuple-element.45), channel_id=1, source_target_pairs={{4,8},{12,16},{20,24},{28,32},{36,40},{44,48},{52,56},{60,64},{68,... | collective-permute-start | bytes 245768 | tf_op jit(solution)/shard_map/ppermute | solution.py:57
  4.9 7.2 %collective-permute-start.1 = (bf16[256,640]{1,0:T(8,128)(2,1)S(1)}, bf16[256,640]{1,0:T(8,128)(2,1)S(1)}, u32[]{:S(2)}, u32[]{:S(2)}) collective-permute-start(bf16[256,640]{1,0:T(8,128)(2,1)S(1)} %get-tuple-element.46), channel_id=1, source_target_pairs={{0,4},{4,0},{8,12},{12,8},{16,20},{20,16},{24,28},{28,24},{32,36},... | collective-permute-start | bytes 983048 | tf_op jit(solution)/shard_map/ppermute | solution.py:50
  10.9 12.7 %collective-permute-start.2 = (bf16[256,640]{1,0:T(8,128)(2,1)S(1)}, bf16[256,640]{1,0:T(8,128)(2,1)S(1)}, u32[]{:S(2)}, u32[]{:S(2)}) collective-permute-start(bf16[256,640]{1,0:T(8,128)(2,1)S(1)} %get-tuple-element.49), channel_id=1, source_target_pairs={{8,16},{12,20},{24,32},{28,36},{40,48},{44,52},{56,64},{60,68},{72... | collective-permute-start | bytes 983048 | tf_op jit(solution)/shard_map/ppermute | solution.py:57
  11.6 11.9 %collective-permute-start.3 = (bf16[256,640]{1,0:T(8,128)(2,1)S(1)}, bf16[256,640]{1,0:T(8,128)(2,1)S(1)}, u32[]{:S(2)}, u32[]{:S(2)}) collective-permute-start(bf16[256,640]{1,0:T(8,128)(2,1)S(1)} %get-tuple-element.50), channel_id=1, source_target_pairs={{0,8},{4,12},{8,0},{12,4},{16,24},{20,28},{24,16},{28,20},{32,40},... | collective-permute-start | bytes 983048 | tf_op jit(solution)/shard_map/ppermute | solution.py:50
  12.2 11.4 %collective-permute-start.6 = (bf16[64,640]{1,0:T(8,128)(2,1)S(1)}, bf16[64,640]{1,0:T(8,128)(2,1)S(1)}, u32[]{:S(2)}, u32[]{:S(2)}) collective-permute-start(bf16[64,640]{1,0:T(8,128)(2,1)S(1)} %collective-permute-done.share0), channel_id=1, source_target_pairs={{0,2},{1,3},{2,0},{3,1},{4,6},{5,7},{6,4},{7,5},{8,10},{9,11},{10,... | collective-permute-start | bytes 245768 | tf_op jit(solution)/shard_map/ppermute | solution.py:61
  15.1 8.5 %collective-permute-start.5 = (bf16[64,640]{1,0:T(8,128)(2,1)S(1)}, bf16[64,640]{1,0:T(8,128)(2,1)S(1)}, u32[]{:S(2)}, u32[]{:S(2)}) collective-permute-start(bf16[64,640]{1,0:T(8,128)(2,1)S(1)} %collective-permute-done.share0), channel_id=1, source_target_pairs={{0,1},{1,0},{2,3},{3,2},{4,5},{5,4},{6,7},{7,6},{8,9},{9,8},{10,11... | collective-permute-start | bytes 245768 | tf_op jit(solution)/shard_map/ppermute | solution.py:61
  15.5 8.1 %collective-permute-start.4 = (bf16[64,640]{1,0:T(8,128)(2,1)S(1)}, bf16[64,640]{1,0:T(8,128)(2,1)S(1)}, u32[]{:S(2)}, u32[]{:S(2)}) collective-permute-start(bf16[64,640]{1,0:T(8,128)(2,1)S(1)} %collective-permute-done.share0), channel_id=1, source_target_pairs={{0,3},{1,2},{2,1},{3,0},{4,7},{5,6},{6,5},{7,4},{8,11},{9,10},{10,... | collective-permute-start | bytes 245768 | tf_op jit(solution)/shard_map/ppermute | solution.py:61
  15.9 7.7 %copy-start.1 = (bf16[640,256]{1,0:T(8,128)(2,1)S(1)}, bf16[640,256]{1,0:T(8,128)(2,1)}, u32[]{:S(2)}) copy-start(bf16[640,256]{1,0:T(8,128)(2,1)} %neigh_w.3) | copy-start | bytes 983044
  15.9 7.7 %copy-start.6 = (bf16[512,256]{1,0:T(8,128)(2,1)S(1)}, bf16[512,256]{1,0:T(8,128)(2,1)}, u32[]{:S(2)}) copy-start(bf16[512,256]{1,0:T(8,128)(2,1)} %cot.1) | copy-start | bytes 786436
  25.9 2.2 %collective-permute-start.7 = (bf16[640,256]{1,0:T(8,128)(2,1)S(1)}, bf16[640,256]{1,0:T(8,128)(2,1)S(1)}, u32[]{:S(2)}, u32[]{:S(2)}) collective-permute-start(bf16[640,256]{1,0:T(8,128)(2,1)S(1)} %get-tuple-element.56), channel_id=1, source_target_pairs={{0,4},{4,0},{8,12},{12,8},{16,20},{20,16},{24,28},{28,24},{32,36},... | collective-permute-start | bytes 983048 | tf_op jit(solution)/shard_map/ppermute | solution.py:50
  27.2 6.8 %copy-start = (bf16[640,256]{1,0:T(8,128)(2,1)S(1)}, bf16[640,256]{1,0:T(8,128)(2,1)}, u32[]{:S(2)}) copy-start(bf16[640,256]{1,0:T(8,128)(2,1)} %self_w.3) | copy-start | bytes 983044
  28.9 14.9 %all-to-all-start = ((bf16[32,40,128]{2,1,0:T(8,128)(2,1)}), bf16[32,40,128]{2,1,0:T(8,128)(2,1)}, u32[]{:S(2)}, u32[]{:S(2)}) async-start(bf16[32,40,128]{2,1,0:T(8,128)(2,1)} %shard_map.134), calls=%async_computation | async-start | bytes 655360 | tf_op jit(solution)/shard_map/all_to_all | solution.py:67
  35.7 0.7 %copy-start.2 = (bf16[640,256]{1,0:T(8,128)(2,1)}, bf16[640,256]{1,0:T(8,128)(2,1)S(1)}, u32[]{:S(2)}) copy-start(bf16[640,256]{1,0:T(8,128)(2,1)S(1)} %get-tuple-element.74.self_w) | copy-start | bytes 983044
  36.5 0.7 %copy-start.4 = (bf16[640,256]{1,0:T(8,128)(2,1)}, bf16[640,256]{1,0:T(8,128)(2,1)S(1)}, u32[]{:S(2)}) copy-start(bf16[640,256]{1,0:T(8,128)(2,1)S(1)} %get-tuple-element.75.neigh_w) | copy-start | bytes 983044
  37.2 16.5 %copy-start.3 = (bf16[640,256]{1,0:T(8,128)(2,1)S(1)}, bf16[640,256]{1,0:T(8,128)(2,1)}, u32[]{:S(2)}) copy-start(bf16[640,256]{1,0:T(8,128)(2,1)} %copy-done.2) | copy-start | bytes 983044
  37.2 16.5 %copy-start.5 = (bf16[640,256]{1,0:T(8,128)(2,1)S(1)}, bf16[640,256]{1,0:T(8,128)(2,1)}, u32[]{:S(2)}) copy-start(bf16[640,256]{1,0:T(8,128)(2,1)} %copy-done.4) | copy-start | bytes 983044
  37.2 16.4 %collective-permute-start.9 = (bf16[256,256]{1,0:T(8,128)(2,1)}, bf16[256,256]{1,0:T(8,128)(2,1)S(1)}, u32[]{:S(2)}, u32[]{:S(2)}) collective-permute-start(bf16[256,256]{1,0:T(8,128)(2,1)} %get-tuple-element.76), channel_id=1, source_target_pairs={{8,16},{12,20},{24,32},{28,36},{40,48},{44,52},{56,64},{60,68},{72... | collective-permute-start | bytes 393224 | tf_op jit(solution)/shard_map/ppermute | solution.py:57
  39.5 14.1 %collective-permute-start.10 = (bf16[256,256]{1,0:T(8,128)(2,1)}, bf16[256,256]{1,0:T(8,128)(2,1)S(1)}, u32[]{:S(2)}, u32[]{:S(2)}) collective-permute-start(bf16[256,256]{1,0:T(8,128)(2,1)} %get-tuple-element.77), channel_id=1, source_target_pairs={{4,8},{12,16},{20,24},{28,32},{36,40},{44,48},{52,56},{60,64},{68,... | collective-permute-start | bytes 393224 | tf_op jit(solution)/shard_map/ppermute | solution.py:57
  40.6 13.0 %collective-permute-start.11 = (bf16[256,256]{1,0:T(8,128)(2,1)}, bf16[256,256]{1,0:T(8,128)(2,1)S(1)}, u32[]{:S(2)}, u32[]{:S(2)}) collective-permute-start(bf16[256,256]{1,0:T(8,128)(2,1)} %get-tuple-element.78), channel_id=1, source_target_pairs={{0,8},{4,12},{8,0},{12,4},{16,24},{20,28},{24,16},{28,20},{32,40},... | collective-permute-start | bytes 393224 | tf_op jit(solution)/shard_map/ppermute | solution.py:50
  40.9 12.7 %collective-permute-start.12 = (bf16[256,256]{1,0:T(8,128)(2,1)}, bf16[256,256]{1,0:T(8,128)(2,1)S(1)}, u32[]{:S(2)}, u32[]{:S(2)}) collective-permute-start(bf16[256,256]{1,0:T(8,128)(2,1)} %get-tuple-element.79), channel_id=1, source_target_pairs={{0,4},{4,0},{8,12},{12,8},{16,20},{20,16},{24,28},{28,24},{32,36},... | collective-permute-start | bytes 393224 | tf_op jit(solution)/shard_map/ppermute | solution.py:50
  45.5 17.0 %all-to-all-start.1 = ((bf16[32,40,128]{2,1,0:T(8,128)(2,1)}), bf16[32,40,128]{2,1,0:T(8,128)(2,1)S(1)}, u32[]{:S(2)}, u32[]{:S(2)}) async-start(bf16[32,40,128]{2,1,0:T(8,128)(2,1)} %shard_map.136), calls=%async_computation.1 | async-start | bytes 655360 | tf_op jit(solution)/shard_map/all_to_all | solution.py:67
  54.8 10.4 %collective-permute-start.13 = (bf16[160,512]{1,0:T(8,128)(2,1)S(1)}, bf16[160,512]{1,0:T(8,128)(2,1)S(1)}, u32[]{:S(2)}, u32[]{:S(2)}) collective-permute-start(bf16[160,512]{1,0:T(8,128)(2,1)S(1)} %get-tuple-element.81), channel_id=1, source_target_pairs={{0,2},{1,3},{2,0},{3,1},{4,6},{5,7},{6,4},{7,5},{8,10},{9,11},{10,... | collective-permute-start | bytes 491528 | tf_op jit(solution)/shard_map/ppermute | solution.py:61
  57.8 7.4 %collective-permute-start.14 = (bf16[160,512]{1,0:T(8,128)(2,1)S(1)}, bf16[160,512]{1,0:T(8,128)(2,1)S(1)}, u32[]{:S(2)}, u32[]{:S(2)}) collective-permute-start(bf16[160,512]{1,0:T(8,128)(2,1)S(1)} %get-tuple-element.82), channel_id=1, source_target_pairs={{0,1},{1,0},{2,3},{3,2},{4,5},{5,4},{6,7},{7,6},{8,9},{9,8},{10,11... | collective-permute-start | bytes 491528 | tf_op jit(solution)/shard_map/ppermute | solution.py:61
  58.2 7.3 %collective-permute-start.15 = (bf16[160,512]{1,0:T(8,128)(2,1)S(1)}, bf16[160,512]{1,0:T(8,128)(2,1)S(1)}, u32[]{:S(2)}, u32[]{:S(2)}) collective-permute-start(bf16[160,512]{1,0:T(8,128)(2,1)S(1)} %get-tuple-element.83), channel_id=1, source_target_pairs={{0,3},{1,2},{2,1},{3,0},{4,7},{5,6},{6,5},{7,4},{8,11},{9,10},{10,... | collective-permute-start | bytes 491528 | tf_op jit(solution)/shard_map/ppermute | solution.py:61
  62.5 3.9 %collective-permute-start.8 = (bf16[32,40,128]{2,1,0:T(8,128)(2,1)S(1)}, bf16[32,40,128]{2,1,0:T(8,128)(2,1)S(1)}, u32[]{:S(2)}, u32[]{:S(2)}) collective-permute-start(bf16[32,40,128]{2,1,0:T(8,128)(2,1)S(1)} %all-to-all-done.1.mine), channel_id=1, source_target_pairs={{0,4},{4,0},{8,12},{12,8},{16,20},{20,16},{24,28},{28,24},{32,36},... | collective-permute-start | bytes 983048 | tf_op jit(solution)/shard_map/ppermute | solution.py:50

commit v9 on v7

--- a/solution.py
+++ b/solution.py
@@ -209,7 +209,9 @@
     mean_high = mean.astype(BF16)
     mean_rest = (mean - mean_high.astype(F32)).astype(BF16)
     weights = neigh_w[...]
-    pre = own_pre[...] + dot(mean_high, weights) + dot(mean_rest, weights)
+    both = dot(jnp.concatenate([mean_high, mean_rest], axis=0), weights)
+    count = mean.shape[0]
+    pre = own_pre[...] + both[:count] + both[count:]
     sig = jax.nn.sigmoid(pre)
     activated[...] = (pre * sig).astype(BF16)
     grad = cot[...].astype(F32) * sig * (1.0 + pre * (1.0 - sig))

time: 66.6 us -> 66.3 us (level)
  transfers between devices with their start and end apart: 18 -> 18, of which waited for: 7 -> 7; matrix products, arithmetic and copies ran while one was open for 1% -> 1% of each run, Pallas kernels for 11% -> 12%
where the time goes in v9:
time: 66.3 us; the launch traced here: 65.9 us
  starting transfers between devices  39 us (59%)
  Pallas kernels  12.7 us (19%)
  waiting for transfers between devices  10.3 us (16%)
  local copies, waits for them, and re-layouts  2.26 us (3%)
  between operations  0.83 us (1%)
  other arithmetic  0.74 us (1%)
    all_to_all x2, starting transfers between devices, exchange(): return lax.all_to_all(array, 'dom', 0, 0, axis_index_groups=groups)  12.8 us
    ppermute x6, starting transfers between devices, dom_swap(): return lax.ppermute(array, 'dom', [(i, i ^ mask) for i in range(count)])  11.4 us
    ppermute x6, starting transfers between devices, hid_swap(): return lax.ppermute(array, 'hid', [(i, i ^ mask) for i in range(HID)])  7.47 us
    ppermute x4, starting transfers between devices, dom_pairs(): return lax.ppermute(array, 'dom', pairs + [(j, i) for i, j in pairs])  7.29 us
    all_to_all x2, waiting for transfers between devices, exchange(): return lax.all_to_all(array, 'dom', 0, 0, axis_index_groups=groups)  4.43 us
    ppermute x4, waiting for transfers between devices, dom_pairs(): return lax.ppermute(array, 'dom', pairs + [(j, i) for i, j in pairs])  4.23 us
    pallas_call x1, Pallas kernels, on_device(): call(before_kernel, [((n, n), BF16), ((n, slots), BF16), ((n, width), F32...  3.47 us
    unnamed x18, local copies, waits for them, and re-layouts  2.26 us
  transfers between devices with their start and end apart: 18, of which 7 were waited for; matrix products, arithmetic and copies ran while one was open for 1% of the time, Pallas kernels for 12%

profile of v9, /device:TPU:1, one launch (start us, length us, event | category | flops | bytes accessed | tf_op | source)
XLA Modules:
  0.0 65.9 jit_solution(15817579122828895216)
XLA Ops:
  0.6 1.2 %shard_map.129 = (bf16[256,640]{1,0:T(8,128)(2,1)S(1)}, bf16[64,640]{1,0:T(8,128)(2,1)S(1)}, bf16[256,640]{1,0:T(8,128)(2,1)S(1)}, bf16[256,640]{1,0:T(8,128)(2,1)S(1)}, bf16[512,640]{1,0:T(8,128)(2,1)S(1)}) custom-call(s32[1,2,4]{2,1,0:T(2,128)} %bitcast.4, bf16[512,640]{1,0:T(8,128)(2,1)} %feats.1), custom_call_target="tpu_custom_call" | custom-call | bytes 2000000 | tf_op jit(solution)/shard_map/pallas_call | solution.py:366
  1.8 3.1 %collective-permute-start = (bf16[64,640]{1,0:T(8,128)(2,1)S(1)}, bf16[64,640]{1,0:T(8,128)(2,1)S(1)}, u32[]{:S(2)}, u32[]{:S(2)}) collective-permute-start(bf16[64,640]{1,0:T(8,128)(2,1)S(1)} %get-tuple-element.45), channel_id=1, source_target_pairs={{4,8},{12,16},{20,24},{28,32},{36,40},{44,48},{52,56},{60,64},{68,... | collective-permute-start | bytes 245768 | tf_op jit(solution)/shard_map/ppermute | solution.py:56
  4.9 6.0 %collective-permute-start.1 = (bf16[256,640]{1,0:T(8,128)(2,1)S(1)}, bf16[256,640]{1,0:T(8,128)(2,1)S(1)}, u32[]{:S(2)}, u32[]{:S(2)}) collective-permute-start(bf16[256,640]{1,0:T(8,128)(2,1)S(1)} %get-tuple-element.46), channel_id=1, source_target_pairs={{0,4},{4,0},{8,12},{12,8},{16,20},{20,16},{24,28},{28,24},{32,36},... | collective-permute-start | bytes 983048 | tf_op jit(solution)/shard_map/ppermute | solution.py:49
  10.9 0.7 %collective-permute-start.2 = (bf16[256,640]{1,0:T(8,128)(2,1)S(1)}, bf16[256,640]{1,0:T(8,128)(2,1)S(1)}, u32[]{:S(2)}, u32[]{:S(2)}) collective-permute-start(bf16[256,640]{1,0:T(8,128)(2,1)S(1)} %get-tuple-element.49), channel_id=1, source_target_pairs={{8,16},{12,20},{24,32},{28,36},{40,48},{44,52},{56,64},{60,68},{72... | collective-permute-start | bytes 983048 | tf_op jit(solution)/shard_map/ppermute | solution.py:56
  12.2 2.9 %collective-permute-start.6 = (bf16[64,640]{1,0:T(8,128)(2,1)S(1)}, bf16[64,640]{1,0:T(8,128)(2,1)S(1)}, u32[]{:S(2)}, u32[]{:S(2)}) collective-permute-start(bf16[64,640]{1,0:T(8,128)(2,1)S(1)} %collective-permute-done.share0), channel_id=1, source_target_pairs={{0,2},{1,3},{2,0},{3,1},{4,6},{5,7},{6,4},{7,5},{8,10},{9,11},{10,... | collective-permute-start | bytes 245768 | tf_op jit(solution)/shard_map/ppermute | solution.py:60
  15.1 0.4 collective-permute-start.5
  15.5 0.4 collective-permute-start.4
  15.9 3.5 %shard_map.131 = (bf16[512,512]{1,0:T(8,128)(2,1)S(1)}, bf16[512,1024]{1,0:T(8,128)(2,1)S(1)}, f32[512,640]{1,0:T(8,128)S(1)}, f32[512,128]{1,0:T(8,128)S(1)}, f32[512,256]{1,0:T(8,128)S(1)}) custom-call(s32[1,4,8]{2,1,0:T(4,128)} %neighbors.1, s32[1,2,4]{2,1,0:T(2,128)} %bitcast.6, s32[1,4]{1,0:T(1,128)} %live.1, bf16[640,256]{1,0:T(8,128)(2,1)} %self_w.3, ...), custom_call_target="tpu_custom_call" | custom-call | flops 60000002048 | bytes 6000000 | tf_op jit(solution)/shard_map/pallas_call | solution.py:380
  19.3 4.2 %collective-permute-done.2.got0 = bf16[256,640]{1,0:T(8,128)(2,1)S(1)} collective-permute-done((bf16[256,640]{1,0:T(8,128)(2,1)S(1)}, bf16[256,640]{1,0:T(8,128)(2,1)S(1)}, u32[]{:S(2)}, u32[]{:S(2)}) %collective-permute-start.2) | collective-permute-done | bytes 327712 | tf_op jit(solution)/shard_map/ppermute | solution.py:56
  23.6 2.0 %shard_map.132 = (bf16[512,256]{1,0:T(8,128)(2,1)S(1)}, bf16[512,256]{1,0:T(8,128)(2,1)S(1)}, bf16[512,256]{1,0:T(8,128)(2,1)S(1)}, bf16[512,640]{1,0:T(8,128)(2,1)S(1)}, bf16[640,256]{1,0:T(8,128)(2,1)S(1)}) custom-call(bf16[512,1024]{1,0:T(8,128)(2,1)S(1)} %get-tuple-element.48.edge, bf16[256,640]{1,0:T(8,128)(2,1)S(1)} %collective-permute-done.2.got0, ...), custom_call_target="tpu_custom_call" | custom-call | flops 1600000000 | bytes 8000000 | tf_op jit(solution)/shard_map/pallas_call | solution.py:411
  25.6 0.9 %collective-permute-start.7 = (bf16[640,256]{1,0:T(8,128)(2,1)S(1)}, bf16[640,256]{1,0:T(8,128)(2,1)S(1)}, u32[]{:S(2)}, u32[]{:S(2)}) collective-permute-start(bf16[640,256]{1,0:T(8,128)(2,1)S(1)} %get-tuple-element.56), channel_id=1, source_target_pairs={{0,4},{4,0},{8,12},{12,8},{16,20},{20,16},{24,28},{28,24},{32,36},... | collective-permute-start | bytes 983048 | tf_op jit(solution)/shard_map/ppermute | solution.py:49
  26.5 0.4 shard_map.133.keep
  26.9 0.9 %collective-permute-done.7.got = bf16[640,256]{1,0:T(8,128)(2,1)S(1)} collective-permute-done((bf16[640,256]{1,0:T(8,128)(2,1)S(1)}, bf16[640,256]{1,0:T(8,128)(2,1)S(1)}, u32[]{:S(2)}, u32[]{:S(2)}) %collective-permute-start.7) | collective-permute-done | bytes 327712 | tf_op jit(solution)/shard_map/ppermute | solution.py:49
  27.8 0.8 %shard_map.134 = bf16[32,40,128]{2,1,0:T(8,128)(2,1)} custom-call(f32[640,256]{1,0:T(8,128)S(1)} %shard_map.133.keep, bf16[640,256]{1,0:T(8,128)(2,1)S(1)} %collective-permute-done.7.got), custom_call_target="tpu_custom_call" | custom-call | bytes 1500000 | tf_op jit(solution)/shard_map/pallas_call | solution.py:427
  28.6 5.1 %all-to-all-start = ((bf16[32,40,128]{2,1,0:T(8,128)(2,1)}), bf16[32,40,128]{2,1,0:T(8,128)(2,1)S(1)}, u32[]{:S(2)}, u32[]{:S(2)}) async-start(bf16[32,40,128]{2,1,0:T(8,128)(2,1)} %shard_map.134), calls=%async_computation | async-start | bytes 655360 | tf_op jit(solution)/shard_map/all_to_all | solution.py:66
  33.7 1.7 %shard_map.135 = (bf16[256,256]{1,0:T(8,128)(2,1)}, bf16[256,256]{1,0:T(8,128)(2,1)}, bf16[256,256]{1,0:T(8,128)(2,1)}, bf16[256,256]{1,0:T(8,128)(2,1)S(1)}, bf...) custom-call(s32[1,2,4]{2,1,0:T(2,128)} %bitcast.5, ...), custom_call_target="tpu_custom_call" | custom-call | flops 600000000 | bytes 3000000 | tf_op jit(solution)/shard_map/pallas_call | solution.py:429
  35.4 0.8 %copy-done.2 = f32[512,256]{1,0:T(8,128)} copy-done((f32[512,256]{1,0:T(8,128)}, f32[512,256]{1,0:T(8,128)S(1)}, u32[]{:S(2)}) %copy-start.2) | copy-done | bytes 524312
  36.1 0.7 %copy-done.4 = bf16[640,256]{1,0:T(8,128)(2,1)} copy-done((bf16[640,256]{1,0:T(8,128)(2,1)}, bf16[640,256]{1,0:T(8,128)(2,1)S(1)}, u32[]{:S(2)}) %copy-start.4) | copy-done | bytes 327704
  36.9 0.7 %copy-done.6 = bf16[640,256]{1,0:T(8,128)(2,1)} copy-done((bf16[640,256]{1,0:T(8,128)(2,1)}, bf16[640,256]{1,0:T(8,128)(2,1)S(1)}, u32[]{:S(2)}) %copy-start.6) | copy-done | bytes 327704
  37.6 2.3 %collective-permute-start.9 = (bf16[256,256]{1,0:T(8,128)(2,1)}, bf16[256,256]{1,0:T(8,128)(2,1)S(1)}, u32[]{:S(2)}, u32[]{:S(2)}) collective-permute-start(bf16[256,256]{1,0:T(8,128)(2,1)} %get-tuple-element.76), channel_id=1, source_target_pairs={{8,16},{12,20},{24,32},{28,36},{40,48},{44,52},{56,64},{60,68},{72... | collective-permute-start | bytes 393224 | tf_op jit(solution)/shard_map/ppermute | solution.py:56
  39.9 1.1 %collective-permute-start.10 = (bf16[256,256]{1,0:T(8,128)(2,1)}, bf16[256,256]{1,0:T(8,128)(2,1)S(1)}, u32[]{:S(2)}, u32[]{:S(2)}) collective-permute-start(bf16[256,256]{1,0:T(8,128)(2,1)} %get-tuple-element.77), channel_id=1, source_target_pairs={{4,8},{12,16},{20,24},{28,32},{36,40},{44,48},{52,56},{60,64},{68,... | collective-permute-start | bytes 393224 | tf_op jit(solution)/shard_map/ppermute | solution.py:56
  41.3 1.4 %collective-permute-start.12 = (bf16[256,256]{1,0:T(8,128)(2,1)S(1)}, bf16[256,256]{1,0:T(8,128)(2,1)S(1)}, u32[]{:S(2)}, u32[]{:S(2)}) collective-permute-start(bf16[256,256]{1,0:T(8,128)(2,1)S(1)} %get-tuple-element.79), channel_id=1, source_target_pairs={{0,4},{4,0},{8,12},{12,8},{16,20},{20,16},{24,28},{28,24},{32,36},... | collective-permute-start | bytes 393224 | tf_op jit(solution)/shard_map/ppermute | solution.py:49
  42.8 0.5 all-to-all-done.got
  43.3 0.8 %shard_map.136 = bf16[32,40,128]{2,1,0:T(8,128)(2,1)} custom-call(bf16[32,40,128]{2,1,0:T(8,128)(2,1)S(1)} %all-to-all-done.got), custom_call_target="tpu_custom_call" | custom-call | bytes 700000 | tf_op jit(solution)/shard_map/pallas_call | solution.py:441
  44.1 7.7 %all-to-all-start.1 = ((bf16[32,40,128]{2,1,0:T(8,128)(2,1)}), bf16[32,40,128]{2,1,0:T(8,128)(2,1)S(1)}, u32[]{:S(2)}, u32[]{:S(2)}) async-start(bf16[32,40,128]{2,1,0:T(8,128)(2,1)} %shard_map.136), calls=%async_computation.1 | async-start | bytes 655360 | tf_op jit(solution)/shard_map/all_to_all | solution.py:66
  51.9 1.1 %shard_map.138 = (f32[160,512]{1,0:T(8,128)S(1)}, bf16[160,512]{1,0:T(8,128)(2,1)S(1)}, bf16[160,512]{1,0:T(8,128)(2,1)S(1)}, bf16[160,512]{1,0:T(8,128)(2,1)S(1)}) custom-call(f32[32,128]{1,0:T(8,128)S(1)} %get-tuple-element.71.place, f32[512,256]{1,0:T(8,128)S(1)} %copy-done.3, bf16[512,256]{1,0:T(8,128)(2,1)S(1)} %get-tuple-element.73.low, ...), custom_call_target="tpu_custom_call" | custom-call | flops 60000002048 | bytes 3000000 | tf_op jit(solution)/shard_map/pallas_call | solution.py:444
  53.0 3.0 %collective-permute-start.13 = (bf16[160,512]{1,0:T(8,128)(2,1)S(1)}, bf16[160,512]{1,0:T(8,128)(2,1)S(1)}, u32[]{:S(2)}, u32[]{:S(2)}) collective-permute-start(bf16[160,512]{1,0:T(8,128)(2,1)S(1)} %get-tuple-element.81), channel_id=1, source_target_pairs={{0,2},{1,3},{2,0},{3,1},{4,6},{5,7},{6,4},{7,5},{8,10},{9,11},{10,... | collective-permute-start | bytes 491528 | tf_op jit(solution)/shard_map/ppermute | solution.py:60
  56.0 0.4 collective-permute-start.14
  56.8 3.9 %all-to-all-done.1.mine = bf16[32,40,128]{2,1,0:T(8,128)(2,1)S(1)} async-done(((bf16[32,40,128]{2,1,0:T(8,128)(2,1)}), bf16[32,40,128]{2,1,0:T(8,128)(2,1)S(1)}, u32[]{:S(2)}, u32[]{:S(2)}) %all-to-all-start.1) | async-done | bytes 327712 | tf_op jit(solution)/shard_map/all_to_all | solution.py:66
  60.7 2.7 %collective-permute-start.8 = (bf16[32,40,128]{2,1,0:T(8,128)(2,1)S(1)}, bf16[32,40,128]{2,1,0:T(8,128)(2,1)S(1)}, u32[]{:S(2)}, u32[]{:S(2)}) collective-permute-start(bf16[32,40,128]{2,1,0:T(8,128)(2,1)S(1)} %all-to-all-done.1.mine), channel_id=1, source_target_pairs={{0,4},{4,0},{8,12},{12,8},{16,20},{20,16},{24,28},{28,24},{32,36},... | collective-permute-start | bytes 983048 | tf_op jit(solution)/shard_map/ppermute | solution.py:49
  63.7 0.7 %fusion = bf16[512,160]{0,1:T(8,128)(2,1)} fusion(bf16[160,512]{1,0:T(8,128)(2,1)S(1)} %collective-permute-done.15, bf16[160,512]{1,0:T(8,128)(2,1)S(1)} %collective-permute-done.14, f32[160,512]{1,0:T(8,128)S(1)} %get-tuple-element.80, bf16[160,512]{1,0:T(8,128)(2,1)S(1)} %collective-permute-done.13), kind=kLoop, calls=%fused_computation.1 | loop fusion | flops 573440 | bytes 983040 | tf_op jit(solution)/shard_map/transpose | solution.py:464
  64.7 1.2 %shard_map.137 = (f32[640,256]{1,0:T(8,128)}, f32[640,256]{1,0:T(8,128)}) custom-call(bf16[32,40,128]{2,1,0:T(8,128)(2,1)S(1)} %all-to-all-done.1.mine, bf16[32,40,128]{2,1,0:T(8,128)(2,1)S(1)} %collective-permute-done.8.other), custom_call_target="tpu_custom_call" | custom-call | bytes 2000000 | tf_op jit(solution)/shard_map/pallas_call | solution.py:455
  (33 shorter events, 1.7 us)
Async XLA Ops:
  1.8 10.0 %collective-permute-start = (bf16[64,640]{1,0:T(8,128)(2,1)S(1)}, bf16[64,640]{1,0:T(8,128)(2,1)S(1)}, u32[]{:S(2)}, u32[]{:S(2)}) collective-permute-start(bf16[64,640]{1,0:T(8,128)(2,1)S(1)} %get-tuple-element.45), channel_id=1, source_target_pairs={{4,8},{12,16},{20,24},{28,32},{36,40},{44,48},{52,56},{60,64},{68,... | collective-permute-start | bytes 245768 | tf_op jit(solution)/shard_map/ppermute | solution.py:56
  4.9 7.2 %collective-permute-start.1 = (bf16[256,640]{1,0:T(8,128)(2,1)S(1)}, bf16[256,640]{1,0:T(8,128)(2,1)S(1)}, u32[]{:S(2)}, u32[]{:S(2)}) collective-permute-start(bf16[256,640]{1,0:T(8,128)(2,1)S(1)} %get-tuple-element.46), channel_id=1, source_target_pairs={{0,4},{4,0},{8,12},{12,8},{16,20},{20,16},{24,28},{28,24},{32,36},... | collective-permute-start | bytes 983048 | tf_op jit(solution)/shard_map/ppermute | solution.py:49
  10.9 12.7 %collective-permute-start.2 = (bf16[256,640]{1,0:T(8,128)(2,1)S(1)}, bf16[256,640]{1,0:T(8,128)(2,1)S(1)}, u32[]{:S(2)}, u32[]{:S(2)}) collective-permute-start(bf16[256,640]{1,0:T(8,128)(2,1)S(1)} %get-tuple-element.49), channel_id=1, source_target_pairs={{8,16},{12,20},{24,32},{28,36},{40,48},{44,52},{56,64},{60,68},{72... | collective-permute-start | bytes 983048 | tf_op jit(solution)/shard_map/ppermute | solution.py:56
  11.6 11.9 %collective-permute-start.3 = (bf16[256,640]{1,0:T(8,128)(2,1)S(1)}, bf16[256,640]{1,0:T(8,128)(2,1)S(1)}, u32[]{:S(2)}, u32[]{:S(2)}) collective-permute-start(bf16[256,640]{1,0:T(8,128)(2,1)S(1)} %get-tuple-element.50), channel_id=1, source_target_pairs={{0,8},{4,12},{8,0},{12,4},{16,24},{20,28},{24,16},{28,20},{32,40},... | collective-permute-start | bytes 983048 | tf_op jit(solution)/shard_map/ppermute | solution.py:49
  12.2 11.4 %collective-permute-start.6 = (bf16[64,640]{1,0:T(8,128)(2,1)S(1)}, bf16[64,640]{1,0:T(8,128)(2,1)S(1)}, u32[]{:S(2)}, u32[]{:S(2)}) collective-permute-start(bf16[64,640]{1,0:T(8,128)(2,1)S(1)} %collective-permute-done.share0), channel_id=1, source_target_pairs={{0,2},{1,3},{2,0},{3,1},{4,6},{5,7},{6,4},{7,5},{8,10},{9,11},{10,... | collective-permute-start | bytes 245768 | tf_op jit(solution)/shard_map/ppermute | solution.py:60
  15.1 8.5 %collective-permute-start.5 = (bf16[64,640]{1,0:T(8,128)(2,1)S(1)}, bf16[64,640]{1,0:T(8,128)(2,1)S(1)}, u32[]{:S(2)}, u32[]{:S(2)}) collective-permute-start(bf16[64,640]{1,0:T(8,128)(2,1)S(1)} %collective-permute-done.share0), channel_id=1, source_target_pairs={{0,1},{1,0},{2,3},{3,2},{4,5},{5,4},{6,7},{7,6},{8,9},{9,8},{10,11... | collective-permute-start | bytes 245768 | tf_op jit(solution)/shard_map/ppermute | solution.py:60
  15.5 8.1 %collective-permute-start.4 = (bf16[64,640]{1,0:T(8,128)(2,1)S(1)}, bf16[64,640]{1,0:T(8,128)(2,1)S(1)}, u32[]{:S(2)}, u32[]{:S(2)}) collective-permute-start(bf16[64,640]{1,0:T(8,128)(2,1)S(1)} %collective-permute-done.share0), channel_id=1, source_target_pairs={{0,3},{1,2},{2,1},{3,0},{4,7},{5,6},{6,5},{7,4},{8,11},{9,10},{10,... | collective-permute-start | bytes 245768 | tf_op jit(solution)/shard_map/ppermute | solution.py:60
  15.9 7.7 %copy-start.1 = (bf16[640,256]{1,0:T(8,128)(2,1)S(1)}, bf16[640,256]{1,0:T(8,128)(2,1)}, u32[]{:S(2)}) copy-start(bf16[640,256]{1,0:T(8,128)(2,1)} %neigh_w.3) | copy-start | bytes 983044
  15.9 7.7 %copy-start.8 = (bf16[512,256]{1,0:T(8,128)(2,1)S(1)}, bf16[512,256]{1,0:T(8,128)(2,1)}, u32[]{:S(2)}) copy-start(bf16[512,256]{1,0:T(8,128)(2,1)} %cot.1) | copy-start | bytes 786436
  25.6 2.2 %collective-permute-start.7 = (bf16[640,256]{1,0:T(8,128)(2,1)S(1)}, bf16[640,256]{1,0:T(8,128)(2,1)S(1)}, u32[]{:S(2)}, u32[]{:S(2)}) collective-permute-start(bf16[640,256]{1,0:T(8,128)(2,1)S(1)} %get-tuple-element.56), channel_id=1, source_target_pairs={{0,4},{4,0},{8,12},{12,8},{16,20},{20,16},{24,28},{28,24},{32,36},... | collective-permute-start | bytes 983048 | tf_op jit(solution)/shard_map/ppermute | solution.py:49
  26.9 6.8 %copy-start = (bf16[640,256]{1,0:T(8,128)(2,1)S(1)}, bf16[640,256]{1,0:T(8,128)(2,1)}, u32[]{:S(2)}) copy-start(bf16[640,256]{1,0:T(8,128)(2,1)} %self_w.3) | copy-start | bytes 983044
  28.6 14.8 %all-to-all-start = ((bf16[32,40,128]{2,1,0:T(8,128)(2,1)}), bf16[32,40,128]{2,1,0:T(8,128)(2,1)S(1)}, u32[]{:S(2)}, u32[]{:S(2)}) async-start(bf16[32,40,128]{2,1,0:T(8,128)(2,1)} %shard_map.134), calls=%async_computation | async-start | bytes 655360 | tf_op jit(solution)/shard_map/all_to_all | solution.py:66
  35.3 0.8 %copy-start.2 = (f32[512,256]{1,0:T(8,128)}, f32[512,256]{1,0:T(8,128)S(1)}, u32[]{:S(2)}) copy-start(f32[512,256]{1,0:T(8,128)S(1)} %get-tuple-element.72.start) | copy-start | bytes 1572868
  36.1 0.7 %copy-start.4 = (bf16[640,256]{1,0:T(8,128)(2,1)}, bf16[640,256]{1,0:T(8,128)(2,1)S(1)}, u32[]{:S(2)}) copy-start(bf16[640,256]{1,0:T(8,128)(2,1)S(1)} %get-tuple-element.74.self_w) | copy-start | bytes 983044
  36.9 0.7 %copy-start.6 = (bf16[640,256]{1,0:T(8,128)(2,1)}, bf16[640,256]{1,0:T(8,128)(2,1)S(1)}, u32[]{:S(2)}) copy-start(bf16[640,256]{1,0:T(8,128)(2,1)S(1)} %get-tuple-element.75.neigh_w) | copy-start | bytes 983044
  37.6 14.3 %copy-start.3 = (f32[512,256]{1,0:T(8,128)S(1)}, f32[512,256]{1,0:T(8,128)}, u32[]{:S(2)}) copy-start(f32[512,256]{1,0:T(8,128)} %copy-done.2) | copy-start | bytes 1572868
  37.6 14.3 %copy-start.5 = (bf16[640,256]{1,0:T(8,128)(2,1)S(1)}, bf16[640,256]{1,0:T(8,128)(2,1)}, u32[]{:S(2)}) copy-start(bf16[640,256]{1,0:T(8,128)(2,1)} %copy-done.4) | copy-start | bytes 983044
  37.6 14.3 %copy-start.7 = (bf16[640,256]{1,0:T(8,128)(2,1)S(1)}, bf16[640,256]{1,0:T(8,128)(2,1)}, u32[]{:S(2)}) copy-start(bf16[640,256]{1,0:T(8,128)(2,1)} %copy-done.6) | copy-start | bytes 983044
  37.6 14.3 %collective-permute-start.9 = (bf16[256,256]{1,0:T(8,128)(2,1)}, bf16[256,256]{1,0:T(8,128)(2,1)S(1)}, u32[]{:S(2)}, u32[]{:S(2)}) collective-permute-start(bf16[256,256]{1,0:T(8,128)(2,1)} %get-tuple-element.76), channel_id=1, source_target_pairs={{8,16},{12,20},{24,32},{28,36},{40,48},{44,52},{56,64},{60,68},{72... | collective-permute-start | bytes 393224 | tf_op jit(solution)/shard_map/ppermute | solution.py:56
  39.9 12.0 %collective-permute-start.10 = (bf16[256,256]{1,0:T(8,128)(2,1)}, bf16[256,256]{1,0:T(8,128)(2,1)S(1)}, u32[]{:S(2)}, u32[]{:S(2)}) collective-permute-start(bf16[256,256]{1,0:T(8,128)(2,1)} %get-tuple-element.77), channel_id=1, source_target_pairs={{4,8},{12,16},{20,24},{28,32},{36,40},{44,48},{52,56},{60,64},{68,... | collective-permute-start | bytes 393224 | tf_op jit(solution)/shard_map/ppermute | solution.py:56
  41.0 10.8 %collective-permute-start.11 = (bf16[256,256]{1,0:T(8,128)(2,1)}, bf16[256,256]{1,0:T(8,128)(2,1)S(1)}, u32[]{:S(2)}, u32[]{:S(2)}) collective-permute-start(bf16[256,256]{1,0:T(8,128)(2,1)} %get-tuple-element.78), channel_id=1, source_target_pairs={{0,8},{4,12},{8,0},{12,4},{16,24},{20,28},{24,16},{28,20},{32,40},... | collective-permute-start | bytes 393224 | tf_op jit(solution)/shard_map/ppermute | solution.py:49
  41.3 10.6 %collective-permute-start.12 = (bf16[256,256]{1,0:T(8,128)(2,1)S(1)}, bf16[256,256]{1,0:T(8,128)(2,1)S(1)}, u32[]{:S(2)}, u32[]{:S(2)}) collective-permute-start(bf16[256,256]{1,0:T(8,128)(2,1)S(1)} %get-tuple-element.79), channel_id=1, source_target_pairs={{0,4},{4,0},{8,12},{12,8},{16,20},{20,16},{24,28},{28,24},{32,36},... | collective-permute-start | bytes 393224 | tf_op jit(solution)/shard_map/ppermute | solution.py:49
  44.1 16.6 %all-to-all-start.1 = ((bf16[32,40,128]{2,1,0:T(8,128)(2,1)}), bf16[32,40,128]{2,1,0:T(8,128)(2,1)S(1)}, u32[]{:S(2)}, u32[]{:S(2)}) async-start(bf16[32,40,128]{2,1,0:T(8,128)(2,1)} %shard_map.136), calls=%async_computation.1 | async-start | bytes 655360 | tf_op jit(solution)/shard_map/all_to_all | solution.py:66
  53.0 10.4 %collective-permute-start.13 = (bf16[160,512]{1,0:T(8,128)(2,1)S(1)}, bf16[160,512]{1,0:T(8,128)(2,1)S(1)}, u32[]{:S(2)}, u32[]{:S(2)}) collective-permute-start(bf16[160,512]{1,0:T(8,128)(2,1)S(1)} %get-tuple-element.81), channel_id=1, source_target_pairs={{0,2},{1,3},{2,0},{3,1},{4,6},{5,7},{6,4},{7,5},{8,10},{9,11},{10,... | collective-permute-start | bytes 491528 | tf_op jit(solution)/shard_map/ppermute | solution.py:60
  56.0 7.4 %collective-permute-start.14 = (bf16[160,512]{1,0:T(8,128)(2,1)S(1)}, bf16[160,512]{1,0:T(8,128)(2,1)S(1)}, u32[]{:S(2)}, u32[]{:S(2)}) collective-permute-start(bf16[160,512]{1,0:T(8,128)(2,1)S(1)} %get-tuple-element.82), channel_id=1, source_target_pairs={{0,1},{1,0},{2,3},{3,2},{4,5},{5,4},{6,7},{7,6},{8,9},{9,8},{10,11... | collective-permute-start | bytes 491528 | tf_op jit(solution)/shard_map/ppermute | solution.py:60
  56.4 7.2 %collective-permute-start.15 = (bf16[160,512]{1,0:T(8,128)(2,1)S(1)}, bf16[160,512]{1,0:T(8,128)(2,1)S(1)}, u32[]{:S(2)}, u32[]{:S(2)}) collective-permute-start(bf16[160,512]{1,0:T(8,128)(2,1)S(1)} %get-tuple-element.83), channel_id=1, source_target_pairs={{0,3},{1,2},{2,1},{3,0},{4,7},{5,6},{6,5},{7,4},{8,11},{9,10},{10,... | collective-permute-start | bytes 491528 | tf_op jit(solution)/shard_map/ppermute | solution.py:60
  60.7 4.0 %collective-permute-start.8 = (bf16[32,40,128]{2,1,0:T(8,128)(2,1)S(1)}, bf16[32,40,128]{2,1,0:T(8,128)(2,1)S(1)}, u32[]{:S(2)}, u32[]{:S(2)}) collective-permute-start(bf16[32,40,128]{2,1,0:T(8,128)(2,1)S(1)} %all-to-all-done.1.mine), channel_id=1, source_target_pairs={{0,4},{4,0},{8,12},{12,8},{16,20},{20,16},{24,28},{28,24},{32,36},... | collective-permute-start | bytes 983048 | tf_op jit(solution)/shard_map/ppermute | solution.py:49
